TPU v7x, 256 devices: a whole 4x4x8 slice. The times are simulated.
256 devices in a mesh: wide: 64 (over z, x, y_hi), narrow: 4 (over y_lo, core).
Axes of the slice: x: 4, y: 4 (y_hi: 2, y_lo: 2; y = y_hi * 2 + y_lo), z: 8, core: 2. Of those that a mesh axis runs over, the one named last changes fastest.
Arguments:
- waveforms: bfloat16 [512, 12, 16384], P('wide', None, 'narrow'), may hold values from -122 to 122
- templates: bfloat16 [512, 12, 300], P('wide'), may hold values from -15 to 15
- det_station: int32 [512, 64], P('wide', 'narrow'), may hold values from 0 to 511, as said below
- det_block: int32 [512, 64], P('wide', 'narrow'), may hold values from 0 to 124, as said below
- det_count: int32 [512], P('wide'), may hold values from 1 to 64, 20480 in all
Outputs:
- detections: float32 [512, 64, 128], P('wide', 'narrow')
Inputs may be any that keep to these rules, and one draw needn't show every extreme that they name: `det_station`: in the slots of one device (one index of wide's templates, row slots of one part of the hour), at most 4 rows name stations s of one value of s // 8; exactly 4 do for one such value, the same one for every device of a part of the hour; padding rows included. `det_block`: row slot r names a block of part p = r // 16 of the hour, 4096 // 128 * p or later and before 4096 // 128 * (p + 1); every named block's windows end inside the hour. Rows from det_count on are padding.
All inputs are finite; a program needn't handle non-finite values. No bound on the sum of `det_count` on one device may be relied on, other than what follows from the above.
Results may differ from a plain program's by a relative error of at most 0.003.
Values may be sent and summed in bfloat16 or wider, within the bound.
No kernel may reach another device: no remote copies, remote signals or barrier semaphores. Data moves between devices by JAX's collectives and lax.ppermute only.
A program may use at most 128 MiB of HBM per device.

v0:
```python
import math

import jax
import jax.numpy as jnp
from jax import lax
from jax.sharding import PartitionSpec as P

CH = 12
L = 300
BLK = 128


EPS = 1e-06


def from_behind(value, axis, steps):
    count = lax.axis_size(axis)
    initial, last = (max(0, -steps), min(count, count - steps))
    return lax.ppermute(value, axis, [(source, source + steps) for source in range(initial, last)])


def prepare(templates_part):
    values = templates_part.astype(jnp.float32)
    centred = values - jnp.mean(values, axis=2, keepdims=True)
    template_scale = jnp.sqrt(jnp.mean(centred * centred, axis=2) + EPS)
    return (centred.astype(jnp.bfloat16), template_scale)


def window_scores(windows, rounded, template_scale):
    count_in, channels, span_width = windows.shape
    groups = count_in * channels
    signal = windows.reshape(1, groups, span_width)
    kernel = rounded.reshape(groups, 1, L)
    products = lax.conv_general_dilated(
        signal,
        kernel,
        (1,),
        "VALID",
        feature_group_count=groups,
        preferred_element_type=jnp.float32,
    )
    values = signal.astype(jnp.float32)
    stacked = jnp.concatenate([values, values * values], axis=0)
    ones_kernel = jnp.ones((groups, 1, L), jnp.float32)
    window_sums = (
        lax.conv_general_dilated(
            stacked,
            ones_kernel,
            (1,),
            "VALID",
            feature_group_count=groups,
            precision=lax.Precision.HIGHEST,
        )
        / L
    )
    average = window_sums[:1]
    inverse = 1.0 / jnp.sqrt(window_sums[1:] - average * average + EPS)
    length_out = span_width - L + 1
    weighted = (products * inverse).reshape(count_in, channels, length_out)
    weighted = weighted / template_scale[:, :, None]
    total = math.sqrt(L / CH) / L * jnp.sum(weighted, axis=1)
    return total[:, :BLK]


def owner_scores(row_windows, rounded, template_scale):
    own_count, rows_part, channels, span_width = row_windows.shape
    group_size = math.gcd(own_count, 8)
    turns = own_count // group_size

    def one_group(bundle):
        windows, kernels, scales = bundle
        kernel_rows = jnp.broadcast_to(kernels[:, None], (group_size, rows_part, channels, L))
        scale_rows = jnp.broadcast_to(scales[:, None], (group_size, rows_part, channels))
        scores = window_scores(
            windows.reshape(group_size * rows_part, channels, span_width),
            kernel_rows.reshape(group_size * rows_part, channels, L),
            scale_rows.reshape(group_size * rows_part, channels),
        )
        return scores.reshape(group_size, rows_part, BLK)

    result = lax.map(
        one_group,
        (
            row_windows.reshape(turns, group_size, rows_part, channels, span_width),
            rounded.reshape(turns, group_size, channels, L),
            template_scale.reshape(turns, group_size, channels),
        ),
    )
    return result.reshape(own_count, rows_part, BLK)


def local(waveforms, templates, det_station, det_block, det_count):
    stations_here, channels, segment = waveforms.shape
    own_count, rows_part = det_station.shape
    wide_count = lax.axis_size("wide")
    narrow_index = lax.axis_index("narrow")
    row_total = own_count * rows_part
    capacity = max(2, 2 * row_total // wide_count)
    span = BLK + L - 1
    padded_width = (span + 127) // 128 * 128
    tail_samples = from_behind(waveforms[:, :, : L - 1], "narrow", -1)
    filler = jnp.zeros((stations_here, channels, padded_width - BLK - (L - 1)), waveforms.dtype)
    extended = jnp.concatenate([waveforms, tail_samples, filler], axis=2)
    stations = det_station.reshape(row_total)
    holders = stations // stations_here
    local_station = stations - holders * stations_here
    local_block = det_block.reshape(row_total) - narrow_index * (segment // BLK)
    onehot = (holders[:, None] == jnp.arange(wide_count, dtype=jnp.int32)[None, :]).astype(
        jnp.int32
    )
    ranking = jnp.sum((jnp.cumsum(onehot, axis=0) - 1) * onehot, axis=1)
    position = holders * capacity + ranking
    row_values = jnp.stack([local_station, local_block], axis=1)
    buffer = jnp.zeros((wide_count * capacity,) + row_values.shape[1:], row_values.dtype)
    requests = (
        buffer.at[position].set(row_values).reshape((wide_count, capacity) + row_values.shape[1:])
    )
    requests_in = lax.all_to_all(requests, "wide", split_axis=0, concat_axis=0, tiled=True)
    flattened = requests_in.reshape(-1, requests_in.shape[-1])

    def one_window(station, block_index):
        return lax.dynamic_slice(
            extended, (station, jnp.int32(0), block_index * BLK), (1, channels, padded_width)
        )[0]

    windows = jax.vmap(one_window)(flattened[:, 0], flattened[:, 1]).reshape(
        requests_in.shape[:2] + (channels, padded_width)
    )
    returned = lax.all_to_all(windows, "wide", split_axis=0, concat_axis=0, tiled=True)
    row_windows = returned.reshape(wide_count * capacity, channels, padded_width)[position]
    rounded, template_scale = prepare(templates)
    result = owner_scores(
        row_windows.reshape(own_count, rows_part, channels, padded_width), rounded, template_scale
    )
    row_number = narrow_index * rows_part + jnp.arange(rows_part, dtype=jnp.int32)
    in_use = row_number[None, :] < det_count[:, None]
    return jnp.where(in_use[..., None], result, jnp.float32(0.0))


def solution(mesh):
    placed = (
        P("wide", None, "narrow"),
        P("wide", None, None),
        P("wide", "narrow"),
        P("wide", "narrow"),
        P("wide"),
    )
    return jax.shard_map(
        local, mesh=mesh, in_specs=placed, out_specs=P("wide", "narrow", None), check_vma=False
    )
```

profile of v0, /device:TPU:8, one launch (start us, length us, event | category | flops | bytes accessed | tf_op | source)
XLA Modules:
  0.0 726.9 jit_solution(9893925767118190096)
XLA Ops:
  0.0 0.8 reshape.245
  0.8 0.8 reshape.244
  2.0 0.7 broadcast_subtract_fusion
  2.9 0.9 scatter_custom_fusion
  3.8 1.1 copy.45
  4.9 13.7 %all-to-all-start = ((s32[64,4,2]{1,2,0:T(2,128)}), s32[64,4,2]{1,2,0:T(2,128)S(1)}, u32[]{:S(2)}, u32[]{:S(2)}) async-start(s32[64,4,2]{1,2,0:T(2,128)} %copy.45), calls=%async_computation | async-start | bytes 131072 | tf_op jit(solution)/shard_map/all_to_all | solution.py:118
  18.6 0.9 slice.21
  19.5 2.4 collective-permute-start
  21.9 8.9 %all-to-all-done = s32[64,4,2]{1,2,0:T(2,128)S(1)} async-done(((s32[64,4,2]{1,2,0:T(2,128)}), s32[64,4,2]{1,2,0:T(2,128)S(1)}, u32[]{:S(2)}, u32[]{:S(2)}) %all-to-all-start) | async-done | bytes 2080 | tf_op jit(solution)/shard_map/all_to_all | solution.py:118
  31.0 1.2 concatenate.10
  32.2 7.7 %copy.47 = bf16[8,12,4480]{1,0,2:T(8,128)(2,1)} copy(bf16[8,12,4480]{2,0,1:T(8,128)(2,1)S(1)} %concatenate.10) | data formatting | bytes 1720320 | tf_op jit(solution)/shard_map/concatenate | solution.py:103
  39.9 93.4 %gather_fusion = bf16[256,12,512]{1,0,2:T(8,128)(2,1)} fusion(bf16[8,12,4480]{1,0,2:T(8,128)(2,1)} %copy.47, s32[256]{0:T(256)S(1)} %bitcast.20), kind=kCustom, calls=%fused_computation | custom fusion | bytes 6294528 | tf_op jit(solution)/shard_map/vmap()/gather | solution.py:122
  133.4 43.4 %copy.48 = bf16[64,4,12,512]{3,1,2,0:T(4,128)(2,1)} copy(bf16[64,4,12,512]{2,1,0,3:T(4,128)(2,1)} %bitcast.19) | data formatting | bytes 6291456 | tf_op jit(solution)/shard_map/reshape;vmap()/squeeze | solution.py:126
  176.8 5.0 all-to-all-start.1
  182.1 1.3 broadcast_in_dim.56
  183.4 3.3 reshape.250
  186.7 5.1 copy.52
  193.2 2.2 fusion.21
  195.4 59.9 %all-to-all-done.1 = bf16[64,4,12,512]{3,1,2,0:T(4,128)(2,1)S(1)} async-done(((bf16[64,4,12,512]{3,1,2,0:T(4,128)(2,1)}), bf16[64,4,12,512]{3,1,2,0:T(4,128)(2,1)S(1)}, u32[]{:S(2)}, u32[]{:S(2)}) %all-to-all-start.1) | async-done | bytes 3145760 | tf_op jit(solution)/shard_map/all_to_all | solution.py:129
  255.3 3.1 copy.49
  258.5 4.2 gather_fusion.1
  262.6 2.5 reshape.249
  265.1 2.1 convert_element_type.28
  267.2 2.1 convert_multiply_fusion
  269.3 5.9 copy.51
  275.3 6.2 pad_maximum_fusion
  281.5 10.6 %copy.53 = f32[2,1536,512]{1,0,2:T(2,128)} copy(f32[2,1536,512]{2,1,0:T(8,128)} %pad_maximum_fusion) | data formatting | bytes 12582912 | tf_op jit(solution)/shard_map/while/body/eval_jaxpr/concatenate | solution.py:43
  292.0 58.9 %convolution_multiply_fusion = f32[2,1536,213]{1,0,2:T(2,128)S(1)} fusion(f32[2,1536,512]{1,0,2:T(2,128)} %copy.53, f32[1536,1,300]{0,1,2:T(1,128)S(1)} %copy-done.1), kind=kOutput, calls=%fused_computation.4 | convolution fusion | flops 2356263936 | bytes 10752000 | tf_op jit(solution)/shard_map/while/body/eval_jaxpr/conv_general_dilated | solution.py:46
  351.0 370.7 %convolution_multiply_fusion.1 = f32[1,1536,213]{1,0,2:T(1,128)S(1)} fusion(bf16[1,1536,512]{1,0,2:T(2,128)(2,1)S(1)} %copy-done, bf16[1536,1,300]{0,1,2:T(2,128)(2,1)S(1)} %copy-done.2, f32[2,1536,213]{1,0,2:T(2,128)S(1)} %convolution_multiply_fusion), kind=kOutput, calls=%fused_computation.5 | convolution fusion | flops 197609472 | bytes 6420480 | tf_op jit(solution)/shard_map/while/body/eval_jaxpr/conv_general_dilated | solution.py:34
  721.8 2.3 copy.54
  724.1 1.5 reshape.251
  726.2 0.7 broadcast_select_fusion
  (40 shorter events, 3.1 us)
Async XLA Ops:
  4.9 25.9 %all-to-all-start = ((s32[64,4,2]{1,2,0:T(2,128)}), s32[64,4,2]{1,2,0:T(2,128)S(1)}, u32[]{:S(2)}, u32[]{:S(2)}) async-start(s32[64,4,2]{1,2,0:T(2,128)} %copy.45), calls=%async_computation | async-start | bytes 131072 | tf_op jit(solution)/shard_map/all_to_all | solution.py:118
  19.5 11.5 %collective-permute-start = (bf16[8,12,299]{2,0,1:T(8,128)(2,1)S(1)}, bf16[8,12,299]{2,0,1:T(8,128)(2,1)S(1)}, u32[]{:S(2)}, u32[]{:S(2)}) collective-permute-start(bf16[8,12,299]{2,0,1:T(8,128)(2,1)S(1)} %slice.21), channel_id=1, source_target_pairs={{1,0},{2,1},{3,2},{5,4},{6,5},{7,6},{9,8},{10,9},{11,10},{13,12},{... | collective-permute-start | bytes 172232 | tf_op jit(solution)/shard_map/ppermute | solution.py:19
  176.8 5.1 copy-start.3
  176.8 78.6 %all-to-all-start.1 = ((bf16[64,4,12,512]{3,1,2,0:T(4,128)(2,1)}), bf16[64,4,12,512]{3,1,2,0:T(4,128)(2,1)S(1)}, u32[]{:S(2)}, u32[]{:S(2)}) async-start(bf16[64,4,12,512]{3,1,2,0:T(4,128)(2,1)} %copy.48), calls=%async_computation.1 | async-start | bytes 6291456 | tf_op jit(solution)/shard_map/all_to_all | solution.py:129
  183.4 9.1 %copy-start.6 = (s32[8]{0:T(128)S(1)}, s32[8]{0:T(128)}, u32[]{:S(2)}) copy-start(s32[8]{0:T(128)} %param.9) | copy-start | bytes 100
  281.5 10.6 %copy-start.1 = (f32[1536,1,300]{0,1,2:T(1,128)S(1)}, f32[1536,1,300]{0,1,2:T(1,128)}, u32[]{:S(2)}) copy-start(f32[1536,1,300]{0,1,2:T(1,128)} %fusion.21) | copy-start | bytes 5529604
  292.0 58.9 %copy-start = (bf16[1,1536,512]{1,0,2:T(2,128)(2,1)S(1)}, bf16[1,1536,512]{1,0,2:T(2,128)(2,1)}, u32[]{:S(2)}) copy-start(bf16[1,1536,512]{1,0,2:T(2,128)(2,1)} %copy.51) | copy-start | bytes 4718596
  292.0 59.0 %copy-start.2 = (bf16[1536,1,300]{0,1,2:T(2,128)(2,1)S(1)}, bf16[1536,1,300]{0,1,2:T(2,128)(2,1)}, u32[]{:S(2)}) copy-start(bf16[1536,1,300]{0,1,2:T(2,128)(2,1)} %copy.52) | copy-start | bytes 2764804
  721.7 3.8 copy-start.4
  724.1 2.1 copy-start.5
where the time goes:
time: 732 us; the launch traced here: 727 us
  matrix products  430 us (59%)
  local copies, waits for them, and re-layouts  193 us (26%)
  waiting for transfers between devices  68.8 us (9%)
  starting transfers between devices  21.1 us (3%)
  other arithmetic  13.9 us (2%)
    conv_general_dilated x1, matrix products, window_scores(): lax.conv_general_dilated(signal, kernel, (1,), 'VALID', feature_group_cou...  371 us
    gather x1, local copies, waits for them, and re-layouts, one_window(): lax.dynamic_slice(extended, (station, jnp.int32(0), block_index * BLK), (...  93.4 us
    all_to_all x1, waiting for transfers between devices, local(): lax.all_to_all(windows, 'wide', split_axis=0, concat_axis=0, tiled=True)  59.9 us
    conv_general_dilated x1, matrix products, window_scores(): lax.conv_general_dilated(stacked, ones_kernel, (1,), 'VALID', feature_gro...  58.9 us
    squeeze x1, local copies, waits for them, and re-layouts, local(): jax.vmap(one_window)(flattened[:, 0], flattened[:, 1])  43.4 us
  transfers between devices with their start and end apart: 3, of which 2 were waited for; matrix products, arithmetic and copies ran while one was open for 2% of the time, Pallas kernels for 0%

commit v1 on v0

v1 whole, which is shorter than its diff:
```python
import functools

import jax
import jax.numpy as jnp
from jax import lax
from jax.experimental import pallas as pl
from jax.experimental.pallas import tpu as pltpu
from jax.sharding import PartitionSpec as P

CH = 12
L = 300
BLK = 128
EPS = 1e-06
CAP = 4
UNIT = 32
SHIFTS = 16
GROUP = 16
VMEM_LIMIT = 60 * 1024 * 1024
NT = (((1,), (1,)), ((), ()))
TN = (((0,), (0,)), ((), ()))


def lanes_of(shape):
    return lax.broadcasted_iota(jnp.int32, shape, len(shape) - 1)


def rows_of(shape):
    return lax.broadcasted_iota(jnp.int32, shape, len(shape) - 2)


def to_bf16(values):
    return values.astype(jnp.bfloat16)


def to_f32(values):
    return values.astype(jnp.float32)


def pack_kernel(station_ref, block_ref, templates_ref, sent_ref, place_ref, padded, units, units16, used):
    templates = templates_ref.shape[0]
    rows_part = station_ref.shape[1]
    padded[...] = jnp.zeros_like(padded)
    units[...] = jnp.zeros_like(units)
    for k in range(templates):
        values = to_f32(templates_ref[k])
        centred = values - jnp.sum(values, axis=1, keepdims=True) / L
        power = jnp.sum(centred * centred, axis=1, keepdims=True) / L
        factor = 1.0 / (60.0 * jnp.sqrt(power + EPS))
        padded[k, :, 0:L] = to_f32(to_bf16(centred))
        units[k, 0:12, :] = padded[k, :, 0:128]
        units[k, 12:24, :] = padded[k, :, 128:256]
        rest = padded[k, :, 256:384]
        units[k, 24:30, :] = rest[0:6] + pltpu.roll(rest, 64, 1)[6:12]
        high = to_f32(to_bf16(factor))
        middle = to_f32(to_bf16(factor - high))
        low = to_f32(to_bf16(factor - high - middle))
        lane, row = lanes_of((CH, 128)), rows_of((CH, 128))
        spread = jnp.where(
            lane == row,
            high,
            jnp.where(lane == row + 16, middle, jnp.where(lane == row + 32, low, 0.0)),
        )
        units[k, 30:31, :] = jnp.sum(spread, axis=0, keepdims=True)
        units16[k] = to_bf16(units[k])

    def clear(h, carry):
        sent_ref[pl.ds(CAP * h, CAP)] = jnp.zeros((CAP, UNIT, 128), jnp.bfloat16)
        used[h] = 0
        return carry

    lax.fori_loop(0, used.shape[0], clear, 0)
    lane, row = lanes_of((16, 128)), rows_of((16, 128))
    at_station = (row == 14) & (lane == 48)
    at_block = (row == 14) & (lane == 49)

    def place(r, carry):
        k = r // rows_part
        station = station_ref[k, r % rows_part]
        block = block_ref[k, r % rows_part] & 31
        holder = station // 8
        rank = jnp.minimum(used[holder], CAP - 1)
        used[holder] = rank + 1
        slot = holder * CAP + rank
        place_ref[r] = slot
        sent_ref[slot, 0:16, :] = units16[k, 0:16, :]
        upper = units[k, 16:32, :]
        upper = jnp.where(at_station, (station & 7).astype(jnp.float32), upper)
        upper = jnp.where(at_block, block.astype(jnp.float32), upper)
        sent_ref[slot, 16:32, :] = to_bf16(upper)
        return carry

    lax.fori_loop(0, templates * rows_part, place, 0, unroll=4)


def pack(station, block, templates, holders):
    count = templates.shape[0]
    return pl.pallas_call(
        pack_kernel,
        out_shape=(
            jax.ShapeDtypeStruct((holders * CAP, UNIT, 128), jnp.bfloat16),
            jax.ShapeDtypeStruct((count * station.shape[1],), jnp.int32),
        ),
        in_specs=[
            pl.BlockSpec(memory_space=pltpu.SMEM),
            pl.BlockSpec(memory_space=pltpu.SMEM),
            pl.BlockSpec(memory_space=pltpu.VMEM),
        ],
        out_specs=(
            pl.BlockSpec(memory_space=pltpu.VMEM),
            pl.BlockSpec(memory_space=pltpu.SMEM),
        ),
        scratch_shapes=[
            pltpu.VMEM((count, CH, 384), jnp.float32),
            pltpu.VMEM((count, UNIT, 128), jnp.float32),
            pltpu.VMEM((count, UNIT, 128), jnp.bfloat16),
            pltpu.SMEM((holders,), jnp.int32),
        ],
        compiler_params=pltpu.CompilerParams(vmem_limit_bytes=VMEM_LIMIT),
    )(station, block, templates)


def station_kernel(wave_ref, tail_ref, shifted_ref, inverse_ref, signal, stacked):
    segment = wave_ref.shape[2]
    blocks = inverse_ref.shape[1]
    pieces = shifted_ref.shape[1]
    signal[CH:16, :] = jnp.zeros_like(signal[CH:16, :])
    signal[0:CH, 0:segment] = to_f32(wave_ref[0])
    signal[0:CH, segment:] = to_f32(tail_ref[0])
    lane, row = lanes_of((SHIFTS, 128)), rows_of((SHIFTS, 128))
    source = (lane + 8 * row) & 127
    inside = lane + 8 * row < 128

    def shift(piece, carry):
        start = pl.multiple_of(piece * 128, 128)
        here = signal[:, pl.ds(start, 128)]
        after = signal[:, pl.ds(start + 128, 128)]
        for c in range(CH):
            left = jnp.take_along_axis(jnp.broadcast_to(here[c : c + 1], (SHIFTS, 128)), source, axis=1)
            right = jnp.take_along_axis(jnp.broadcast_to(after[c : c + 1], (SHIFTS, 128)), source, axis=1)
            shifted_ref[0, piece, c] = to_bf16(jnp.where(inside, left, right))
        return carry

    lax.fori_loop(0, pieces, shift, 0)
    for b in range(blocks):
        stacked[16 * b : 16 * b + 16, :] = signal[:, 128 * b : 128 * b + 512]
    sample, position = rows_of((512, 128)), lanes_of((512, 128))
    band = to_bf16(jnp.where((sample >= position) & (sample < position + L), 1.0, 0.0))
    values = stacked[...]
    squares = values * values
    high = to_bf16(squares)
    low = to_bf16(squares - to_f32(high))
    first = jnp.dot(to_bf16(values), band, preferred_element_type=jnp.float32) / L
    second = (
        jnp.dot(high, band, preferred_element_type=jnp.float32)
        + jnp.dot(low, band, preferred_element_type=jnp.float32)
    ) / L
    inverse = 1.0 / jnp.sqrt(second - first * first + EPS)
    inverse_ref[0] = inverse.reshape(blocks, 16, 128)


def station_tables(wave, tail):
    stations, channels, segment = wave.shape
    blocks = segment // BLK
    extra = tail.shape[2]
    return pl.pallas_call(
        station_kernel,
        grid=(stations,),
        out_shape=(
            jax.ShapeDtypeStruct((stations, blocks + 2, channels, SHIFTS, 128), jnp.bfloat16),
            jax.ShapeDtypeStruct((stations, blocks, 16, 128), jnp.float32),
        ),
        in_specs=[
            pl.BlockSpec((1, channels, segment), lambda s: (s, 0, 0)),
            pl.BlockSpec((1, channels, extra), lambda s: (s, 0, 0)),
        ],
        out_specs=(
            pl.BlockSpec((1, blocks + 2, channels, SHIFTS, 128), lambda s: (s, 0, 0, 0, 0)),
            pl.BlockSpec((1, blocks, 16, 128), lambda s: (s, 0, 0, 0)),
        ),
        scratch_shapes=[
            pltpu.VMEM((16, segment + extra), jnp.float32),
            pltpu.VMEM((16 * blocks, 512), jnp.float32),
        ],
        compiler_params=pltpu.CompilerParams(vmem_limit_bytes=32 * 1024 * 1024),
        cost_estimate=pl.CostEstimate(flops=3_000_000_000, bytes_accessed=20_000_000, transcendentals=500_000),
    )(wave, tail)


def score_kernel(
    station_ref, block_ref, units_ref, marks_ref, shifted_ref, inverse_ref, scores_ref, kernels, windows
):
    lane, row = lanes_of((8, 128)), rows_of((8, 128))
    before = lane < row
    low_half = lane < 64
    member = lane // SHIFTS
    inverse_source = 8 * (lane % SHIFTS) + row
    natural_source = SHIFTS * row + lane // 8
    expand = to_bf16(jnp.where(lanes_of((GROUP, 256)) // SHIFTS == rows_of((GROUP, 256)), 1.0, 0.0))

    def template_rows(unit):
        swapped = pltpu.roll(unit, 64, 1)
        result = []
        for c in range(CH):
            third = unit[24 + c : 25 + c] if c < 6 else swapped[18 + c : 19 + c]
            parts = [unit[c : c + 1], unit[12 + c : 13 + c], third]
            parts = [jnp.broadcast_to(part, (8, 128)) for part in parts]
            parts[2] = jnp.where(low_half, parts[2], 0.0)
            turned = [pltpu.roll(part, 0, 1, stride=1, stride_axis=0) for part in parts]
            result.append(
                [
                    jnp.where(before, 0.0, turned[0]),
                    jnp.where(before, turned[0], turned[1]),
                    jnp.where(before, turned[1], turned[2]),
                ]
            )
        return result

    def one_group(group, carry):
        base = group * GROUP
        for pair in range(GROUP // 2):
            rows = []
            for g in (2 * pair, 2 * pair + 1):
                station, block = station_ref[base + g], block_ref[base + g]
                for a in range(3):
                    windows[:, 16 * g : 16 * g + 16, 128 * a : 128 * a + 128] = shifted_ref[station, block + a]
                rows.append(template_rows(to_f32(units_ref[base + g])))
            for c in range(CH):
                for a in range(3):
                    both = jnp.concatenate([rows[0][c][a], rows[1][c][a]], axis=0)
                    kernels[c, 16 * pair : 16 * pair + 16, 128 * a : 128 * a + 128] = to_bf16(both)
        marks = marks_ref[pl.ds(pl.multiple_of(base, GROUP), GROUP), :]
        spread = lax.dot_general(marks, expand, TN, preferred_element_type=jnp.float32)
        factors = spread[0:12] + spread[16:28] + spread[32:44]
        totals = [jnp.zeros((8, 128), jnp.float32) for _ in range(2)]
        for c in range(CH):
            products = lax.dot_general(kernels[c], windows[c], NT, preferred_element_type=jnp.float32)
            for half in range(2):
                chosen = jnp.zeros((8, 128), jnp.float32)
                scale = jnp.zeros((8, 128), jnp.float32)
                for m in range(8):
                    g = 8 * half + m
                    station, block = station_ref[base + g], block_ref[base + g]
                    inverse = jnp.broadcast_to(inverse_ref[station, block, c : c + 1, :], (8, 128))
                    inverse = jnp.take_along_axis(inverse, inverse_source, axis=1)
                    mine = products[8 * g : 8 * g + 8, 128 * half : 128 * half + 128]
                    chosen = jnp.where(member == m, mine, chosen)
                    scale = jnp.where(member == m, inverse, scale)
                factor = factors[c : c + 1, 128 * half : 128 * half + 128]
                totals[half] = totals[half] + chosen * scale * factor
        for half in range(2):
            natural = jnp.zeros((8, 128), jnp.float32)
            for i in range(8):
                spread_row = jnp.broadcast_to(totals[half][i : i + 1], (8, 128))
                spread_row = jnp.take_along_axis(spread_row, natural_source, axis=1)
                natural = jnp.where(lane % 8 == i, spread_row, natural)
            for o in range(2):
                scores_ref[group * 4 + half * 2 + o] = natural[4 * o : 4 * o + 4]
        return carry

    lax.fori_loop(0, units_ref.shape[0] // GROUP, one_group, 0)


def slot_scores(stations, blocks, units, marks, shifted, inverse):
    slots = units.shape[0]
    smem = pl.BlockSpec(memory_space=pltpu.SMEM)
    vmem = pl.BlockSpec(memory_space=pltpu.VMEM)
    return pl.pallas_call(
        score_kernel,
        out_shape=jax.ShapeDtypeStruct((slots // CAP, CAP, BLK), jnp.float32),
        in_specs=[smem, smem, vmem, vmem, vmem, vmem],
        out_specs=vmem,
        scratch_shapes=[
            pltpu.VMEM((CH, 8 * GROUP, 384), jnp.bfloat16),
            pltpu.VMEM((CH, SHIFTS * GROUP, 384), jnp.bfloat16),
        ],
        compiler_params=pltpu.CompilerParams(vmem_limit_bytes=VMEM_LIMIT),
    )(stations, blocks, units, marks, shifted, inverse)


def unpack_kernel(place_ref, limit_ref, scores_ref, out_ref):
    templates, rows_part, _ = out_ref.shape
    for k in range(templates):
        for r in range(rows_part):
            slot = place_ref[k * rows_part + r]
            found = scores_ref[slot // CAP, pl.ds(slot % CAP, 1), :]
            out_ref[k, r : r + 1, :] = jnp.where(r < limit_ref[k], found, 0.0)


def unpack(place, limit, scores, shape):
    smem = pl.BlockSpec(memory_space=pltpu.SMEM)
    vmem = pl.BlockSpec(memory_space=pltpu.VMEM)
    return pl.pallas_call(
        unpack_kernel,
        out_shape=jax.ShapeDtypeStruct(shape, jnp.float32),
        in_specs=[smem, smem, vmem],
        out_specs=vmem,
        compiler_params=pltpu.CompilerParams(vmem_limit_bytes=VMEM_LIMIT),
    )(place, limit, scores)


def local(waveforms, templates, det_station, det_block, det_count):
    own_count, rows_part = det_station.shape
    wide_count = lax.axis_size("wide")
    narrow_count = lax.axis_size("narrow")
    exchange = functools.partial(lax.all_to_all, axis_name="wide", split_axis=0, concat_axis=0, tiled=True)
    sent, place = pack(det_station, det_block, templates, wide_count)
    units = exchange(sent.reshape(wide_count, CAP * UNIT, 128)).reshape(wide_count * CAP, UNIT, 128)
    tail = lax.ppermute(
        waveforms[:, :, : 3 * BLK], "narrow", [(i, i - 1) for i in range(1, narrow_count)]
    )
    shifted, inverse = station_tables(waveforms, tail)
    marks = units[:, 30, :]
    scores = slot_scores(
        marks[:, 48].astype(jnp.int32), marks[:, 49].astype(jnp.int32), units, marks, shifted, inverse
    )
    returned = exchange(scores)
    limit = det_count - lax.axis_index("narrow") * rows_part
    return unpack(place, limit, returned, (own_count, rows_part, BLK))


def solution(mesh):
    placed = (
        P("wide", None, "narrow"),
        P("wide", None, None),
        P("wide", "narrow"),
        P("wide", "narrow"),
        P("wide"),
    )
    return jax.shard_map(
        local, mesh=mesh, in_specs=placed, out_specs=P("wide", "narrow", None), check_vma=False
    )
```

time: 732 us -> 130 us (0.18)
  the two profiles are of different devices: /device:TPU:8 before, /device:TPU:1 now
where the time goes in v1:
time: 130 us; the launch traced here: 129 us
  Pallas kernels  70.3 us (54%)
  starting transfers between devices  30.1 us (23%)
  waiting for transfers between devices  18.1 us (14%)
  local copies, waits for them, and re-layouts  8.94 us (7%)
  other arithmetic  1.7 us (1%)
    pallas_call x1, Pallas kernels, station_tables(): pl.pallas_call(station_kernel, grid=(stations,), out_shape=(jax.ShapeDtyp...  32.7 us
    pallas_call x1, Pallas kernels, slot_scores(): pl.pallas_call(score_kernel, out_shape=jax.ShapeDtypeStruct((slots // CAP...  30 us
    all_to_all x1, starting transfers between devices, local(): exchange(sent.reshape(wide_count, CAP * UNIT, 128))  15.3 us
    all_to_all x1, starting transfers between devices, local(): returned = exchange(scores)  12 us
    all_to_all x1, waiting for transfers between devices, local(): returned = exchange(scores)  11.1 us
    unnamed x17, local copies, waits for them, and re-layouts  8.79 us
    ppermute x1, waiting for transfers between devices, local(): lax.ppermute(waveforms[:, :, :3 * BLK], 'narrow', [(i, i - 1) for i in ra...  6.97 us
    pallas_call x1, Pallas kernels, pack(): pl.pallas_call(pack_kernel, out_shape=(jax.ShapeDtypeStruct((holders * CA...  5.19 us
  transfers between devices with their start and end apart: 3, of which 2 were waited for; matrix products, arithmetic and copies ran while one was open for 1% of the time, Pallas kernels for 25%

profile of v1, /device:TPU:1, one launch (start us, length us, event | category | flops | bytes accessed | tf_op | source)
XLA Modules:
  0.0 129.2 jit_solution(5852865817386786326)
XLA Ops:
  0.0 1.5 %copy.10.templates_ref = bf16[8,12,300]{2,1,0:T(8,128)(2,1)} copy(bf16[8,12,300]{2,0,1:T(8,128)(2,1)} %param.6) | data formatting | bytes 115200 | tf_op args[1]
  1.5 5.2 %shard_map.55 = (bf16[256,32,128]{2,1,0:T(8,128)(2,1)}, s32[128]{0:T(128)}) custom-call(s32[8,16]{1,0:T(8,128)} %station_ref.1, s32[8,16]{1,0:T(8,128)} %block_ref.1, bf16[8,12,300]{2,1,0:T(8,128)(2,1)} %copy.10.templates_ref), custom_call_target="tpu_custom_call" | custom-call | tf_op jit(solution)/shard_map/pallas_call | solution.py:97
  6.7 0.0 copy-start.4
  6.7 15.3 %all-to-all-start = ((bf16[64,128,128]{2,1,0:T(8,128)(2,1)}), bf16[64,128,128]{2,1,0:T(8,128)(2,1)S(1)}, u32[]{:S(2)}, u32[]{:S(2)}) async-start(bf16[64,128,128]{2,1,0:T(8,128)(2,1)} %bitcast.7), calls=%async_computation | async-start | bytes 4194304 | tf_op jit(solution)/shard_map/all_to_all | solution.py:307
  22.0 0.0 copy-done.4
  22.0 0.5 copy.13.wave_ref
  22.5 2.9 %collective-permute-start = (bf16[8,12,384]{2,1,0:T(8,128)(2,1)S(1)}, bf16[8,12,384]{2,1,0:T(8,128)(2,1)S(1)}, u32[]{:S(2)}, u32[]{:S(2)}) collective-permute-start(bf16[8,12,384]{2,1,0:T(8,128)(2,1)S(1)} %slice.19), channel_id=1, source_target_pairs={{1,0},{2,1},{3,2},{5,4},{6,5},{7,6},{9,8},{10,9},{11,10},{13,12},{... | collective-permute-start | bytes 221192 | tf_op jit(solution)/shard_map/ppermute | solution.py:308
  25.4 7.0 %collective-permute-done.tail_ref = bf16[8,12,384]{2,1,0:T(8,128)(2,1)S(1)} collective-permute-done((bf16[8,12,384]{2,1,0:T(8,128)(2,1)S(1)}, bf16[8,12,384]{2,1,0:T(8,128)(2,1)S(1)}, u32[]{:S(2)}, u32[]{:S(2)}) %collective-permute-start) | collective-permute-done | bytes 73760 | tf_op jit(solution)/shard_map/ppermute | solution.py:308
  32.3 32.7 %shard_map.56 = (bf16[8,34,12,16,128]{4,3,2,1,0:T(8,128)(2,1)S(1)}, f32[8,32,16,128]{3,2,1,0:T(8,128)S(1)}) custom-call(bf16[8,12,4096]{2,1,0:T(8,128)(2,1)S(1)} %copy.13.wave_ref, bf16[8,12,384]{2,1,0:T(8,128)(2,1)S(1)} %collective-permute-done.tail_ref), custom_call_target="tpu_custom_call" | custom-call | flops 3000000000 | bytes 20000000 | tf_op jit(solution)/shard_map/pallas_call | solution.py:165
  65.0 0.0 copy-start
  65.0 4.8 %copy-done = bf16[8,34,12,16,128]{4,3,2,1,0:T(8,128)(2,1)} copy-done((bf16[8,34,12,16,128]{4,3,2,1,0:T(8,128)(2,1)}, bf16[8,34,12,16,128]{4,3,2,1,0:T(8,128)(2,1)S(1)}, u32[]{:S(2)}) %copy-start) | copy-done | bytes 13369368
  69.8 0.0 copy-start.1
  69.8 1.3 %copy-done.1 = f32[8,32,16,128]{3,2,1,0:T(8,128)} copy-done((f32[8,32,16,128]{3,2,1,0:T(8,128)}, f32[8,32,16,128]{3,2,1,0:T(8,128)S(1)}, u32[]{:S(2)}) %copy-start.1) | copy-done | bytes 2097176
  71.1 0.0 all-to-all-done
  71.1 0.0 copy-start.2
  71.1 0.1 slice.16
  71.3 0.0 copy-start.3
  71.3 1.1 convert_reduce_fusion
  72.4 0.0 copy-done.2
  72.5 0.0 copy-done.3
  72.5 0.0 copy-start.6
  72.5 30.0 %shard_map.57 = f32[64,4,128]{2,1,0:T(4,128)} custom-call(s32[256]{0:T(256)} %get-tuple-element.14.station_ref, s32[256]{0:T(256)} %get-tuple-element.13.block_ref, bf16[256,32,128]{2,1,0:T(8,128)(2,1)} %bitcast.6, bf16[256,128]{1,0:T(8,128)(2,1)} %bitcast.9, bf16[8,34,12,16,128]{4,3,2,1,0:T(8,128)(2,1)} %copy-done, f32[8,32,16,128]{3,2,1,0:T(8,128)} %copy-done.1), custom_call_target="tpu_custom_call" | custom-call | tf_op jit(solution)/shard_map/pallas_call | solution.py:267
  102.5 12.0 %all-to-all-start.1 = ((f32[64,4,128]{2,1,0:T(4,128)}), f32[64,4,128]{2,1,0:T(4,128)S(1)}, u32[]{:S(2)}, u32[]{:S(2)}) async-start(f32[64,4,128]{2,1,0:T(4,128)} %shard_map.57), calls=%async_computation.1 | async-start | bytes 262144 | tf_op jit(solution)/shard_map/all_to_all | solution.py:316
  114.4 0.0 copy-done.6
  114.4 0.6 broadcast_subtract_fusion.limit_ref
  115.0 11.1 %all-to-all-done.1.scores_ref = f32[64,4,128]{2,1,0:T(4,128)S(1)} async-done(((f32[64,4,128]{2,1,0:T(4,128)}), f32[64,4,128]{2,1,0:T(4,128)S(1)}, u32[]{:S(2)}, u32[]{:S(2)}) %all-to-all-start.1) | async-done | bytes 131104 | tf_op jit(solution)/shard_map/all_to_all | solution.py:316
  126.1 0.0 copy-start.5
  126.1 0.6 copy-done.5
  126.7 2.4 %shard_map.58 = f32[8,16,128]{2,1,0:T(8,128)} custom-call(s32[128]{0:T(128)} %get-tuple-element.9.place_ref, s32[8]{0:T(128)} %broadcast_subtract_fusion.limit_ref, f32[64,4,128]{2,1,0:T(4,128)} %copy-done.5), custom_call_target="tpu_custom_call" | custom-call | tf_op jit(solution)/shard_map/pallas_call | solution.py:292
  (2 shorter events, 0.0 us)
Async XLA Ops:
  6.7 15.3 %copy-start.4 = (bf16[8,12,4096]{2,0,1:T(8,128)(2,1)S(1)}, bf16[8,12,4096]{2,0,1:T(8,128)(2,1)}, u32[]{:S(2)}) copy-start(bf16[8,12,4096]{2,0,1:T(8,128)(2,1)} %param.5) | copy-start | bytes 2359300
  6.7 64.4 %all-to-all-start = ((bf16[64,128,128]{2,1,0:T(8,128)(2,1)}), bf16[64,128,128]{2,1,0:T(8,128)(2,1)S(1)}, u32[]{:S(2)}, u32[]{:S(2)}) async-start(bf16[64,128,128]{2,1,0:T(8,128)(2,1)} %bitcast.7), calls=%async_computation | async-start | bytes 4194304 | tf_op jit(solution)/shard_map/all_to_all | solution.py:307
  22.5 9.8 %collective-permute-start = (bf16[8,12,384]{2,1,0:T(8,128)(2,1)S(1)}, bf16[8,12,384]{2,1,0:T(8,128)(2,1)S(1)}, u32[]{:S(2)}, u32[]{:S(2)}) collective-permute-start(bf16[8,12,384]{2,1,0:T(8,128)(2,1)S(1)} %slice.19), channel_id=1, source_target_pairs={{1,0},{2,1},{3,2},{5,4},{6,5},{7,6},{9,8},{10,9},{11,10},{13,12},{... | collective-permute-start | bytes 221192 | tf_op jit(solution)/shard_map/ppermute | solution.py:308
  65.0 4.8 %copy-start = (bf16[8,34,12,16,128]{4,3,2,1,0:T(8,128)(2,1)}, bf16[8,34,12,16,128]{4,3,2,1,0:T(8,128)(2,1)S(1)}, u32[]{:S(2)}) copy-start(bf16[8,34,12,16,128]{4,3,2,1,0:T(8,128)(2,1)S(1)} %get-tuple-element.11.shifted_ref) | copy-start | bytes 40108036
  69.8 1.3 %copy-start.1 = (f32[8,32,16,128]{3,2,1,0:T(8,128)}, f32[8,32,16,128]{3,2,1,0:T(8,128)S(1)}, u32[]{:S(2)}) copy-start(f32[8,32,16,128]{3,2,1,0:T(8,128)S(1)} %get-tuple-element.12.inverse_ref) | copy-start | bytes 6291460
  71.1 1.3 %copy-start.2 = (bf16[64,128,128]{2,1,0:T(8,128)(2,1)}, bf16[64,128,128]{2,1,0:T(8,128)(2,1)S(1)}, u32[]{:S(2)}) copy-start(bf16[64,128,128]{2,1,0:T(8,128)(2,1)S(1)} %all-to-all-done) | copy-start | bytes 6291460
  71.3 1.2 copy-start.3
  72.5 42.0 %copy-start.6 = (s32[8]{0:T(128)S(1)}, s32[8]{0:T(128)}, u32[]{:S(2)}) copy-start(s32[8]{0:T(128)} %param.9) | copy-start | bytes 100
  102.5 23.6 %all-to-all-start.1 = ((f32[64,4,128]{2,1,0:T(4,128)}), f32[64,4,128]{2,1,0:T(4,128)S(1)}, u32[]{:S(2)}, u32[]{:S(2)}) async-start(f32[64,4,128]{2,1,0:T(4,128)} %shard_map.57), calls=%async_computation.1 | async-start | bytes 262144 | tf_op jit(solution)/shard_map/all_to_all | solution.py:316
  126.1 0.6 copy-start.5

commit v2 on v1

v2 whole, which is shorter than its diff:
```python
import jax
import jax.numpy as jnp
from jax import lax
from jax.experimental import pallas as pl
from jax.experimental.pallas import tpu as pltpu
from jax.sharding import PartitionSpec as P

CH = 12
L = 300
BLK = 128
EPS = 1e-06
CAP = 4
UNIT = 32
PLANE = 8
X, Y = 4, 2
PLANE_STEPS = ((0, 0), (1, 0), (3, 0), (0, 1), (2, 0), (1, 1), (3, 1), (2, 1))
Z_STEPS = (0, 1, 7, 2, 6, 3, 5, 4)
SHIFTS = 16
GROUP = 16
VMEM_LIMIT = 24 * 1024 * 1024
NT = (((1,), (1,)), ((), ()))
TN = (((0,), (0,)), ((), ()))


def lanes_of(shape):
    return lax.broadcasted_iota(jnp.int32, shape, len(shape) - 1)


def rows_of(shape):
    return lax.broadcasted_iota(jnp.int32, shape, len(shape) - 2)


def to_bf16(values):
    return values.astype(jnp.bfloat16)


def to_f32(values):
    return values.astype(jnp.float32)


def read_scalars(rows, weights, staged, scalars, sem):
    lane = lanes_of((8, 128))
    picked = jnp.zeros((8, 128), jnp.float32)
    for place, weight in weights:
        picked = jnp.where(lane == place, float(weight), picked)
    values = lax.dot_general(to_bf16(picked), rows, NT, preferred_element_type=jnp.float32)
    staged[...] = values.astype(jnp.int32)
    copy = pltpu.make_async_copy(staged, scalars, sem)
    copy.start()
    copy.wait()


def pack_kernel(station_ref, block_ref, templates_ref, *refs):
    sent_refs, (place_ref, padded, units, table, used) = refs[: len(Z_STEPS)], refs[len(Z_STEPS) :]
    channels, templates, _ = templates_ref.shape
    rows_part = station_ref.shape[1]
    values = to_f32(templates_ref[...])
    centred = values - jnp.sum(values, axis=2, keepdims=True) / L
    power = jnp.sum(centred * centred, axis=2, keepdims=True) / L
    factor = 1.0 / (60.0 * jnp.sqrt(power + EPS))
    padded[...] = jnp.zeros_like(padded)
    padded[:, :, 0:L] = to_f32(to_bf16(centred))
    high = to_f32(to_bf16(factor))
    middle = to_f32(to_bf16(factor - high))
    low = to_f32(to_bf16(factor - high - middle))
    lane = lanes_of((templates, 128))
    marks = jnp.zeros((templates, 128), jnp.float32)
    for c in range(channels):
        marks = jnp.where(lane == c, high[c], marks)
        marks = jnp.where(lane == c + 16, middle[c], marks)
        marks = jnp.where(lane == c + 32, low[c], marks)
        units[:, c, :] = padded[c, :, 0:128]
        units[:, 12 + c, :] = padded[c, :, 128:256]
    for c in range(6):
        units[:, 24 + c, :] = padded[c, :, 256:384] + pltpu.roll(padded[c + 6, :, 256:384], 64, 1)
    units[:, 30, :] = marks
    units[:, 31, :] = jnp.zeros_like(marks)
    for sent_ref in sent_refs:
        sent_ref[0:templates] = to_bf16(units[...])
    table[...] = jnp.zeros_like(table)

    def clear(h, carry):
        used[h] = 0
        return carry

    lax.fori_loop(0, used.shape[0], clear, 0, unroll=8)
    lane = lanes_of((1, 128))

    def place(r, carry):
        k = r // rows_part
        station = station_ref[k, r % rows_part]
        block = block_ref[k, r % rows_part] & 31
        holder = station // 8
        rank = jnp.minimum(used[holder], CAP - 1)
        used[holder] = rank + 1
        slot = holder * CAP + rank
        place_ref[r] = slot
        entry = jnp.where(lane == 0, k, jnp.where(lane == 48, station & 7, jnp.where(lane == 49, block, 0)))
        table[pl.ds(slot, 1), :] = to_f32(entry)
        return carry

    lax.fori_loop(0, templates * rows_part, place, 0, unroll=8)
    here = lax.axis_index("wide") // PLANE
    for step, sent_ref in zip(Z_STEPS, sent_refs):
        start = pl.multiple_of((here + step) % len(Z_STEPS) * UNIT, UNIT)
        sent_ref[templates] = to_bf16(table[pl.ds(start, UNIT), :])


def pack(station, block, templates, holders):
    channels, count, _ = templates.shape
    smem = pl.BlockSpec(memory_space=pltpu.SMEM)
    vmem = pl.BlockSpec(memory_space=pltpu.VMEM)
    return pl.pallas_call(
        pack_kernel,
        out_shape=(
            *[jax.ShapeDtypeStruct((count + 1, UNIT, 128), jnp.bfloat16)] * len(Z_STEPS),
            jax.ShapeDtypeStruct((count * station.shape[1],), jnp.int32),
        ),
        in_specs=[smem, smem, vmem],
        out_specs=(*[vmem] * len(Z_STEPS), smem),
        scratch_shapes=[
            pltpu.VMEM((channels, count, 384), jnp.float32),
            pltpu.VMEM((count, UNIT, 128), jnp.float32),
            pltpu.VMEM((holders * CAP, 128), jnp.float32),
            pltpu.SMEM((holders,), jnp.int32),
        ],
        compiler_params=pltpu.CompilerParams(vmem_limit_bytes=VMEM_LIMIT),
    )(station, block, templates)


def member_after(member, step):
    return (member // Y + step[0]) % X * Y + (member % Y + step[1]) % Y


def route_kernel(*refs):
    sources = len(Z_STEPS)
    held_refs, sent_refs = refs[:sources], refs[sources : sources + PLANE]
    tables, staged, chosen_ref, sem = refs[sources + PLANE :]
    me = lax.axis_index("wide") % PLANE
    last = held_refs[0].shape[0] - 1
    for source, held_ref in enumerate(held_refs):
        tables[source] = to_f32(held_ref[last])
    entries = jnp.concatenate([held_ref[last] for held_ref in held_refs], axis=0)
    read_scalars(entries, ((0, 1),), staged, chosen_ref, sem)
    lane, row = lanes_of((16, 128)), rows_of((16, 128))
    marked = (row == 14) & (lane >= 48) & (lane < 50)
    for step, sent_ref in zip(PLANE_STEPS, sent_refs):
        first = member_after(me, step) * CAP
        for source, held_ref in enumerate(held_refs):
            for j in range(CAP):
                chosen = chosen_ref[0, source * UNIT + first + j]
                slot = source * CAP + j
                sent_ref[slot, 0:16, :] = held_ref[chosen, 0:16, :]
                upper = to_f32(held_ref[chosen, 16:32, :])
                entry = jnp.broadcast_to(tables[source, pl.ds(first + j, 1), :], (16, 128))
                sent_ref[slot, 16:32, :] = to_bf16(jnp.where(marked, entry, upper))


def route(held):
    sources = len(held)
    vmem = pl.BlockSpec(memory_space=pltpu.VMEM)
    return pl.pallas_call(
        route_kernel,
        out_shape=[jax.ShapeDtypeStruct((sources * CAP, UNIT, 128), jnp.bfloat16)] * PLANE,
        in_specs=[vmem] * sources,
        out_specs=[vmem] * PLANE,
        scratch_shapes=[
            pltpu.VMEM((sources, UNIT, 128), jnp.float32),
            pltpu.VMEM((8, sources * UNIT), jnp.int32),
            pltpu.SMEM((8, sources * UNIT), jnp.int32),
            pltpu.SemaphoreType.DMA,
        ],
        compiler_params=pltpu.CompilerParams(vmem_limit_bytes=VMEM_LIMIT),
    )(*held)


def station_kernel(wave_ref, tail_ref, shifted_ref, inverse_ref, signal, stacked):
    segment = wave_ref.shape[2]
    blocks = inverse_ref.shape[1]
    pieces = shifted_ref.shape[1]
    signal[CH:16, :] = jnp.zeros_like(signal[CH:16, :])
    signal[0:CH, 0:segment] = to_f32(wave_ref[0])
    signal[0:CH, segment:] = to_f32(tail_ref[0])
    lane, row = lanes_of((SHIFTS, 128)), rows_of((SHIFTS, 128))
    source = (lane + 8 * row) & 127
    inside = lane + 8 * row < 128

    for c in range(CH):
        before = None
        for piece in range(pieces + 1):
            here = jnp.broadcast_to(signal[c : c + 1, 128 * piece : 128 * piece + 128], (SHIFTS, 128))
            here = jnp.take_along_axis(here, source, axis=1)
            if piece > 0:
                shifted_ref[0, piece - 1, c] = to_bf16(jnp.where(inside, before, here))
            before = here
    for b in range(blocks):
        stacked[16 * b : 16 * b + 16, :] = signal[:, 128 * b : 128 * b + 512]
    sample, position = rows_of((512, 128)), lanes_of((512, 128))
    band = to_bf16(jnp.where((sample >= position) & (sample < position + L), 1.0, 0.0))
    values = stacked[...]
    squares = values * values
    high = to_bf16(squares)
    low = to_bf16(squares - to_f32(high))
    first = jnp.dot(to_bf16(values), band, preferred_element_type=jnp.float32) / L
    second = (
        jnp.dot(high, band, preferred_element_type=jnp.float32)
        + jnp.dot(low, band, preferred_element_type=jnp.float32)
    ) / L
    inverse = 1.0 / jnp.sqrt(second - first * first + EPS)
    inverse_ref[0] = inverse.reshape(blocks, 16, 128)


def station_tables(wave, tail):
    stations, channels, segment = wave.shape
    blocks = segment // BLK
    extra = tail.shape[2]
    return pl.pallas_call(
        station_kernel,
        grid=(stations,),
        out_shape=(
            jax.ShapeDtypeStruct((stations, blocks + 2, channels, SHIFTS, 128), jnp.bfloat16),
            jax.ShapeDtypeStruct((stations, blocks, 16, 128), jnp.float32),
        ),
        in_specs=[
            pl.BlockSpec((1, channels, segment), lambda s: (s, 0, 0)),
            pl.BlockSpec((1, channels, extra), lambda s: (s, 0, 0)),
        ],
        out_specs=(
            pl.BlockSpec((1, blocks + 2, channels, SHIFTS, 128), lambda s: (s, 0, 0, 0, 0)),
            pl.BlockSpec((1, blocks, 16, 128), lambda s: (s, 0, 0, 0)),
        ),
        scratch_shapes=[
            pltpu.VMEM((16, segment + extra), jnp.float32),
            pltpu.VMEM((16 * blocks, 512), jnp.float32),
        ],
        compiler_params=pltpu.CompilerParams(vmem_limit_bytes=VMEM_LIMIT),
        cost_estimate=pl.CostEstimate(flops=3_000_000_000, bytes_accessed=20_000_000, transcendentals=500_000),
    )(wave, tail)


def score_kernel(
    first_ref, second_ref, shifted_ref, inverse_ref, scores_ref, rows, marked, staged, codes, sem
):
    lane, row = lanes_of((8, 128)), rows_of((8, 128))
    before = lane < row
    member = lane // SHIFTS
    inverse_source = 8 * (lane % SHIFTS) + row
    natural_source = SHIFTS * row + lane // 8
    expand = to_bf16(jnp.where(lanes_of((GROUP, 256)) // SHIFTS == rows_of((GROUP, 256)), 1.0, 0.0))
    count = first_ref.shape[0]
    for start, units_ref in ((0, first_ref), (count, second_ref)):
        units = units_ref[...]
        marked[start : start + count] = units[:, 30, :]
        third = to_f32(units[:, 16:32, :])[:, 8:16, :]
        low_half = lanes_of(third.shape) < 64
        rows[start : start + count, 0:24, :] = to_f32(units)[:, 0:24, :]
        rows[start : start + count, 24:32, :] = jnp.where(low_half, third, 0.0)
        rows[start : start + count, 32:40, :] = jnp.where(low_half, pltpu.roll(third, 64, 2), 0.0)
    read_scalars(marked[...], ((48, 32), (49, 1)), staged, codes, sem)

    def template_rows(g, c):
        turned = []
        for r in (c, 12 + c, 24 + c if c < 6 else 26 + c):
            part = jnp.broadcast_to(rows[g, r : r + 1, :], (8, 128))
            turned.append(pltpu.roll(part, 0, 1, stride=1, stride_axis=0))
        return [
            jnp.where(before, 0.0, turned[0]),
            jnp.where(before, turned[0], turned[1]),
            jnp.where(before, turned[1], turned[2]),
        ]

    def score(group, carry):
        base = pl.multiple_of(group * GROUP, GROUP)
        marks = marked[pl.ds(base, GROUP), :]
        spread = lax.dot_general(marks, expand, TN, preferred_element_type=jnp.float32)
        factors = spread[0:12] + spread[16:28] + spread[32:44]
        totals = [jnp.zeros((8, 128), jnp.float32) for _ in range(2)]
        places = [(codes[0, base + g] // 32, codes[0, base + g] % 32) for g in range(GROUP)]
        for c in range(CH):
            pairs = []
            for pair in range(GROUP // 2):
                one, two = template_rows(base + 2 * pair, c), template_rows(base + 2 * pair + 1, c)
                both = [to_bf16(jnp.concatenate([one[a], two[a]], axis=0)) for a in range(3)]
                pairs.append(jnp.concatenate(both, axis=1))
            products = lax.dot_general(
                jnp.concatenate(pairs, axis=0),
                jnp.concatenate(
                    [
                        jnp.concatenate([shifted_ref[s, b + a, c] for s, b in places], axis=0)
                        for a in range(3)
                    ],
                    axis=1,
                ),
                NT,
                preferred_element_type=jnp.float32,
            )
            for half in range(2):
                chosen = jnp.zeros((8, 128), jnp.float32)
                scale = jnp.zeros((8, 128), jnp.float32)
                for m in range(8):
                    g = 8 * half + m
                    station, block = places[g]
                    inverse = jnp.broadcast_to(inverse_ref[station, block, c : c + 1, :], (8, 128))
                    inverse = jnp.take_along_axis(inverse, inverse_source, axis=1)
                    mine = products[8 * g : 8 * g + 8, 128 * half : 128 * half + 128]
                    chosen = jnp.where(member == m, mine, chosen)
                    scale = jnp.where(member == m, inverse, scale)
                factor = factors[c : c + 1, 128 * half : 128 * half + 128]
                totals[half] = totals[half] + chosen * scale * factor
        for half in range(2):
            natural = jnp.zeros((8, 128), jnp.float32)
            for i in range(8):
                spread_row = jnp.broadcast_to(totals[half][i : i + 1], (8, 128))
                spread_row = jnp.take_along_axis(spread_row, natural_source, axis=1)
                natural = jnp.where(lane % 8 == i, spread_row, natural)
            for o in range(2):
                scores_ref[group * 4 + half * 2 + o] = natural[4 * o : 4 * o + 4]
        return carry

    lax.fori_loop(0, 2 * count // GROUP, score, 0)


def slot_scores(first, second, shifted, inverse):
    slots = 2 * first.shape[0]
    vmem = pl.BlockSpec(memory_space=pltpu.VMEM)
    return pl.pallas_call(
        score_kernel,
        out_shape=jax.ShapeDtypeStruct((slots // CAP, CAP, BLK), jnp.float32),
        in_specs=[vmem] * 4,
        out_specs=vmem,
        scratch_shapes=[
            pltpu.VMEM((slots, 40, 128), jnp.float32),
            pltpu.VMEM((slots, 128), jnp.bfloat16),
            pltpu.VMEM((8, slots), jnp.int32),
            pltpu.SMEM((8, slots), jnp.int32),
            pltpu.SemaphoreType.DMA,
        ],
        compiler_params=pltpu.CompilerParams(vmem_limit_bytes=VMEM_LIMIT),
        cost_estimate=pl.CostEstimate(flops=4_000_000_000, bytes_accessed=4_000_000, transcendentals=0),
    )(first, second, shifted, inverse)


def arrange_kernel(*refs):
    scores_refs, out_ref = refs[:-1], refs[-1]
    z, me = lax.axis_index("wide") // PLANE, lax.axis_index("wide") % PLANE
    for number, step in enumerate(PLANE_STEPS):
        scores_ref, start = scores_refs[number // 2], number % 2 * len(Z_STEPS)
        member = member_after(me, (X - step[0], Y - step[1]))
        for source, offset in enumerate(Z_STEPS):
            owner = (z + len(Z_STEPS) - offset) % len(Z_STEPS) * PLANE + member
            out_ref[owner] = scores_ref[start + source]


def arrange(scores):
    vmem = pl.BlockSpec(memory_space=pltpu.VMEM)
    return pl.pallas_call(
        arrange_kernel,
        out_shape=jax.ShapeDtypeStruct((len(Z_STEPS) * PLANE, CAP, BLK), jnp.float32),
        in_specs=[vmem] * len(scores),
        out_specs=vmem,
        compiler_params=pltpu.CompilerParams(vmem_limit_bytes=VMEM_LIMIT),
    )(*scores)


def unpack_kernel(place_ref, limit_ref, scores_ref, out_ref):
    templates, rows_part, _ = out_ref.shape
    for k in range(templates):
        for r in range(rows_part):
            slot = place_ref[k * rows_part + r]
            found = scores_ref[slot // CAP, pl.ds(slot % CAP, 1), :]
            out_ref[k, r : r + 1, :] = jnp.where(r < limit_ref[k], found, 0.0)


def unpack(place, limit, scores, shape):
    smem = pl.BlockSpec(memory_space=pltpu.SMEM)
    vmem = pl.BlockSpec(memory_space=pltpu.VMEM)
    return pl.pallas_call(
        unpack_kernel,
        out_shape=jax.ShapeDtypeStruct(shape, jnp.float32),
        in_specs=[smem, smem, vmem],
        out_specs=vmem,
        compiler_params=pltpu.CompilerParams(vmem_limit_bytes=VMEM_LIMIT),
    )(place, limit, scores)


def local(waveforms, templates, det_station, det_block, det_count):
    own_count, rows_part = det_station.shape
    wide_count = lax.axis_size("wide")
    narrow_count = lax.axis_size("narrow")
    planes = wide_count // PLANE
    members = [(z, p) for z in range(planes) for p in range(PLANE)]
    *sent, place = pack(det_station, det_block, jnp.transpose(templates, (1, 0, 2)), wide_count)
    held = [sent[0]]
    for step, value in zip(Z_STEPS[1:], sent[1:]):
        pairs = [(PLANE * z + p, PLANE * ((z + step) % planes) + p) for z, p in members]
        held.append(lax.ppermute(value, "wide", pairs))
    tail = lax.ppermute(
        waveforms[:, :, : 3 * BLK], "narrow", [(i, i - 1) for i in range(1, narrow_count)]
    )
    shifted, inverse = station_tables(waveforms, tail)
    routed = route(held)
    arrived = []
    for step, units in zip(PLANE_STEPS, routed):
        if step != (0, 0):
            pairs = [(PLANE * z + p, PLANE * z + member_after(p, step)) for z, p in members]
            units = lax.ppermute(units, "wide", pairs)
        arrived.append(units)
    scores = [slot_scores(*arrived[i : i + 2], shifted, inverse) for i in range(0, PLANE, 2)]
    returned = lax.all_to_all(arrange(scores), "wide", split_axis=0, concat_axis=0, tiled=True)
    limit = det_count - lax.axis_index("narrow") * rows_part
    return unpack(place, limit, returned, (own_count, rows_part, BLK))


def solution(mesh):
    placed = (
        P("wide", None, "narrow"),
        P("wide", None, None),
        P("wide", "narrow"),
        P("wide", "narrow"),
        P("wide"),
    )
    return jax.shard_map(
        local, mesh=mesh, in_specs=placed, out_specs=P("wide", "narrow", None), check_vma=False
    )
```

time: 130 us -> 102 us (0.78)
  the two profiles are of different devices: /device:TPU:1 before, /device:TPU:8 now
where the time goes in v2:
time: 102 us
  starting transfers between devices  46.3 us (45%)
  Pallas kernels  32.4 us (32%)
  waiting for transfers between devices  19.2 us (19%)
  local copies, waits for them, and re-layouts  3.86 us (4%)
    ppermute x7, starting transfers between devices, local(): held.append(lax.ppermute(value, 'wide', pairs))  19.7 us
    pallas_call x4, Pallas kernels, slot_scores(): pl.pallas_call(score_kernel, out_shape=jax.ShapeDtypeStruct((slots // CAP...  19.3 us
    ppermute x7, starting transfers between devices, local(): units = lax.ppermute(units, 'wide', pairs)  15.4 us
    all_to_all x1, waiting for transfers between devices, local(): lax.all_to_all(arrange(scores), 'wide', split_axis=0, concat_axis=0, tile...  12.4 us
    all_to_all x1, starting transfers between devices, local(): lax.all_to_all(arrange(scores), 'wide', split_axis=0, concat_axis=0, tile...  9.28 us
    ppermute x7, waiting for transfers between devices, local(): units = lax.ppermute(units, 'wide', pairs)  5.74 us
    pallas_call x1, Pallas kernels, station_tables(): pl.pallas_call(station_kernel, grid=(stations,), out_shape=(jax.ShapeDtyp...  5.2 us
    unnamed x9, local copies, waits for them, and re-layouts  3.85 us
  transfers between devices with their start and end apart: 16, of which 3 were waited for; matrix products, arithmetic and copies ran while one was open for 2% of the time, Pallas kernels for 21%

profile of v2, /device:TPU:8, one launch (start us, length us, event | category | flops | bytes accessed | tf_op | source)
XLA Modules:
  0.0 101.9 jit_solution(17199176892247508144)
XLA Ops:
  0.0 0.9 copy-done
  0.9 0.7 copy-done.1
  1.6 0.7 copy-done.2
  2.3 3.6 %shard_map.55 = (bf16[9,32,128]{2,1,0:T(8,128)(2,1)S(1)}, bf16[9,32,128]{2,1,0:T(8,128)(2,1)S(1)}, bf16[9,32,128]{2,1,0:T(8,128)(2,1)S(1)}, bf16[9,32,128]{2,1,0...) custom-call(s32[8,16]{1,0:T(8,128)S(1)} %copy-done.1, ...), custom_call_target="tpu_custom_call" | custom-call | tf_op jit(solution)/shard_map/pallas_call | solution.py:113
  5.9 2.0 %collective-permute-start = (bf16[9,32,128]{2,1,0:T(8,128)(2,1)S(1)}, bf16[9,32,128]{2,1,0:T(8,128)(2,1)S(1)}, u32[]{:S(2)}, u32[]{:S(2)}) collective-permute-start(bf16[9,32,128]{2,1,0:T(8,128)(2,1)S(1)} %get-tuple-element.26), channel_id=1, source_target_pairs={{0,32},{4,36},{8,40},{12,44},{16,48},{20,52},{24,56},{28,60},{32,6... | collective-permute-start | bytes 221192 | tf_op jit(solution)/shard_map/ppermute | solution.py:396
  7.9 4.0 %collective-permute-start.1 = (bf16[9,32,128]{2,1,0:T(8,128)(2,1)S(1)}, bf16[9,32,128]{2,1,0:T(8,128)(2,1)S(1)}, u32[]{:S(2)}, u32[]{:S(2)}) collective-permute-start(bf16[9,32,128]{2,1,0:T(8,128)(2,1)S(1)} %get-tuple-element.27), channel_id=1, source_target_pairs={{0,224},{4,228},{8,232},{12,236},{16,240},{20,244},{24,248},{28,25... | collective-permute-start | bytes 221192 | tf_op jit(solution)/shard_map/ppermute | solution.py:396
  11.9 4.1 %collective-permute-start.3 = (bf16[9,32,128]{2,1,0:T(8,128)(2,1)S(1)}, bf16[9,32,128]{2,1,0:T(8,128)(2,1)S(1)}, u32[]{:S(2)}, u32[]{:S(2)}) collective-permute-start(bf16[9,32,128]{2,1,0:T(8,128)(2,1)S(1)} %get-tuple-element.29), channel_id=1, source_target_pairs={{0,192},{4,196},{8,200},{12,204},{16,208},{20,212},{24,216},{28,22... | collective-permute-start | bytes 221192 | tf_op jit(solution)/shard_map/ppermute | solution.py:396
  16.1 0.6 collective-permute-start.4
  16.7 4.4 %collective-permute-start.5 = (bf16[9,32,128]{2,1,0:T(8,128)(2,1)S(1)}, bf16[9,32,128]{2,1,0:T(8,128)(2,1)S(1)}, u32[]{:S(2)}, u32[]{:S(2)}) collective-permute-start(bf16[9,32,128]{2,1,0:T(8,128)(2,1)S(1)} %get-tuple-element.31), channel_id=1, source_target_pairs={{0,160},{4,164},{8,168},{12,172},{16,176},{20,180},{24,184},{28,18... | collective-permute-start | bytes 221192 | tf_op jit(solution)/shard_map/ppermute | solution.py:396
  21.1 4.5 %collective-permute-start.6 = (bf16[9,32,128]{2,1,0:T(8,128)(2,1)S(1)}, bf16[9,32,128]{2,1,0:T(8,128)(2,1)S(1)}, u32[]{:S(2)}, u32[]{:S(2)}) collective-permute-start(bf16[9,32,128]{2,1,0:T(8,128)(2,1)S(1)} %get-tuple-element.32), channel_id=1, source_target_pairs={{0,128},{4,132},{8,136},{12,140},{16,144},{20,148},{24,152},{28,15... | collective-permute-start | bytes 221192 | tf_op jit(solution)/shard_map/ppermute | solution.py:396
  25.6 1.6 %copy.7.wave_ref = bf16[8,12,4096]{2,1,0:T(8,128)(2,1)S(1)} copy(bf16[8,12,4096]{2,0,1:T(8,128)(2,1)} %param.5) | data formatting | bytes 1572864 | tf_op args[0]
  27.2 1.9 %collective-permute-start.8 = (bf16[8,12,384]{2,1,0:T(8,128)(2,1)S(1)}, bf16[8,12,384]{2,1,0:T(8,128)(2,1)S(1)}, u32[]{:S(2)}, u32[]{:S(2)}) collective-permute-start(bf16[8,12,384]{2,1,0:T(8,128)(2,1)S(1)} %slice.4), channel_id=1, source_target_pairs={{1,0},{2,1},{3,2},{5,4},{6,5},{7,6},{9,8},{10,9},{11,10},{13,12},{... | collective-permute-start | bytes 221192 | tf_op jit(solution)/shard_map/ppermute | solution.py:397
  29.2 1.0 collective-permute-done.6.refs_7_
  30.1 1.4 %shard_map.56 = (bf16[32,32,128]{2,1,0:T(8,128)(2,1)S(1)}, bf16[32,32,128]{2,1,0:T(8,128)(2,1)S(1)}, bf16[32,32,128]{2,1,0:T(8,128)(2,1)S(1)}, bf16[32,32,128]{2...) custom-call(bf16[9,32,128]{2,1,0:T(8,128)(2,1)S(1)} %get-tuple-eleme, ...), custom_call_target="tpu_custom_call" | custom-call | tf_op jit(solution)/shard_map/pallas_call | solution.py:162
  31.6 4.6 %collective-permute-start.13 = (bf16[32,32,128]{2,1,0:T(8,128)(2,1)S(1)}, bf16[32,32,128]{2,1,0:T(8,128)(2,1)S(1)}, u32[]{:S(2)}, u32[]{:S(2)}) collective-permute-start(bf16[32,32,128]{2,1,0:T(8,128)(2,1)S(1)} %get-tuple-element.41), channel_id=1, source_target_pairs={{0,28},{4,24},{8,4},{12,0},{16,12},{20,8},{24,20},{28,16},{32,60},... | collective-permute-start | bytes 786440 | tf_op jit(solution)/shard_map/ppermute | solution.py:406
  36.1 1.5 %collective-permute-start.14 = (bf16[32,32,128]{2,1,0:T(8,128)(2,1)S(1)}, bf16[32,32,128]{2,1,0:T(8,128)(2,1)S(1)}, u32[]{:S(2)}, u32[]{:S(2)}) collective-permute-start(bf16[32,32,128]{2,1,0:T(8,128)(2,1)S(1)} %get-tuple-element.42), channel_id=1, source_target_pairs={{0,20},{4,16},{8,28},{12,24},{16,4},{20,0},{24,12},{28,8},{32,52},... | collective-permute-start | bytes 786440 | tf_op jit(solution)/shard_map/ppermute | solution.py:406
  37.6 2.7 %collective-permute-start.11 = (bf16[32,32,128]{2,1,0:T(8,128)(2,1)S(1)}, bf16[32,32,128]{2,1,0:T(8,128)(2,1)S(1)}, u32[]{:S(2)}, u32[]{:S(2)}) collective-permute-start(bf16[32,32,128]{2,1,0:T(8,128)(2,1)S(1)} %get-tuple-element.39), channel_id=1, source_target_pairs={{0,16},{4,20},{8,24},{12,28},{16,0},{20,4},{24,8},{28,12},{32,48},... | collective-permute-start | bytes 786440 | tf_op jit(solution)/shard_map/ppermute | solution.py:406
  40.3 1.0 collective-permute-start.12
  41.3 1.3 %collective-permute-start.10 = (bf16[32,32,128]{2,1,0:T(8,128)(2,1)S(1)}, bf16[32,32,128]{2,1,0:T(8,128)(2,1)S(1)}, u32[]{:S(2)}, u32[]{:S(2)}) collective-permute-start(bf16[32,32,128]{2,1,0:T(8,128)(2,1)S(1)} %get-tuple-element.38), channel_id=1, source_target_pairs={{0,4},{4,0},{8,12},{12,8},{16,20},{20,16},{24,28},{28,24},{32,36},... | collective-permute-start | bytes 786440 | tf_op jit(solution)/shard_map/ppermute | solution.py:406
  42.6 5.2 %shard_map.57 = (bf16[8,34,12,16,128]{4,3,2,1,0:T(8,128)(2,1)S(1)}, f32[8,32,16,128]{3,2,1,0:T(8,128)S(1)}) custom-call(bf16[8,12,4096]{2,1,0:T(8,128)(2,1)S(1)} %copy.7.wave_ref, bf16[8,12,384]{2,1,0:T(8,128)(2,1)S(1)} %collective-permute-done.8.tail_ref), custom_call_target="tpu_custom_call" | custom-call | flops 3000000000 | bytes 20000000 | tf_op jit(solution)/shard_map/pallas_call | solution.py:217
  47.8 5.7 %collective-permute-done.13.first_ref = bf16[32,32,128]{2,1,0:T(8,128)(2,1)S(1)} collective-permute-done((bf16[32,32,128]{2,1,0:T(8,128)(2,1)S(1)}, bf16[32,32,128]{2,1,0:T(8,128)(2,1)S(1)}, u32[]{:S(2)}, u32[]{:S(2)}) %collective-permute-start.13) | collective-permute-done | bytes 262176 | tf_op jit(solution)/shard_map/ppermute | solution.py:406
  53.6 4.4 %collective-permute-start.9 = (bf16[32,32,128]{2,1,0:T(8,128)(2,1)S(1)}, bf16[32,32,128]{2,1,0:T(8,128)(2,1)S(1)}, u32[]{:S(2)}, u32[]{:S(2)}) collective-permute-start(bf16[32,32,128]{2,1,0:T(8,128)(2,1)S(1)} %get-tuple-element.37), channel_id=1, source_target_pairs={{0,24},{4,28},{8,0},{12,4},{16,8},{20,12},{24,16},{28,20},{32,56},... | collective-permute-start | bytes 786440 | tf_op jit(solution)/shard_map/ppermute | solution.py:406
  57.9 0.0 collective-permute-start.7
  57.9 4.8 %shard_map.61.refs_3_ = f32[16,4,128]{2,1,0:T(4,128)S(1)} custom-call(bf16[32,32,128]{2,1,0:T(8,128)(2,1)S(1)} %collective-permute-done.13.first_ref, bf16[32,32,128]{2,1,0:T(8,128)(2,1)S(1)} %collective-permute-done.14.second_ref, bf16[8,34,12,16,128]{4,3,2,1,0:T(8,128)(2,1)S(1)} %get-tuple-element.35.shifted_ref, ...), custom_call_target="tpu_custom_call" | custom-call | flops 4000000000 | bytes 4000000 | tf_op jit(solution)/shard_map/pallas_call | solution.py:326
  62.8 4.8 %shard_map.60.refs_2_ = f32[16,4,128]{2,1,0:T(4,128)S(1)} custom-call(bf16[32,32,128]{2,1,0:T(8,128)(2,1)S(1)} %collective-permute-done.11.first_ref, bf16[32,32,128]{2,1,0:T(8,128)(2,1)S(1)} %collective-permute-done.12.second_ref, bf16[8,34,12,16,128]{4,3,2,1,0:T(8,128)(2,1)S(1)} %get-tuple-element.35.shifted_ref, ...), custom_call_target="tpu_custom_call" | custom-call | flops 4000000000 | bytes 4000000 | tf_op jit(solution)/shard_map/pallas_call | solution.py:326
  67.6 0.0 copy-start.3
  67.6 4.8 %shard_map.59.refs_1_ = f32[16,4,128]{2,1,0:T(4,128)S(1)} custom-call(bf16[32,32,128]{2,1,0:T(8,128)(2,1)S(1)} %collective-permute-done.9.first_ref, bf16[32,32,128]{2,1,0:T(8,128)(2,1)S(1)} %collective-permute-done.10.second_ref, bf16[8,34,12,16,128]{4,3,2,1,0:T(8,128)(2,1)S(1)} %get-tuple-element.35.shifted_ref, ...), custom_call_target="tpu_custom_call" | custom-call | flops 4000000000 | bytes 4000000 | tf_op jit(solution)/shard_map/pallas_call | solution.py:326
  72.5 4.8 %shard_map.58.refs_0_ = f32[16,4,128]{2,1,0:T(4,128)S(1)} custom-call(bf16[32,32,128]{2,1,0:T(8,128)(2,1)S(1)} %get-tuple-element.33.first_ref, bf16[32,32,128]{2,1,0:T(8,128)(2,1)S(1)} %collective-permute-done.7.second_ref, bf16[8,34,12,16,128]{4,3,2,1,0:T(8,128)(2,1)S(1)} %get-tuple-element.35.shifted_ref, f32[8,32,16,128]{3,2,1,0:T(8,128)S(1)} %get-tuple-element.36.inverse_ref), custom_call_target="tpu_custom_call" | custom-call | flops 4000000000 | bytes 4000000 | tf_op jit(solution)/shard_map/pallas_call | solution.py:326
  77.3 0.8 shard_map.62
  78.1 9.3 %all-to-all-start = ((f32[64,4,128]{2,1,0:T(4,128)}), f32[64,4,128]{2,1,0:T(4,128)S(1)}, u32[]{:S(2)}, u32[]{:S(2)}) async-start(f32[64,4,128]{2,1,0:T(4,128)} %shard_map.62), calls=%async_computation | async-start | bytes 262144 | tf_op jit(solution)/shard_map/all_to_all | solution.py:409
  87.4 12.4 %all-to-all-done.scores_ref = f32[64,4,128]{2,1,0:T(4,128)S(1)} async-done(((f32[64,4,128]{2,1,0:T(4,128)}), f32[64,4,128]{2,1,0:T(4,128)S(1)}, u32[]{:S(2)}, u32[]{:S(2)}) %all-to-all-start) | async-done | bytes 131104 | tf_op jit(solution)/shard_map/all_to_all | solution.py:409
  99.8 2.1 %shard_map.63 = f32[8,16,128]{2,1,0:T(8,128)} custom-call(s32[128]{0:T(128)S(1)} %get-tuple-element.24.place_ref, s32[8]{0:T(128)S(1)} %broadcast_subtract_fusion.limit_ref, f32[64,4,128]{2,1,0:T(4,128)S(1)} %all-to-all-done.scores_ref), custom_call_target="tpu_custom_call" | custom-call | tf_op jit(solution)/shard_map/pallas_call | solution.py:377
  (20 shorter events, 0.1 us)
Async XLA Ops:
  0.0 0.9 copy-start
  0.9 0.7 copy-start.1
  1.6 0.7 copy-start.2
  5.9 10.8 %collective-permute-start = (bf16[9,32,128]{2,1,0:T(8,128)(2,1)S(1)}, bf16[9,32,128]{2,1,0:T(8,128)(2,1)S(1)}, u32[]{:S(2)}, u32[]{:S(2)}) collective-permute-start(bf16[9,32,128]{2,1,0:T(8,128)(2,1)S(1)} %get-tuple-element.26), channel_id=1, source_target_pairs={{0,32},{4,36},{8,40},{12,44},{16,48},{20,52},{24,56},{28,60},{32,6... | collective-permute-start | bytes 221192 | tf_op jit(solution)/shard_map/ppermute | solution.py:396
  7.9 13.2 %collective-permute-start.1 = (bf16[9,32,128]{2,1,0:T(8,128)(2,1)S(1)}, bf16[9,32,128]{2,1,0:T(8,128)(2,1)S(1)}, u32[]{:S(2)}, u32[]{:S(2)}) collective-permute-start(bf16[9,32,128]{2,1,0:T(8,128)(2,1)S(1)} %get-tuple-element.27), channel_id=1, source_target_pairs={{0,224},{4,228},{8,232},{12,236},{16,240},{20,244},{24,248},{28,25... | collective-permute-start | bytes 221192 | tf_op jit(solution)/shard_map/ppermute | solution.py:396
  11.9 15.3 %collective-permute-start.2 = (bf16[9,32,128]{2,1,0:T(8,128)(2,1)S(1)}, bf16[9,32,128]{2,1,0:T(8,128)(2,1)S(1)}, u32[]{:S(2)}, u32[]{:S(2)}) collective-permute-start(bf16[9,32,128]{2,1,0:T(8,128)(2,1)S(1)} %get-tuple-element.28), channel_id=1, source_target_pairs={{0,64},{4,68},{8,72},{12,76},{16,80},{20,84},{24,88},{28,92},{32,9... | collective-permute-start | bytes 221192 | tf_op jit(solution)/shard_map/ppermute | solution.py:396
  11.9 17.2 %collective-permute-start.3 = (bf16[9,32,128]{2,1,0:T(8,128)(2,1)S(1)}, bf16[9,32,128]{2,1,0:T(8,128)(2,1)S(1)}, u32[]{:S(2)}, u32[]{:S(2)}) collective-permute-start(bf16[9,32,128]{2,1,0:T(8,128)(2,1)S(1)} %get-tuple-element.29), channel_id=1, source_target_pairs={{0,192},{4,196},{8,200},{12,204},{16,208},{20,212},{24,216},{28,22... | collective-permute-start | bytes 221192 | tf_op jit(solution)/shard_map/ppermute | solution.py:396
  16.1 13.1 %collective-permute-start.4 = (bf16[9,32,128]{2,1,0:T(8,128)(2,1)S(1)}, bf16[9,32,128]{2,1,0:T(8,128)(2,1)S(1)}, u32[]{:S(2)}, u32[]{:S(2)}) collective-permute-start(bf16[9,32,128]{2,1,0:T(8,128)(2,1)S(1)} %get-tuple-element.30), channel_id=1, source_target_pairs={{0,96},{4,100},{8,104},{12,108},{16,112},{20,116},{24,120},{28,124... | collective-permute-start | bytes 221192 | tf_op jit(solution)/shard_map/ppermute | solution.py:396
  16.7 12.5 %collective-permute-start.5 = (bf16[9,32,128]{2,1,0:T(8,128)(2,1)S(1)}, bf16[9,32,128]{2,1,0:T(8,128)(2,1)S(1)}, u32[]{:S(2)}, u32[]{:S(2)}) collective-permute-start(bf16[9,32,128]{2,1,0:T(8,128)(2,1)S(1)} %get-tuple-element.31), channel_id=1, source_target_pairs={{0,160},{4,164},{8,168},{12,172},{16,176},{20,180},{24,184},{28,18... | collective-permute-start | bytes 221192 | tf_op jit(solution)/shard_map/ppermute | solution.py:396
  21.1 9.1 %collective-permute-start.6 = (bf16[9,32,128]{2,1,0:T(8,128)(2,1)S(1)}, bf16[9,32,128]{2,1,0:T(8,128)(2,1)S(1)}, u32[]{:S(2)}, u32[]{:S(2)}) collective-permute-start(bf16[9,32,128]{2,1,0:T(8,128)(2,1)S(1)} %get-tuple-element.32), channel_id=1, source_target_pairs={{0,128},{4,132},{8,136},{12,140},{16,144},{20,148},{24,152},{28,15... | collective-permute-start | bytes 221192 | tf_op jit(solution)/shard_map/ppermute | solution.py:396
  27.2 14.1 %collective-permute-start.8 = (bf16[8,12,384]{2,1,0:T(8,128)(2,1)S(1)}, bf16[8,12,384]{2,1,0:T(8,128)(2,1)S(1)}, u32[]{:S(2)}, u32[]{:S(2)}) collective-permute-start(bf16[8,12,384]{2,1,0:T(8,128)(2,1)S(1)} %slice.4), channel_id=1, source_target_pairs={{1,0},{2,1},{3,2},{5,4},{6,5},{7,6},{9,8},{10,9},{11,10},{13,12},{... | collective-permute-start | bytes 221192 | tf_op jit(solution)/shard_map/ppermute | solution.py:397
  31.6 22.0 %collective-permute-start.13 = (bf16[32,32,128]{2,1,0:T(8,128)(2,1)S(1)}, bf16[32,32,128]{2,1,0:T(8,128)(2,1)S(1)}, u32[]{:S(2)}, u32[]{:S(2)}) collective-permute-start(bf16[32,32,128]{2,1,0:T(8,128)(2,1)S(1)} %get-tuple-element.41), channel_id=1, source_target_pairs={{0,28},{4,24},{8,4},{12,0},{16,12},{20,8},{24,20},{28,16},{32,60},... | collective-permute-start | bytes 786440 | tf_op jit(solution)/shard_map/ppermute | solution.py:406
  36.1 21.8 %collective-permute-start.14 = (bf16[32,32,128]{2,1,0:T(8,128)(2,1)S(1)}, bf16[32,32,128]{2,1,0:T(8,128)(2,1)S(1)}, u32[]{:S(2)}, u32[]{:S(2)}) collective-permute-start(bf16[32,32,128]{2,1,0:T(8,128)(2,1)S(1)} %get-tuple-element.42), channel_id=1, source_target_pairs={{0,20},{4,16},{8,28},{12,24},{16,4},{20,0},{24,12},{28,8},{32,52},... | collective-permute-start | bytes 786440 | tf_op jit(solution)/shard_map/ppermute | solution.py:406
  37.6 25.2 %collective-permute-start.11 = (bf16[32,32,128]{2,1,0:T(8,128)(2,1)S(1)}, bf16[32,32,128]{2,1,0:T(8,128)(2,1)S(1)}, u32[]{:S(2)}, u32[]{:S(2)}) collective-permute-start(bf16[32,32,128]{2,1,0:T(8,128)(2,1)S(1)} %get-tuple-element.39), channel_id=1, source_target_pairs={{0,16},{4,20},{8,24},{12,28},{16,0},{20,4},{24,8},{28,12},{32,48},... | collective-permute-start | bytes 786440 | tf_op jit(solution)/shard_map/ppermute | solution.py:406
  40.3 22.4 %collective-permute-start.12 = (bf16[32,32,128]{2,1,0:T(8,128)(2,1)S(1)}, bf16[32,32,128]{2,1,0:T(8,128)(2,1)S(1)}, u32[]{:S(2)}, u32[]{:S(2)}) collective-permute-start(bf16[32,32,128]{2,1,0:T(8,128)(2,1)S(1)} %get-tuple-element.40), channel_id=1, source_target_pairs={{0,12},{4,8},{8,20},{12,16},{16,28},{20,24},{24,4},{28,0},{32,44},... | collective-permute-start | bytes 786440 | tf_op jit(solution)/shard_map/ppermute | solution.py:406
  41.3 26.3 %collective-permute-start.10 = (bf16[32,32,128]{2,1,0:T(8,128)(2,1)S(1)}, bf16[32,32,128]{2,1,0:T(8,128)(2,1)S(1)}, u32[]{:S(2)}, u32[]{:S(2)}) collective-permute-start(bf16[32,32,128]{2,1,0:T(8,128)(2,1)S(1)} %get-tuple-element.38), channel_id=1, source_target_pairs={{0,4},{4,0},{8,12},{12,8},{16,20},{20,16},{24,28},{28,24},{32,36},... | collective-permute-start | bytes 786440 | tf_op jit(solution)/shard_map/ppermute | solution.py:406
  53.6 14.1 %collective-permute-start.9 = (bf16[32,32,128]{2,1,0:T(8,128)(2,1)S(1)}, bf16[32,32,128]{2,1,0:T(8,128)(2,1)S(1)}, u32[]{:S(2)}, u32[]{:S(2)}) collective-permute-start(bf16[32,32,128]{2,1,0:T(8,128)(2,1)S(1)} %get-tuple-element.37), channel_id=1, source_target_pairs={{0,24},{4,28},{8,0},{12,4},{16,8},{20,12},{24,16},{28,20},{32,56},... | collective-permute-start | bytes 786440 | tf_op jit(solution)/shard_map/ppermute | solution.py:406
  57.9 14.5 %collective-permute-start.7 = (bf16[32,32,128]{2,1,0:T(8,128)(2,1)S(1)}, bf16[32,32,128]{2,1,0:T(8,128)(2,1)S(1)}, u32[]{:S(2)}, u32[]{:S(2)}) collective-permute-start(bf16[32,32,128]{2,1,0:T(8,128)(2,1)S(1)} %get-tuple-element.34), channel_id=1, source_target_pairs={{0,8},{4,12},{8,16},{12,20},{16,24},{20,28},{24,0},{28,4},{32,40},... | collective-permute-start | bytes 786440 | tf_op jit(solution)/shard_map/ppermute | solution.py:406
  67.6 19.8 %copy-start.3 = (s32[8]{0:T(128)S(1)}, s32[8]{0:T(128)}, u32[]{:S(2)}) copy-start(s32[8]{0:T(128)} %param.9) | copy-start | bytes 100
  78.1 21.8 %all-to-all-start = ((f32[64,4,128]{2,1,0:T(4,128)}), f32[64,4,128]{2,1,0:T(4,128)S(1)}, u32[]{:S(2)}, u32[]{:S(2)}) async-start(f32[64,4,128]{2,1,0:T(4,128)} %shard_map.62), calls=%async_computation | async-start | bytes 262144 | tf_op jit(solution)/shard_map/all_to_all | solution.py:409

commit v3 on v2

--- a/solution.py
+++ b/solution.py
@@ -14,7 +14,7 @@
 PLANE = 8
 X, Y = 4, 2
 PLANE_STEPS = ((0, 0), (1, 0), (3, 0), (0, 1), (2, 0), (1, 1), (3, 1), (2, 1))
-Z_STEPS = (0, 1, 7, 2, 6, 3, 5, 4)
+CALLS = ((1, 2), (3, 4), (5, 6), (0, 7))
 SHIFTS = 16
 GROUP = 16
 VMEM_LIMIT = 24 * 1024 * 1024
@@ -47,11 +47,10 @@
     staged[...] = values.astype(jnp.int32)
     copy = pltpu.make_async_copy(staged, scalars, sem)
     copy.start()
-    copy.wait()
-
-
-def pack_kernel(station_ref, block_ref, templates_ref, *refs):
-    sent_refs, (place_ref, padded, units, table, used) = refs[: len(Z_STEPS)], refs[len(Z_STEPS) :]
+    return copy
+
+
+def pack_kernel(station_ref, block_ref, templates_ref, sent_ref, place_ref, padded, units, table, used):
     channels, templates, _ = templates_ref.shape
     rows_part = station_ref.shape[1]
     values = to_f32(templates_ref[...])
@@ -75,8 +74,8 @@
         units[:, 24 + c, :] = padded[c, :, 256:384] + pltpu.roll(padded[c + 6, :, 256:384], 64, 1)
     units[:, 30, :] = marks
     units[:, 31, :] = jnp.zeros_like(marks)
-    for sent_ref in sent_refs:
-        sent_ref[0:templates] = to_bf16(units[...])
+    for z in range(sent_ref.shape[0]):
+        sent_ref[z, 0:templates] = to_bf16(units[...])
     table[...] = jnp.zeros_like(table)
 
     def clear(h, carry):
@@ -100,10 +99,8 @@
         return carry
 
     lax.fori_loop(0, templates * rows_part, place, 0, unroll=8)
-    here = lax.axis_index("wide") // PLANE
-    for step, sent_ref in zip(Z_STEPS, sent_refs):
-        start = pl.multiple_of((here + step) % len(Z_STEPS) * UNIT, UNIT)
-        sent_ref[templates] = to_bf16(table[pl.ds(start, UNIT), :])
+    for z in range(sent_ref.shape[0]):
+        sent_ref[z, templates] = to_bf16(table[UNIT * z : UNIT * z + UNIT, :])
 
 
 def pack(station, block, templates, holders):
@@ -113,18 +110,18 @@
     return pl.pallas_call(
         pack_kernel,
         out_shape=(
-            *[jax.ShapeDtypeStruct((count + 1, UNIT, 128), jnp.bfloat16)] * len(Z_STEPS),
+            jax.ShapeDtypeStruct((holders // PLANE, count + 1, UNIT, 128), jnp.bfloat16),
             jax.ShapeDtypeStruct((count * station.shape[1],), jnp.int32),
         ),
         in_specs=[smem, smem, vmem],
-        out_specs=(*[vmem] * len(Z_STEPS), smem),
+        out_specs=(vmem, smem),
         scratch_shapes=[
             pltpu.VMEM((channels, count, 384), jnp.float32),
             pltpu.VMEM((count, UNIT, 128), jnp.float32),
             pltpu.VMEM((holders * CAP, 128), jnp.float32),
             pltpu.SMEM((holders,), jnp.int32),
         ],
-        compiler_params=pltpu.CompilerParams(vmem_limit_bytes=VMEM_LIMIT),
+        compiler_params=pltpu.CompilerParams(vmem_limit_bytes=60 * 1024 * 1024),
     )(station, block, templates)
 
 
@@ -132,37 +129,35 @@
     return (member // Y + step[0]) % X * Y + (member % Y + step[1]) % Y
 
 
-def route_kernel(*refs):
-    sources = len(Z_STEPS)
-    held_refs, sent_refs = refs[:sources], refs[sources : sources + PLANE]
-    tables, staged, chosen_ref, sem = refs[sources + PLANE :]
+def route_kernel(held_ref, ready_ref, *refs):
+    sources = held_ref.shape[0]
+    sent_refs, (tables, staged, chosen_ref, sem) = refs[:PLANE], refs[PLANE:]
     me = lax.axis_index("wide") % PLANE
-    last = held_refs[0].shape[0] - 1
-    for source, held_ref in enumerate(held_refs):
-        tables[source] = to_f32(held_ref[last])
-    entries = jnp.concatenate([held_ref[last] for held_ref in held_refs], axis=0)
-    read_scalars(entries, ((0, 1),), staged, chosen_ref, sem)
+    last = held_ref.shape[1] - 1
+    tables[...] = to_f32(held_ref[:, last])
+    entries = jnp.concatenate([held_ref[source, last] for source in range(sources)], axis=0)
+    read_scalars(entries, ((0, 1),), staged, chosen_ref, sem).wait()
     lane, row = lanes_of((16, 128)), rows_of((16, 128))
     marked = (row == 14) & (lane >= 48) & (lane < 50)
     for step, sent_ref in zip(PLANE_STEPS, sent_refs):
         first = member_after(me, step) * CAP
-        for source, held_ref in enumerate(held_refs):
+        for source in range(sources):
             for j in range(CAP):
                 chosen = chosen_ref[0, source * UNIT + first + j]
                 slot = source * CAP + j
-                sent_ref[slot, 0:16, :] = held_ref[chosen, 0:16, :]
-                upper = to_f32(held_ref[chosen, 16:32, :])
+                sent_ref[slot, 0:16, :] = held_ref[source, chosen, 0:16, :]
+                upper = to_f32(held_ref[source, chosen, 16:32, :])
                 entry = jnp.broadcast_to(tables[source, pl.ds(first + j, 1), :], (16, 128))
                 sent_ref[slot, 16:32, :] = to_bf16(jnp.where(marked, entry, upper))
 
 
-def route(held):
-    sources = len(held)
+def route(held, ready):
+    sources = held.shape[0]
     vmem = pl.BlockSpec(memory_space=pltpu.VMEM)
     return pl.pallas_call(
         route_kernel,
         out_shape=[jax.ShapeDtypeStruct((sources * CAP, UNIT, 128), jnp.bfloat16)] * PLANE,
-        in_specs=[vmem] * sources,
+        in_specs=[vmem, pl.BlockSpec(memory_space=pl.ANY)],
         out_specs=[vmem] * PLANE,
         scratch_shapes=[
             pltpu.VMEM((sources, UNIT, 128), jnp.float32),
@@ -171,7 +166,8 @@
             pltpu.SemaphoreType.DMA,
         ],
         compiler_params=pltpu.CompilerParams(vmem_limit_bytes=VMEM_LIMIT),
-    )(*held)
+        cost_estimate=pl.CostEstimate(flops=10_000_000_000, bytes_accessed=40_000_000, transcendentals=0),
+    )(held, ready)
 
 
 def station_kernel(wave_ref, tail_ref, shifted_ref, inverse_ref, signal, stacked):
@@ -249,14 +245,16 @@
     expand = to_bf16(jnp.where(lanes_of((GROUP, 256)) // SHIFTS == rows_of((GROUP, 256)), 1.0, 0.0))
     count = first_ref.shape[0]
     for start, units_ref in ((0, first_ref), (count, second_ref)):
+        marked[start : start + count] = units_ref[:, 30, :]
+    copy = read_scalars(marked[...], ((48, 32), (49, 1)), staged, codes, sem)
+    for start, units_ref in ((0, first_ref), (count, second_ref)):
         units = units_ref[...]
-        marked[start : start + count] = units[:, 30, :]
         third = to_f32(units[:, 16:32, :])[:, 8:16, :]
         low_half = lanes_of(third.shape) < 64
         rows[start : start + count, 0:24, :] = to_f32(units)[:, 0:24, :]
         rows[start : start + count, 24:32, :] = jnp.where(low_half, third, 0.0)
         rows[start : start + count, 32:40, :] = jnp.where(low_half, pltpu.roll(third, 64, 2), 0.0)
-    read_scalars(marked[...], ((48, 32), (49, 1)), staged, codes, sem)
+    copy.wait()
 
     def template_rows(g, c):
         turned = []
@@ -342,20 +340,21 @@
 
 def arrange_kernel(*refs):
     scores_refs, out_ref = refs[:-1], refs[-1]
-    z, me = lax.axis_index("wide") // PLANE, lax.axis_index("wide") % PLANE
-    for number, step in enumerate(PLANE_STEPS):
-        scores_ref, start = scores_refs[number // 2], number % 2 * len(Z_STEPS)
-        member = member_after(me, (X - step[0], Y - step[1]))
-        for source, offset in enumerate(Z_STEPS):
-            owner = (z + len(Z_STEPS) - offset) % len(Z_STEPS) * PLANE + member
-            out_ref[owner] = scores_ref[start + source]
+    me = lax.axis_index("wide") % PLANE
+    planes = out_ref.shape[0] // PLANE
+    for scores_ref, pair in zip(scores_refs, CALLS):
+        for place, number in enumerate(pair):
+            step = PLANE_STEPS[number]
+            member = member_after(me, (X - step[0], Y - step[1]))
+            for z in range(planes):
+                out_ref[z * PLANE + member] = scores_ref[place * planes + z]
 
 
 def arrange(scores):
     vmem = pl.BlockSpec(memory_space=pltpu.VMEM)
     return pl.pallas_call(
         arrange_kernel,
-        out_shape=jax.ShapeDtypeStruct((len(Z_STEPS) * PLANE, CAP, BLK), jnp.float32),
+        out_shape=jax.ShapeDtypeStruct((len(scores) * scores[0].shape[0], CAP, BLK), jnp.float32),
         in_specs=[vmem] * len(scores),
         out_specs=vmem,
         compiler_params=pltpu.CompilerParams(vmem_limit_bytes=VMEM_LIMIT),
@@ -389,23 +388,28 @@
     narrow_count = lax.axis_size("narrow")
     planes = wide_count // PLANE
     members = [(z, p) for z in range(planes) for p in range(PLANE)]
-    *sent, place = pack(det_station, det_block, jnp.transpose(templates, (1, 0, 2)), wide_count)
-    held = [sent[0]]
-    for step, value in zip(Z_STEPS[1:], sent[1:]):
-        pairs = [(PLANE * z + p, PLANE * ((z + step) % planes) + p) for z, p in members]
-        held.append(lax.ppermute(value, "wide", pairs))
+    sent, place = pack(det_station, det_block, jnp.transpose(templates, (1, 0, 2)), wide_count)
+    held = lax.all_to_all(
+        sent.reshape(planes, (own_count + 1) * UNIT, 128),
+        "wide",
+        split_axis=0,
+        concat_axis=0,
+        tiled=True,
+        axis_index_groups=[[PLANE * z + p for z in range(planes)] for p in range(PLANE)],
+    )
+    held = held.reshape(planes, own_count + 1, UNIT, 128)
     tail = lax.ppermute(
         waveforms[:, :, : 3 * BLK], "narrow", [(i, i - 1) for i in range(1, narrow_count)]
     )
     shifted, inverse = station_tables(waveforms, tail)
-    routed = route(held)
+    routed = route(held, inverse)
     arrived = []
     for step, units in zip(PLANE_STEPS, routed):
         if step != (0, 0):
             pairs = [(PLANE * z + p, PLANE * z + member_after(p, step)) for z, p in members]
             units = lax.ppermute(units, "wide", pairs)
         arrived.append(units)
-    scores = [slot_scores(*arrived[i : i + 2], shifted, inverse) for i in range(0, PLANE, 2)]
+    scores = [slot_scores(arrived[a], arrived[b], shifted, inverse) for a, b in CALLS]
     returned = lax.all_to_all(arrange(scores), "wide", split_axis=0, concat_axis=0, tiled=True)
     limit = det_count - lax.axis_index("narrow") * rows_part
     return unpack(place, limit, returned, (own_count, rows_part, BLK))

time: 102 us -> 98.2 us (0.963); the launches traced: 102 us -> 97.1 us
  starting transfers between devices: 46.3 us -> 36.1 us
  waiting for transfers between devices: 19.2 us -> 21.8 us
  local copies, waits for them, and re-layouts: 3.86 us -> 6.4 us
    ppermute x7 -> x0, starting transfers between devices: 19.7 us -> none  [local(): held.append(lax.ppermute(value, 'wide', pairs))]
    all_to_all x0 -> x1, starting transfers between devices: none -> 8.48 us  [local(): lax.all_to_all(sent.reshape(planes, (own_count + 1) * UNIT, 128), 'wide',...]
    all_to_all x0 -> x1, waiting for transfers between devices: none -> 3.16 us  [local(): lax.all_to_all(sent.reshape(planes, (own_count + 1) * UNIT, 128), 'wide',...]
    unnamed x9, local copies, waits for them, and re-layouts: 3.85 us -> 6.39 us
    ppermute x7, starting transfers between devices: 15.4 us -> 17.6 us  [local(): units = lax.ppermute(units, 'wide', pairs)]
    ppermute x1, waiting for transfers between devices: 0.01 us -> 2.19 us  [local(): lax.ppermute(waveforms[:, :, :3 * BLK], 'narrow', [(i, i - 1) for i in ra...]
    ppermute x7, waiting for transfers between devices: 5.74 us -> 3.9 us  [local(): units = lax.ppermute(units, 'wide', pairs)]
    all_to_all x1, starting transfers between devices: 9.28 us -> 8.07 us  [local(): lax.all_to_all(arrange(scores), 'wide', split_axis=0, concat_axis=0, tile...]
  transfers between devices with their start and end apart: 16 -> 10, of which waited for: 3 -> 5; matrix products, arithmetic and copies ran while one was open for 2% -> 2% of each run, Pallas kernels for 21% -> 20%
where the time goes in v3:
time: 98.2 us; the launch traced here: 97.1 us
  starting transfers between devices  36.1 us (37%)
  Pallas kernels  32.6 us (33%)
  waiting for transfers between devices  21.8 us (22%)
  local copies, waits for them, and re-layouts  6.4 us (7%)
    pallas_call x4, Pallas kernels, slot_scores(): pl.pallas_call(score_kernel, out_shape=jax.ShapeDtypeStruct((slots // CAP...  19.1 us
    ppermute x7, starting transfers between devices, local(): units = lax.ppermute(units, 'wide', pairs)  17.6 us
    all_to_all x1, waiting for transfers between devices, local(): lax.all_to_all(arrange(scores), 'wide', split_axis=0, concat_axis=0, tile...  12.5 us
    all_to_all x1, starting transfers between devices, local(): lax.all_to_all(sent.reshape(planes, (own_count + 1) * UNIT, 128), 'wide',...  8.48 us
    all_to_all x1, starting transfers between devices, local(): lax.all_to_all(arrange(scores), 'wide', split_axis=0, concat_axis=0, tile...  8.07 us
    unnamed x9, local copies, waits for them, and re-layouts  6.39 us
    pallas_call x1, Pallas kernels, station_tables(): pl.pallas_call(station_kernel, grid=(stations,), out_shape=(jax.ShapeDtyp...  5.2 us
    pallas_call x1, Pallas kernels, pack(): pl.pallas_call(pack_kernel, out_shape=(jax.ShapeDtypeStruct((holders // P...  4.1 us
  transfers between devices with their start and end apart: 10, of which 5 were waited for; matrix products, arithmetic and copies ran while one was open for 2% of the time, Pallas kernels for 20%

profile of v3, /device:TPU:8, one launch (start us, length us, event | category | flops | bytes accessed | tf_op | source)
XLA Modules:
  0.0 97.1 jit_solution(5358779076539769731)
XLA Ops:
  0.0 4.1 %shard_map.55 = (bf16[8,9,32,128]{3,2,1,0:T(8,128)(2,1)}, s32[128]{0:T(128)}) custom-call(s32[8,16]{1,0:T(8,128)} %station_ref.1, s32[8,16]{1,0:T(8,128)} %block_ref.1, bf16[12,8,300]{2,1,0:T(8,128)(2,1)} %bitcast.5), custom_call_target="tpu_custom_call" | custom-call | tf_op jit(solution)/shard_map/pallas_call | solution.py:110
  4.1 8.5 %all-to-all-start = ((bf16[8,288,128]{2,1,0:T(8,128)(2,1)}), bf16[8,288,128]{2,1,0:T(8,128)(2,1)S(1)}, u32[]{:S(2)}, u32[]{:S(2)}) async-start(bf16[8,288,128]{2,1,0:T(8,128)(2,1)} %bitcast.4), calls=%async_computation | async-start | bytes 1179648 | tf_op jit(solution)/shard_map/all_to_all | solution.py:392
  12.6 1.6 %copy.7.wave_ref = bf16[8,12,4096]{2,1,0:T(8,128)(2,1)S(1)} copy(bf16[8,12,4096]{2,0,1:T(8,128)(2,1)} %param.5) | data formatting | bytes 1572864 | tf_op args[0]
  14.2 1.9 %collective-permute-start = (bf16[8,12,384]{2,1,0:T(8,128)(2,1)S(1)}, bf16[8,12,384]{2,1,0:T(8,128)(2,1)S(1)}, u32[]{:S(2)}, u32[]{:S(2)}) collective-permute-start(bf16[8,12,384]{2,1,0:T(8,128)(2,1)S(1)} %slice.4), channel_id=1, source_target_pairs={{1,0},{2,1},{3,2},{5,4},{6,5},{7,6},{9,8},{10,9},{11,10},{13,12},{... | collective-permute-start | bytes 221192 | tf_op jit(solution)/shard_map/ppermute | solution.py:401
  16.1 2.2 %collective-permute-done.tail_ref = bf16[8,12,384]{2,1,0:T(8,128)(2,1)S(1)} collective-permute-done((bf16[8,12,384]{2,1,0:T(8,128)(2,1)S(1)}, bf16[8,12,384]{2,1,0:T(8,128)(2,1)S(1)}, u32[]{:S(2)}, u32[]{:S(2)}) %collective-permute-start) | collective-permute-done | bytes 73760 | tf_op jit(solution)/shard_map/ppermute | solution.py:401
  18.3 5.2 %shard_map.56 = (bf16[8,34,12,16,128]{4,3,2,1,0:T(8,128)(2,1)S(1)}, f32[8,32,16,128]{3,2,1,0:T(8,128)S(1)}) custom-call(bf16[8,12,4096]{2,1,0:T(8,128)(2,1)S(1)} %copy.7.wave_ref, bf16[8,12,384]{2,1,0:T(8,128)(2,1)S(1)} %collective-permute-done.tail_ref), custom_call_target="tpu_custom_call" | custom-call | flops 3000000000 | bytes 20000000 | tf_op jit(solution)/shard_map/pallas_call | solution.py:213
  23.5 4.8 %copy-done = bf16[8,34,12,16,128]{4,3,2,1,0:T(8,128)(2,1)} copy-done((bf16[8,34,12,16,128]{4,3,2,1,0:T(8,128)(2,1)}, bf16[8,34,12,16,128]{4,3,2,1,0:T(8,128)(2,1)S(1)}, u32[]{:S(2)}) %copy-start) | copy-done | bytes 13369368
  28.3 3.2 %all-to-all-done = bf16[8,288,128]{2,1,0:T(8,128)(2,1)S(1)} async-done(((bf16[8,288,128]{2,1,0:T(8,128)(2,1)}), bf16[8,288,128]{2,1,0:T(8,128)(2,1)S(1)}, u32[]{:S(2)}, u32[]{:S(2)}) %all-to-all-start) | async-done | bytes 589856 | tf_op jit(solution)/shard_map/all_to_all | solution.py:392
  31.5 1.4 %shard_map.57 = (bf16[32,32,128]{2,1,0:T(8,128)(2,1)S(1)}, bf16[32,32,128]{2,1,0:T(8,128)(2,1)S(1)}, bf16[32,32,128]{2,1,0:T(8,128)(2,1)S(1)}, bf16[32,32,128]{2...) custom-call(bf16[8,9,32,128]{3,2,1,0:T(8,128)(2,1)S(1)} %bitcast.3, ...), custom_call_target="tpu_custom_call" | custom-call | flops 10000000000 | bytes 40000000 | tf_op jit(solution)/shard_map/pallas_call | solution.py:157
  32.9 4.8 %collective-permute-start.7 = (bf16[32,32,128]{2,1,0:T(8,128)(2,1)S(1)}, bf16[32,32,128]{2,1,0:T(8,128)(2,1)S(1)}, u32[]{:S(2)}, u32[]{:S(2)}) collective-permute-start(bf16[32,32,128]{2,1,0:T(8,128)(2,1)S(1)} %get-tuple-element.28), channel_id=1, source_target_pairs={{0,20},{4,16},{8,28},{12,24},{16,4},{20,0},{24,12},{28,8},{32,52},... | collective-permute-start | bytes 786440 | tf_op jit(solution)/shard_map/ppermute | solution.py:410
  37.7 1.3 %collective-permute-start.5 = (bf16[32,32,128]{2,1,0:T(8,128)(2,1)S(1)}, bf16[32,32,128]{2,1,0:T(8,128)(2,1)S(1)}, u32[]{:S(2)}, u32[]{:S(2)}) collective-permute-start(bf16[32,32,128]{2,1,0:T(8,128)(2,1)S(1)} %get-tuple-element.25), channel_id=1, source_target_pairs={{0,12},{4,8},{8,20},{12,16},{16,28},{20,24},{24,4},{28,0},{32,44},... | collective-permute-start | bytes 786440 | tf_op jit(solution)/shard_map/ppermute | solution.py:410
  39.0 4.4 %collective-permute-start.6 = (bf16[32,32,128]{2,1,0:T(8,128)(2,1)S(1)}, bf16[32,32,128]{2,1,0:T(8,128)(2,1)S(1)}, u32[]{:S(2)}, u32[]{:S(2)}) collective-permute-start(bf16[32,32,128]{2,1,0:T(8,128)(2,1)S(1)} %get-tuple-element.26), channel_id=1, source_target_pairs={{0,28},{4,24},{8,4},{12,0},{16,12},{20,8},{24,20},{28,16},{32,60},... | collective-permute-start | bytes 786440 | tf_op jit(solution)/shard_map/ppermute | solution.py:410
  43.4 1.2 %collective-permute-start.3 = (bf16[32,32,128]{2,1,0:T(8,128)(2,1)S(1)}, bf16[32,32,128]{2,1,0:T(8,128)(2,1)S(1)}, u32[]{:S(2)}, u32[]{:S(2)}) collective-permute-start(bf16[32,32,128]{2,1,0:T(8,128)(2,1)S(1)} %get-tuple-element.23), channel_id=1, source_target_pairs={{0,4},{4,0},{8,12},{12,8},{16,20},{20,16},{24,28},{28,24},{32,36},... | collective-permute-start | bytes 786440 | tf_op jit(solution)/shard_map/ppermute | solution.py:410
  44.6 0.0 collective-permute-start.4
  44.6 2.4 %collective-permute-done.7.second_ref = bf16[32,32,128]{2,1,0:T(8,128)(2,1)S(1)} collective-permute-done((bf16[32,32,128]{2,1,0:T(8,128)(2,1)S(1)}, bf16[32,32,128]{2,1,0:T(8,128)(2,1)S(1)}, u32[]{:S(2)}, u32[]{:S(2)}) %collective-permute-start.7) | collective-permute-done | bytes 262176 | tf_op jit(solution)/shard_map/ppermute | solution.py:410
  47.0 1.6 %collective-permute-start.1 = (bf16[32,32,128]{2,1,0:T(8,128)(2,1)S(1)}, bf16[32,32,128]{2,1,0:T(8,128)(2,1)S(1)}, u32[]{:S(2)}, u32[]{:S(2)}) collective-permute-start(bf16[32,32,128]{2,1,0:T(8,128)(2,1)S(1)} %get-tuple-element.20), channel_id=1, source_target_pairs={{0,8},{4,12},{8,16},{12,20},{16,24},{20,28},{24,0},{28,4},{32,40},... | collective-permute-start | bytes 786440 | tf_op jit(solution)/shard_map/ppermute | solution.py:410
  48.6 4.8 %shard_map.61.refs_3_ = f32[16,4,128]{2,1,0:T(4,128)S(1)} custom-call(bf16[32,32,128]{2,1,0:T(8,128)(2,1)S(1)} %get-tuple-element.27.first_ref, bf16[32,32,128]{2,1,0:T(8,128)(2,1)S(1)} %collective-permute-done.7.second_ref, bf16[8,34,12,16,128]{4,3,2,1,0:T(8,128)(2,1)S(1)} %copy-done.1, f32[8,32,16,128]{3,2,1,0:T(8,128)S(1)} %get-tuple-element.19.ready_ref.inverse_ref), custom_call_target="tpu_custom_call" | custom-call | flops 4000000000 | bytes 4000000 | tf_op jit(solution)/shard_map/pallas_call | solution.py:324
  53.4 1.5 %collective-permute-done.5.first_ref = bf16[32,32,128]{2,1,0:T(8,128)(2,1)S(1)} collective-permute-done((bf16[32,32,128]{2,1,0:T(8,128)(2,1)S(1)}, bf16[32,32,128]{2,1,0:T(8,128)(2,1)S(1)}, u32[]{:S(2)}, u32[]{:S(2)}) %collective-permute-start.5) | collective-permute-done | bytes 262176 | tf_op jit(solution)/shard_map/ppermute | solution.py:410
  54.9 4.3 %collective-permute-start.2 = (bf16[32,32,128]{2,1,0:T(8,128)(2,1)S(1)}, bf16[32,32,128]{2,1,0:T(8,128)(2,1)S(1)}, u32[]{:S(2)}, u32[]{:S(2)}) collective-permute-start(bf16[32,32,128]{2,1,0:T(8,128)(2,1)S(1)} %get-tuple-element.21), channel_id=1, source_target_pairs={{0,24},{4,28},{8,0},{12,4},{16,8},{20,12},{24,16},{28,20},{32,56},... | collective-permute-start | bytes 786440 | tf_op jit(solution)/shard_map/ppermute | solution.py:410
  59.2 0.0 collective-permute-done.6.second_ref
  59.2 4.8 %shard_map.60.refs_2_ = f32[16,4,128]{2,1,0:T(4,128)S(1)} custom-call(bf16[32,32,128]{2,1,0:T(8,128)(2,1)S(1)} %collective-permute-done.5.first_ref, bf16[32,32,128]{2,1,0:T(8,128)(2,1)S(1)} %collective-permute-done.6.second_ref, bf16[8,34,12,16,128]{4,3,2,1,0:T(8,128)(2,1)S(1)} %copy-done.1, f32[8,32,16,128]{3,2,1,0:T(8,128)S(1)} %get-tuple-element.19.ready_ref.inverse_ref), custom_call_target="tpu_custom_call" | custom-call | flops 4000000000 | bytes 4000000 | tf_op jit(solution)/shard_map/pallas_call | solution.py:324
  64.0 0.0 copy-start.3
  64.0 0.0 copy-start.2
  64.1 0.0 collective-permute-done.4.second_ref
  64.1 4.8 %shard_map.59.refs_1_ = f32[16,4,128]{2,1,0:T(4,128)S(1)} custom-call(bf16[32,32,128]{2,1,0:T(8,128)(2,1)S(1)} %collective-permute-done.3.first_ref, bf16[32,32,128]{2,1,0:T(8,128)(2,1)S(1)} %collective-permute-done.4.second_ref, bf16[8,34,12,16,128]{4,3,2,1,0:T(8,128)(2,1)S(1)} %copy-done.1, f32[8,32,16,128]{3,2,1,0:T(8,128)S(1)} %get-tuple-element.19.ready_ref.inverse_ref), custom_call_target="tpu_custom_call" | custom-call | flops 4000000000 | bytes 4000000 | tf_op jit(solution)/shard_map/pallas_call | solution.py:324
  68.9 0.0 collective-permute-done.1.first_ref
  68.9 0.0 collective-permute-done.2.second_ref
  68.9 4.8 %shard_map.58.refs_0_ = f32[16,4,128]{2,1,0:T(4,128)S(1)} custom-call(bf16[32,32,128]{2,1,0:T(8,128)(2,1)S(1)} %collective-permute-done.1.first_ref, bf16[32,32,128]{2,1,0:T(8,128)(2,1)S(1)} %collective-permute-done.2.second_ref, bf16[8,34,12,16,128]{4,3,2,1,0:T(8,128)(2,1)S(1)} %copy-done.1, f32[8,32,16,128]{3,2,1,0:T(8,128)S(1)} %get-tuple-element.19.ready_ref.inverse_ref), custom_call_target="tpu_custom_call" | custom-call | flops 4000000000 | bytes 4000000 | tf_op jit(solution)/shard_map/pallas_call | solution.py:324
  73.7 0.7 shard_map.62
  74.4 8.1 %all-to-all-start.1 = ((f32[64,4,128]{2,1,0:T(4,128)}), f32[64,4,128]{2,1,0:T(4,128)S(1)}, u32[]{:S(2)}, u32[]{:S(2)}) async-start(f32[64,4,128]{2,1,0:T(4,128)} %shard_map.62), calls=%async_computation.1 | async-start | bytes 262144 | tf_op jit(solution)/shard_map/all_to_all | solution.py:413
  82.5 12.5 %all-to-all-done.1.scores_ref = f32[64,4,128]{2,1,0:T(4,128)S(1)} async-done(((f32[64,4,128]{2,1,0:T(4,128)}), f32[64,4,128]{2,1,0:T(4,128)S(1)}, u32[]{:S(2)}, u32[]{:S(2)}) %all-to-all-start.1) | async-done | bytes 131104 | tf_op jit(solution)/shard_map/all_to_all | solution.py:413
  95.0 2.1 %shard_map.63 = f32[8,16,128]{2,1,0:T(8,128)} custom-call(s32[128]{0:T(128)S(1)} %copy-done.2, s32[8]{0:T(128)S(1)} %broadcast_subtract_fusion.limit_ref, f32[64,4,128]{2,1,0:T(4,128)S(1)} %all-to-all-done.1.scores_ref), custom_call_target="tpu_custom_call" | custom-call | tf_op jit(solution)/shard_map/pallas_call | solution.py:376
  (8 shorter events, 0.0 us)
Async XLA Ops:
  4.1 27.4 %all-to-all-start = ((bf16[8,288,128]{2,1,0:T(8,128)(2,1)}), bf16[8,288,128]{2,1,0:T(8,128)(2,1)S(1)}, u32[]{:S(2)}, u32[]{:S(2)}) async-start(bf16[8,288,128]{2,1,0:T(8,128)(2,1)} %bitcast.4), calls=%async_computation | async-start | bytes 1179648 | tf_op jit(solution)/shard_map/all_to_all | solution.py:392
  14.2 4.1 %collective-permute-start = (bf16[8,12,384]{2,1,0:T(8,128)(2,1)S(1)}, bf16[8,12,384]{2,1,0:T(8,128)(2,1)S(1)}, u32[]{:S(2)}, u32[]{:S(2)}) collective-permute-start(bf16[8,12,384]{2,1,0:T(8,128)(2,1)S(1)} %slice.4), channel_id=1, source_target_pairs={{1,0},{2,1},{3,2},{5,4},{6,5},{7,6},{9,8},{10,9},{11,10},{13,12},{... | collective-permute-start | bytes 221192 | tf_op jit(solution)/shard_map/ppermute | solution.py:401
  23.5 4.8 %copy-start = (bf16[8,34,12,16,128]{4,3,2,1,0:T(8,128)(2,1)}, bf16[8,34,12,16,128]{4,3,2,1,0:T(8,128)(2,1)S(1)}, u32[]{:S(2)}) copy-start(bf16[8,34,12,16,128]{4,3,2,1,0:T(8,128)(2,1)S(1)} %get-tuple-element.22.shifted_ref) | copy-start | bytes 40108036
  31.5 17.1 %copy-start.1 = (bf16[8,34,12,16,128]{4,3,2,1,0:T(8,128)(2,1)S(1)}, bf16[8,34,12,16,128]{4,3,2,1,0:T(8,128)(2,1)}, u32[]{:S(2)}) copy-start(bf16[8,34,12,16,128]{4,3,2,1,0:T(8,128)(2,1)} %copy-done) | copy-start | bytes 40108036
  32.9 14.1 %collective-permute-start.7 = (bf16[32,32,128]{2,1,0:T(8,128)(2,1)S(1)}, bf16[32,32,128]{2,1,0:T(8,128)(2,1)S(1)}, u32[]{:S(2)}, u32[]{:S(2)}) collective-permute-start(bf16[32,32,128]{2,1,0:T(8,128)(2,1)S(1)} %get-tuple-element.28), channel_id=1, source_target_pairs={{0,20},{4,16},{8,28},{12,24},{16,4},{20,0},{24,12},{28,8},{32,52},... | collective-permute-start | bytes 786440 | tf_op jit(solution)/shard_map/ppermute | solution.py:410
  37.7 17.2 %collective-permute-start.5 = (bf16[32,32,128]{2,1,0:T(8,128)(2,1)S(1)}, bf16[32,32,128]{2,1,0:T(8,128)(2,1)S(1)}, u32[]{:S(2)}, u32[]{:S(2)}) collective-permute-start(bf16[32,32,128]{2,1,0:T(8,128)(2,1)S(1)} %get-tuple-element.25), channel_id=1, source_target_pairs={{0,12},{4,8},{8,20},{12,16},{16,28},{20,24},{24,4},{28,0},{32,44},... | collective-permute-start | bytes 786440 | tf_op jit(solution)/shard_map/ppermute | solution.py:410
  39.0 20.2 %collective-permute-start.6 = (bf16[32,32,128]{2,1,0:T(8,128)(2,1)S(1)}, bf16[32,32,128]{2,1,0:T(8,128)(2,1)S(1)}, u32[]{:S(2)}, u32[]{:S(2)}) collective-permute-start(bf16[32,32,128]{2,1,0:T(8,128)(2,1)S(1)} %get-tuple-element.26), channel_id=1, source_target_pairs={{0,28},{4,24},{8,4},{12,0},{16,12},{20,8},{24,20},{28,16},{32,60},... | collective-permute-start | bytes 786440 | tf_op jit(solution)/shard_map/ppermute | solution.py:410
  43.4 20.7 %collective-permute-start.3 = (bf16[32,32,128]{2,1,0:T(8,128)(2,1)S(1)}, bf16[32,32,128]{2,1,0:T(8,128)(2,1)S(1)}, u32[]{:S(2)}, u32[]{:S(2)}) collective-permute-start(bf16[32,32,128]{2,1,0:T(8,128)(2,1)S(1)} %get-tuple-element.23), channel_id=1, source_target_pairs={{0,4},{4,0},{8,12},{12,8},{16,20},{20,16},{24,28},{28,24},{32,36},... | collective-permute-start | bytes 786440 | tf_op jit(solution)/shard_map/ppermute | solution.py:410
  44.6 19.4 %collective-permute-start.4 = (bf16[32,32,128]{2,1,0:T(8,128)(2,1)S(1)}, bf16[32,32,128]{2,1,0:T(8,128)(2,1)S(1)}, u32[]{:S(2)}, u32[]{:S(2)}) collective-permute-start(bf16[32,32,128]{2,1,0:T(8,128)(2,1)S(1)} %get-tuple-element.24), channel_id=1, source_target_pairs={{0,16},{4,20},{8,24},{12,28},{16,0},{20,4},{24,8},{28,12},{32,48},... | collective-permute-start | bytes 786440 | tf_op jit(solution)/shard_map/ppermute | solution.py:410
  47.0 21.9 %collective-permute-start.1 = (bf16[32,32,128]{2,1,0:T(8,128)(2,1)S(1)}, bf16[32,32,128]{2,1,0:T(8,128)(2,1)S(1)}, u32[]{:S(2)}, u32[]{:S(2)}) collective-permute-start(bf16[32,32,128]{2,1,0:T(8,128)(2,1)S(1)} %get-tuple-element.20), channel_id=1, source_target_pairs={{0,8},{4,12},{8,16},{12,20},{16,24},{20,28},{24,0},{28,4},{32,40},... | collective-permute-start | bytes 786440 | tf_op jit(solution)/shard_map/ppermute | solution.py:410
  54.9 13.9 %collective-permute-start.2 = (bf16[32,32,128]{2,1,0:T(8,128)(2,1)S(1)}, bf16[32,32,128]{2,1,0:T(8,128)(2,1)S(1)}, u32[]{:S(2)}, u32[]{:S(2)}) collective-permute-start(bf16[32,32,128]{2,1,0:T(8,128)(2,1)S(1)} %get-tuple-element.21), channel_id=1, source_target_pairs={{0,24},{4,28},{8,0},{12,4},{16,8},{20,12},{24,16},{28,20},{32,56},... | collective-permute-start | bytes 786440 | tf_op jit(solution)/shard_map/ppermute | solution.py:410
  64.0 18.5 %copy-start.3 = (s32[8]{0:T(128)S(1)}, s32[8]{0:T(128)}, u32[]{:S(2)}) copy-start(s32[8]{0:T(128)} %param.9) | copy-start | bytes 100
  64.0 31.0 %copy-start.2 = (s32[128]{0:T(128)S(1)}, s32[128]{0:T(128)}, u32[]{:S(2)}) copy-start(s32[128]{0:T(128)} %get-tuple-element.17.place_ref) | copy-start | bytes 1540
  74.4 20.6 %all-to-all-start.1 = ((f32[64,4,128]{2,1,0:T(4,128)}), f32[64,4,128]{2,1,0:T(4,128)S(1)}, u32[]{:S(2)}, u32[]{:S(2)}) async-start(f32[64,4,128]{2,1,0:T(4,128)} %shard_map.62), calls=%async_computation.1 | async-start | bytes 262144 | tf_op jit(solution)/shard_map/all_to_all | solution.py:413

commit v4 on v3

--- a/solution.py
+++ b/solution.py
@@ -14,7 +14,7 @@
 PLANE = 8
 X, Y = 4, 2
 PLANE_STEPS = ((0, 0), (1, 0), (3, 0), (0, 1), (2, 0), (1, 1), (3, 1), (2, 1))
-CALLS = ((1, 2), (3, 4), (5, 6), (0, 7))
+CALLS = ((6, 7), (4, 5), (2, 3), (0, 1))
 SHIFTS = 16
 GROUP = 16
 VMEM_LIMIT = 24 * 1024 * 1024
@@ -85,20 +85,20 @@
     lax.fori_loop(0, used.shape[0], clear, 0, unroll=8)
     lane = lanes_of((1, 128))
 
-    def place(r, carry):
-        k = r // rows_part
-        station = station_ref[k, r % rows_part]
-        block = block_ref[k, r % rows_part] & 31
-        holder = station // 8
+    def place(k, r):
+        station = station_ref[k, r]
+        block = block_ref[k, r] & 31
+        holder = station >> 3
         rank = jnp.minimum(used[holder], CAP - 1)
         used[holder] = rank + 1
         slot = holder * CAP + rank
-        place_ref[r] = slot
+        place_ref[k * rows_part + r] = slot
         entry = jnp.where(lane == 0, k, jnp.where(lane == 48, station & 7, jnp.where(lane == 49, block, 0)))
         table[pl.ds(slot, 1), :] = to_f32(entry)
-        return carry
-
-    lax.fori_loop(0, templates * rows_part, place, 0, unroll=8)
+
+    for k in range(templates):
+        for r in range(rows_part):
+            place(k, r)
     for z in range(sent_ref.shape[0]):
         sent_ref[z, templates] = to_bf16(table[UNIT * z : UNIT * z + UNIT, :])
 
@@ -273,7 +273,7 @@
         spread = lax.dot_general(marks, expand, TN, preferred_element_type=jnp.float32)
         factors = spread[0:12] + spread[16:28] + spread[32:44]
         totals = [jnp.zeros((8, 128), jnp.float32) for _ in range(2)]
-        places = [(codes[0, base + g] // 32, codes[0, base + g] % 32) for g in range(GROUP)]
+        places = [(codes[0, base + g] >> 5, codes[0, base + g] & 31) for g in range(GROUP)]
         for c in range(CH):
             pairs = []
             for pair in range(GROUP // 2):
@@ -366,7 +366,7 @@
     for k in range(templates):
         for r in range(rows_part):
             slot = place_ref[k * rows_part + r]
-            found = scores_ref[slot // CAP, pl.ds(slot % CAP, 1), :]
+            found = scores_ref[slot >> 2, pl.ds(slot & 3, 1), :]
             out_ref[k, r : r + 1, :] = jnp.where(r < limit_ref[k], found, 0.0)
 
 

time: 98.2 us -> 93.3 us (0.950)
  waiting for transfers between devices: 21.8 us -> 18.8 us
  Pallas kernels: 32.6 us -> 30.2 us
  starting transfers between devices: 36.1 us -> 37.4 us
    ppermute x7, waiting for transfers between devices: 3.9 us -> 1.01 us  [local(): units = lax.ppermute(units, 'wide', pairs)]
    pallas_call x1, Pallas kernels: 4.1 us -> 2.91 us  [pack(): pl.pallas_call(pack_kernel, out_shape=(jax.ShapeDtypeStruct((holders // P...]
    all_to_all x1, starting transfers between devices: 8.07 us -> 9.15 us  [local(): lax.all_to_all(arrange(scores), 'wide', split_axis=0, concat_axis=0, tile...]
where the time goes in v4:
time: 93.3 us; the launch traced here: 93 us
  starting transfers between devices  37.4 us (40%)
  Pallas kernels  30.2 us (32%)
  waiting for transfers between devices  18.8 us (20%)
  local copies, waits for them, and re-layouts  6.4 us (7%)
    pallas_call x4, Pallas kernels, slot_scores(): pl.pallas_call(score_kernel, out_shape=jax.ShapeDtypeStruct((slots // CAP...  18.5 us
    ppermute x7, starting transfers between devices, local(): units = lax.ppermute(units, 'wide', pairs)  17.8 us
    all_to_all x1, waiting for transfers between devices, local(): lax.all_to_all(arrange(scores), 'wide', split_axis=0, concat_axis=0, tile...  12.4 us
    all_to_all x1, starting transfers between devices, local(): lax.all_to_all(arrange(scores), 'wide', split_axis=0, concat_axis=0, tile...  9.15 us
    all_to_all x1, starting transfers between devices, local(): lax.all_to_all(sent.reshape(planes, (own_count + 1) * UNIT, 128), 'wide',...  8.48 us
    unnamed x9, local copies, waits for them, and re-layouts  6.39 us
    pallas_call x1, Pallas kernels, station_tables(): pl.pallas_call(station_kernel, grid=(stations,), out_shape=(jax.ShapeDtyp...  5.2 us
    all_to_all x1, waiting for transfers between devices, local(): lax.all_to_all(sent.reshape(planes, (own_count + 1) * UNIT, 128), 'wide',...  3.16 us
  transfers between devices with their start and end apart: 10, of which 5 were waited for; matrix products, arithmetic and copies ran while one was open for 2% of the time, Pallas kernels for 20%

profile of v4, /device:TPU:8, one launch (start us, length us, event | category | flops | bytes accessed | tf_op | source)
XLA Modules:
  0.0 93.0 jit_solution(13143867339704919933)
XLA Ops:
  0.0 2.9 %shard_map.55 = (bf16[8,9,32,128]{3,2,1,0:T(8,128)(2,1)}, s32[128]{0:T(128)}) custom-call(s32[8,16]{1,0:T(8,128)} %station_ref.1, s32[8,16]{1,0:T(8,128)} %block_ref.1, bf16[12,8,300]{2,1,0:T(8,128)(2,1)} %bitcast.5), custom_call_target="tpu_custom_call" | custom-call | tf_op jit(solution)/shard_map/pallas_call | solution.py:110
  2.9 8.5 %all-to-all-start = ((bf16[8,288,128]{2,1,0:T(8,128)(2,1)}), bf16[8,288,128]{2,1,0:T(8,128)(2,1)S(1)}, u32[]{:S(2)}, u32[]{:S(2)}) async-start(bf16[8,288,128]{2,1,0:T(8,128)(2,1)} %bitcast.4), calls=%async_computation | async-start | bytes 1179648 | tf_op jit(solution)/shard_map/all_to_all | solution.py:392
  11.4 1.6 %copy.7.wave_ref = bf16[8,12,4096]{2,1,0:T(8,128)(2,1)S(1)} copy(bf16[8,12,4096]{2,0,1:T(8,128)(2,1)} %param.5) | data formatting | bytes 1572864 | tf_op args[0]
  13.0 1.9 %collective-permute-start = (bf16[8,12,384]{2,1,0:T(8,128)(2,1)S(1)}, bf16[8,12,384]{2,1,0:T(8,128)(2,1)S(1)}, u32[]{:S(2)}, u32[]{:S(2)}) collective-permute-start(bf16[8,12,384]{2,1,0:T(8,128)(2,1)S(1)} %slice.4), channel_id=1, source_target_pairs={{1,0},{2,1},{3,2},{5,4},{6,5},{7,6},{9,8},{10,9},{11,10},{13,12},{... | collective-permute-start | bytes 221192 | tf_op jit(solution)/shard_map/ppermute | solution.py:401
  14.9 2.2 %collective-permute-done.tail_ref = bf16[8,12,384]{2,1,0:T(8,128)(2,1)S(1)} collective-permute-done((bf16[8,12,384]{2,1,0:T(8,128)(2,1)S(1)}, bf16[8,12,384]{2,1,0:T(8,128)(2,1)S(1)}, u32[]{:S(2)}, u32[]{:S(2)}) %collective-permute-start) | collective-permute-done | bytes 73760 | tf_op jit(solution)/shard_map/ppermute | solution.py:401
  17.1 5.2 %shard_map.56 = (bf16[8,34,12,16,128]{4,3,2,1,0:T(8,128)(2,1)S(1)}, f32[8,32,16,128]{3,2,1,0:T(8,128)S(1)}) custom-call(bf16[8,12,4096]{2,1,0:T(8,128)(2,1)S(1)} %copy.7.wave_ref, bf16[8,12,384]{2,1,0:T(8,128)(2,1)S(1)} %collective-permute-done.tail_ref), custom_call_target="tpu_custom_call" | custom-call | flops 3000000000 | bytes 20000000 | tf_op jit(solution)/shard_map/pallas_call | solution.py:213
  22.3 4.8 %copy-done = bf16[8,34,12,16,128]{4,3,2,1,0:T(8,128)(2,1)} copy-done((bf16[8,34,12,16,128]{4,3,2,1,0:T(8,128)(2,1)}, bf16[8,34,12,16,128]{4,3,2,1,0:T(8,128)(2,1)S(1)}, u32[]{:S(2)}) %copy-start) | copy-done | bytes 13369368
  27.1 3.2 %all-to-all-done = bf16[8,288,128]{2,1,0:T(8,128)(2,1)S(1)} async-done(((bf16[8,288,128]{2,1,0:T(8,128)(2,1)}), bf16[8,288,128]{2,1,0:T(8,128)(2,1)S(1)}, u32[]{:S(2)}, u32[]{:S(2)}) %all-to-all-start) | async-done | bytes 589856 | tf_op jit(solution)/shard_map/all_to_all | solution.py:392
  30.3 1.4 %shard_map.57 = (bf16[32,32,128]{2,1,0:T(8,128)(2,1)S(1)}, bf16[32,32,128]{2,1,0:T(8,128)(2,1)S(1)}, bf16[32,32,128]{2,1,0:T(8,128)(2,1)S(1)}, bf16[32,32,128]{2...) custom-call(bf16[8,9,32,128]{3,2,1,0:T(8,128)(2,1)S(1)} %bitcast.3, ...), custom_call_target="tpu_custom_call" | custom-call | flops 10000000000 | bytes 40000000 | tf_op jit(solution)/shard_map/pallas_call | solution.py:157
  31.7 1.6 %collective-permute-start.7 = (bf16[32,32,128]{2,1,0:T(8,128)(2,1)S(1)}, bf16[32,32,128]{2,1,0:T(8,128)(2,1)S(1)}, u32[]{:S(2)}, u32[]{:S(2)}) collective-permute-start(bf16[32,32,128]{2,1,0:T(8,128)(2,1)S(1)} %get-tuple-element.28), channel_id=1, source_target_pairs={{0,8},{4,12},{8,16},{12,20},{16,24},{20,28},{24,0},{28,4},{32,40},... | collective-permute-start | bytes 786440 | tf_op jit(solution)/shard_map/ppermute | solution.py:410
  33.3 1.7 %collective-permute-start.5 = (bf16[32,32,128]{2,1,0:T(8,128)(2,1)S(1)}, bf16[32,32,128]{2,1,0:T(8,128)(2,1)S(1)}, u32[]{:S(2)}, u32[]{:S(2)}) collective-permute-start(bf16[32,32,128]{2,1,0:T(8,128)(2,1)S(1)} %get-tuple-element.25), channel_id=1, source_target_pairs={{0,24},{4,28},{8,0},{12,4},{16,8},{20,12},{24,16},{28,20},{32,56},... | collective-permute-start | bytes 786440 | tf_op jit(solution)/shard_map/ppermute | solution.py:410
  35.0 2.3 %collective-permute-start.6 = (bf16[32,32,128]{2,1,0:T(8,128)(2,1)S(1)}, bf16[32,32,128]{2,1,0:T(8,128)(2,1)S(1)}, u32[]{:S(2)}, u32[]{:S(2)}) collective-permute-start(bf16[32,32,128]{2,1,0:T(8,128)(2,1)S(1)} %get-tuple-element.26), channel_id=1, source_target_pairs={{0,4},{4,0},{8,12},{12,8},{16,20},{20,16},{24,28},{28,24},{32,36},... | collective-permute-start | bytes 786440 | tf_op jit(solution)/shard_map/ppermute | solution.py:410
  37.3 1.8 %collective-permute-start.3 = (bf16[32,32,128]{2,1,0:T(8,128)(2,1)S(1)}, bf16[32,32,128]{2,1,0:T(8,128)(2,1)S(1)}, u32[]{:S(2)}, u32[]{:S(2)}) collective-permute-start(bf16[32,32,128]{2,1,0:T(8,128)(2,1)S(1)} %get-tuple-element.23), channel_id=1, source_target_pairs={{0,16},{4,20},{8,24},{12,28},{16,0},{20,4},{24,8},{28,12},{32,48},... | collective-permute-start | bytes 786440 | tf_op jit(solution)/shard_map/ppermute | solution.py:410
  39.1 1.3 %collective-permute-start.4 = (bf16[32,32,128]{2,1,0:T(8,128)(2,1)S(1)}, bf16[32,32,128]{2,1,0:T(8,128)(2,1)S(1)}, u32[]{:S(2)}, u32[]{:S(2)}) collective-permute-start(bf16[32,32,128]{2,1,0:T(8,128)(2,1)S(1)} %get-tuple-element.24), channel_id=1, source_target_pairs={{0,12},{4,8},{8,20},{12,16},{16,28},{20,24},{24,4},{28,0},{32,44},... | collective-permute-start | bytes 786440 | tf_op jit(solution)/shard_map/ppermute | solution.py:410
  40.4 0.8 collective-permute-done.7.second_ref
  41.2 4.2 %collective-permute-start.1 = (bf16[32,32,128]{2,1,0:T(8,128)(2,1)S(1)}, bf16[32,32,128]{2,1,0:T(8,128)(2,1)S(1)}, u32[]{:S(2)}, u32[]{:S(2)}) collective-permute-start(bf16[32,32,128]{2,1,0:T(8,128)(2,1)S(1)} %get-tuple-element.20), channel_id=1, source_target_pairs={{0,28},{4,24},{8,4},{12,0},{16,12},{20,8},{24,20},{28,16},{32,60},... | collective-permute-start | bytes 786440 | tf_op jit(solution)/shard_map/ppermute | solution.py:410
  45.4 4.6 %shard_map.61.refs_3_ = f32[16,4,128]{2,1,0:T(4,128)S(1)} custom-call(bf16[32,32,128]{2,1,0:T(8,128)(2,1)S(1)} %get-tuple-element.27.first_ref, bf16[32,32,128]{2,1,0:T(8,128)(2,1)S(1)} %collective-permute-done.7.second_ref, bf16[8,34,12,16,128]{4,3,2,1,0:T(8,128)(2,1)S(1)} %copy-done.1, f32[8,32,16,128]{3,2,1,0:T(8,128)S(1)} %get-tuple-element.19.ready_ref.inverse_ref), custom_call_target="tpu_custom_call" | custom-call | flops 4000000000 | bytes 4000000 | tf_op jit(solution)/shard_map/pallas_call | solution.py:324
  50.1 0.0 collective-permute-done.5.first_ref
  50.1 4.9 %collective-permute-start.2 = (bf16[32,32,128]{2,1,0:T(8,128)(2,1)S(1)}, bf16[32,32,128]{2,1,0:T(8,128)(2,1)S(1)}, u32[]{:S(2)}, u32[]{:S(2)}) collective-permute-start(bf16[32,32,128]{2,1,0:T(8,128)(2,1)S(1)} %get-tuple-element.21), channel_id=1, source_target_pairs={{0,20},{4,16},{8,28},{12,24},{16,4},{20,0},{24,12},{28,8},{32,52},... | collective-permute-start | bytes 786440 | tf_op jit(solution)/shard_map/ppermute | solution.py:410
  55.0 0.0 collective-permute-done.6.second_ref
  55.0 4.6 %shard_map.60.refs_2_ = f32[16,4,128]{2,1,0:T(4,128)S(1)} custom-call(bf16[32,32,128]{2,1,0:T(8,128)(2,1)S(1)} %collective-permute-done.5.first_ref, bf16[32,32,128]{2,1,0:T(8,128)(2,1)S(1)} %collective-permute-done.6.second_ref, bf16[8,34,12,16,128]{4,3,2,1,0:T(8,128)(2,1)S(1)} %copy-done.1, f32[8,32,16,128]{3,2,1,0:T(8,128)S(1)} %get-tuple-element.19.ready_ref.inverse_ref), custom_call_target="tpu_custom_call" | custom-call | flops 4000000000 | bytes 4000000 | tf_op jit(solution)/shard_map/pallas_call | solution.py:324
  59.7 0.0 copy-start.3
  59.7 0.0 copy-start.2
  59.7 0.0 collective-permute-done.3.first_ref
  59.7 4.6 %shard_map.59.refs_1_ = f32[16,4,128]{2,1,0:T(4,128)S(1)} custom-call(bf16[32,32,128]{2,1,0:T(8,128)(2,1)S(1)} %collective-permute-done.3.first_ref, bf16[32,32,128]{2,1,0:T(8,128)(2,1)S(1)} %collective-permute-done.4.second_ref, bf16[8,34,12,16,128]{4,3,2,1,0:T(8,128)(2,1)S(1)} %copy-done.1, f32[8,32,16,128]{3,2,1,0:T(8,128)S(1)} %get-tuple-element.19.ready_ref.inverse_ref), custom_call_target="tpu_custom_call" | custom-call | flops 4000000000 | bytes 4000000 | tf_op jit(solution)/shard_map/pallas_call | solution.py:324
  64.3 0.0 collective-permute-done.1.first_ref
  64.3 0.2 collective-permute-done.2.second_ref
  64.5 4.6 %shard_map.58.refs_0_ = f32[16,4,128]{2,1,0:T(4,128)S(1)} custom-call(bf16[32,32,128]{2,1,0:T(8,128)(2,1)S(1)} %collective-permute-done.1.first_ref, bf16[32,32,128]{2,1,0:T(8,128)(2,1)S(1)} %collective-permute-done.2.second_ref, bf16[8,34,12,16,128]{4,3,2,1,0:T(8,128)(2,1)S(1)} %copy-done.1, f32[8,32,16,128]{3,2,1,0:T(8,128)S(1)} %get-tuple-element.19.ready_ref.inverse_ref), custom_call_target="tpu_custom_call" | custom-call | flops 4000000000 | bytes 4000000 | tf_op jit(solution)/shard_map/pallas_call | solution.py:324
  69.1 0.7 shard_map.62
  69.8 9.2 %all-to-all-start.1 = ((f32[64,4,128]{2,1,0:T(4,128)}), f32[64,4,128]{2,1,0:T(4,128)S(1)}, u32[]{:S(2)}, u32[]{:S(2)}) async-start(f32[64,4,128]{2,1,0:T(4,128)} %shard_map.62), calls=%async_computation.1 | async-start | bytes 262144 | tf_op jit(solution)/shard_map/all_to_all | solution.py:413
  79.0 12.4 %all-to-all-done.1.scores_ref = f32[64,4,128]{2,1,0:T(4,128)S(1)} async-done(((f32[64,4,128]{2,1,0:T(4,128)}), f32[64,4,128]{2,1,0:T(4,128)S(1)}, u32[]{:S(2)}, u32[]{:S(2)}) %all-to-all-start.1) | async-done | bytes 131104 | tf_op jit(solution)/shard_map/all_to_all | solution.py:413
  91.5 1.5 %shard_map.63 = f32[8,16,128]{2,1,0:T(8,128)} custom-call(s32[128]{0:T(128)S(1)} %copy-done.2, s32[8]{0:T(128)S(1)} %broadcast_subtract_fusion.limit_ref, f32[64,4,128]{2,1,0:T(4,128)S(1)} %all-to-all-done.1.scores_ref), custom_call_target="tpu_custom_call" | custom-call | tf_op jit(solution)/shard_map/pallas_call | solution.py:376
  (8 shorter events, 0.0 us)
Async XLA Ops:
  2.9 27.4 %all-to-all-start = ((bf16[8,288,128]{2,1,0:T(8,128)(2,1)}), bf16[8,288,128]{2,1,0:T(8,128)(2,1)S(1)}, u32[]{:S(2)}, u32[]{:S(2)}) async-start(bf16[8,288,128]{2,1,0:T(8,128)(2,1)} %bitcast.4), calls=%async_computation | async-start | bytes 1179648 | tf_op jit(solution)/shard_map/all_to_all | solution.py:392
  13.0 4.1 %collective-permute-start = (bf16[8,12,384]{2,1,0:T(8,128)(2,1)S(1)}, bf16[8,12,384]{2,1,0:T(8,128)(2,1)S(1)}, u32[]{:S(2)}, u32[]{:S(2)}) collective-permute-start(bf16[8,12,384]{2,1,0:T(8,128)(2,1)S(1)} %slice.4), channel_id=1, source_target_pairs={{1,0},{2,1},{3,2},{5,4},{6,5},{7,6},{9,8},{10,9},{11,10},{13,12},{... | collective-permute-start | bytes 221192 | tf_op jit(solution)/shard_map/ppermute | solution.py:401
  22.3 4.8 %copy-start = (bf16[8,34,12,16,128]{4,3,2,1,0:T(8,128)(2,1)}, bf16[8,34,12,16,128]{4,3,2,1,0:T(8,128)(2,1)S(1)}, u32[]{:S(2)}) copy-start(bf16[8,34,12,16,128]{4,3,2,1,0:T(8,128)(2,1)S(1)} %get-tuple-element.22.shifted_ref) | copy-start | bytes 40108036
  30.3 15.2 %copy-start.1 = (bf16[8,34,12,16,128]{4,3,2,1,0:T(8,128)(2,1)S(1)}, bf16[8,34,12,16,128]{4,3,2,1,0:T(8,128)(2,1)}, u32[]{:S(2)}) copy-start(bf16[8,34,12,16,128]{4,3,2,1,0:T(8,128)(2,1)} %copy-done) | copy-start | bytes 40108036
  31.7 9.5 %collective-permute-start.7 = (bf16[32,32,128]{2,1,0:T(8,128)(2,1)S(1)}, bf16[32,32,128]{2,1,0:T(8,128)(2,1)S(1)}, u32[]{:S(2)}, u32[]{:S(2)}) collective-permute-start(bf16[32,32,128]{2,1,0:T(8,128)(2,1)S(1)} %get-tuple-element.28), channel_id=1, source_target_pairs={{0,8},{4,12},{8,16},{12,20},{16,24},{20,28},{24,0},{28,4},{32,40},... | collective-permute-start | bytes 786440 | tf_op jit(solution)/shard_map/ppermute | solution.py:410
  33.3 16.8 %collective-permute-start.5 = (bf16[32,32,128]{2,1,0:T(8,128)(2,1)S(1)}, bf16[32,32,128]{2,1,0:T(8,128)(2,1)S(1)}, u32[]{:S(2)}, u32[]{:S(2)}) collective-permute-start(bf16[32,32,128]{2,1,0:T(8,128)(2,1)S(1)} %get-tuple-element.25), channel_id=1, source_target_pairs={{0,24},{4,28},{8,0},{12,4},{16,8},{20,12},{24,16},{28,20},{32,56},... | collective-permute-start | bytes 786440 | tf_op jit(solution)/shard_map/ppermute | solution.py:410
  35.0 20.0 %collective-permute-start.6 = (bf16[32,32,128]{2,1,0:T(8,128)(2,1)S(1)}, bf16[32,32,128]{2,1,0:T(8,128)(2,1)S(1)}, u32[]{:S(2)}, u32[]{:S(2)}) collective-permute-start(bf16[32,32,128]{2,1,0:T(8,128)(2,1)S(1)} %get-tuple-element.26), channel_id=1, source_target_pairs={{0,4},{4,0},{8,12},{12,8},{16,20},{20,16},{24,28},{28,24},{32,36},... | collective-permute-start | bytes 786440 | tf_op jit(solution)/shard_map/ppermute | solution.py:410
  37.3 22.4 %collective-permute-start.3 = (bf16[32,32,128]{2,1,0:T(8,128)(2,1)S(1)}, bf16[32,32,128]{2,1,0:T(8,128)(2,1)S(1)}, u32[]{:S(2)}, u32[]{:S(2)}) collective-permute-start(bf16[32,32,128]{2,1,0:T(8,128)(2,1)S(1)} %get-tuple-element.23), channel_id=1, source_target_pairs={{0,16},{4,20},{8,24},{12,28},{16,0},{20,4},{24,8},{28,12},{32,48},... | collective-permute-start | bytes 786440 | tf_op jit(solution)/shard_map/ppermute | solution.py:410
  39.1 20.6 %collective-permute-start.4 = (bf16[32,32,128]{2,1,0:T(8,128)(2,1)S(1)}, bf16[32,32,128]{2,1,0:T(8,128)(2,1)S(1)}, u32[]{:S(2)}, u32[]{:S(2)}) collective-permute-start(bf16[32,32,128]{2,1,0:T(8,128)(2,1)S(1)} %get-tuple-element.24), channel_id=1, source_target_pairs={{0,12},{4,8},{8,20},{12,16},{16,28},{20,24},{24,4},{28,0},{32,44},... | collective-permute-start | bytes 786440 | tf_op jit(solution)/shard_map/ppermute | solution.py:410
  41.2 23.1 %collective-permute-start.1 = (bf16[32,32,128]{2,1,0:T(8,128)(2,1)S(1)}, bf16[32,32,128]{2,1,0:T(8,128)(2,1)S(1)}, u32[]{:S(2)}, u32[]{:S(2)}) collective-permute-start(bf16[32,32,128]{2,1,0:T(8,128)(2,1)S(1)} %get-tuple-element.20), channel_id=1, source_target_pairs={{0,28},{4,24},{8,4},{12,0},{16,12},{20,8},{24,20},{28,16},{32,60},... | collective-permute-start | bytes 786440 | tf_op jit(solution)/shard_map/ppermute | solution.py:410
  50.1 14.4 %collective-permute-start.2 = (bf16[32,32,128]{2,1,0:T(8,128)(2,1)S(1)}, bf16[32,32,128]{2,1,0:T(8,128)(2,1)S(1)}, u32[]{:S(2)}, u32[]{:S(2)}) collective-permute-start(bf16[32,32,128]{2,1,0:T(8,128)(2,1)S(1)} %get-tuple-element.21), channel_id=1, source_target_pairs={{0,20},{4,16},{8,28},{12,24},{16,4},{20,0},{24,12},{28,8},{32,52},... | collective-permute-start | bytes 786440 | tf_op jit(solution)/shard_map/ppermute | solution.py:410
  59.7 19.4 %copy-start.3 = (s32[8]{0:T(128)S(1)}, s32[8]{0:T(128)}, u32[]{:S(2)}) copy-start(s32[8]{0:T(128)} %param.9) | copy-start | bytes 100
  59.7 31.8 %copy-start.2 = (s32[128]{0:T(128)S(1)}, s32[128]{0:T(128)}, u32[]{:S(2)}) copy-start(s32[128]{0:T(128)} %get-tuple-element.17.place_ref) | copy-start | bytes 1540
  69.8 21.6 %all-to-all-start.1 = ((f32[64,4,128]{2,1,0:T(4,128)}), f32[64,4,128]{2,1,0:T(4,128)S(1)}, u32[]{:S(2)}, u32[]{:S(2)}) async-start(f32[64,4,128]{2,1,0:T(4,128)} %shard_map.62), calls=%async_computation.1 | async-start | bytes 262144 | tf_op jit(solution)/shard_map/all_to_all | solution.py:413

commit v5 on v4

--- a/solution.py
+++ b/solution.py
@@ -14,7 +14,8 @@
 PLANE = 8
 X, Y = 4, 2
 PLANE_STEPS = ((0, 0), (1, 0), (3, 0), (0, 1), (2, 0), (1, 1), (3, 1), (2, 1))
-CALLS = ((6, 7), (4, 5), (2, 3), (0, 1))
+CALLS = ((0, 1), (2, 3), (4, 5), (6, 7))
+HELD_BACK = ((6, 7), (), (), ())
 SHIFTS = 16
 GROUP = 16
 VMEM_LIMIT = 24 * 1024 * 1024
@@ -234,9 +235,9 @@
     )(wave, tail)
 
 
-def score_kernel(
-    first_ref, second_ref, shifted_ref, inverse_ref, scores_ref, rows, marked, staged, codes, sem
-):
+def score_kernel(first_ref, second_ref, shifted_ref, inverse_ref, *refs):
+    held_back = len(refs) // 2 - 3
+    scores_ref, (rows, marked, staged, codes, sem) = refs[held_back], refs[-5:]
     lane, row = lanes_of((8, 128)), rows_of((8, 128))
     before = lane < row
     member = lane // SHIFTS
@@ -318,14 +319,19 @@
     lax.fori_loop(0, 2 * count // GROUP, score, 0)
 
 
-def slot_scores(first, second, shifted, inverse):
+def slot_scores(first, second, shifted, inverse, held_back):
+    anywhere = [pl.BlockSpec(memory_space=pl.ANY)] * len(held_back)
     slots = 2 * first.shape[0]
     vmem = pl.BlockSpec(memory_space=pltpu.VMEM)
     return pl.pallas_call(
         score_kernel,
-        out_shape=jax.ShapeDtypeStruct((slots // CAP, CAP, BLK), jnp.float32),
-        in_specs=[vmem] * 4,
-        out_specs=vmem,
+        out_shape=[
+            jax.ShapeDtypeStruct((slots // CAP, CAP, BLK), jnp.float32),
+            *[jax.ShapeDtypeStruct(array.shape, array.dtype) for array in held_back],
+        ],
+        in_specs=[*[vmem] * 4, *anywhere],
+        out_specs=[vmem, *anywhere],
+        input_output_aliases={4 + i: 1 + i for i in range(len(held_back))},
         scratch_shapes=[
             pltpu.VMEM((slots, 40, 128), jnp.float32),
             pltpu.VMEM((slots, 128), jnp.bfloat16),
@@ -335,7 +341,7 @@
         ],
         compiler_params=pltpu.CompilerParams(vmem_limit_bytes=VMEM_LIMIT),
         cost_estimate=pl.CostEstimate(flops=4_000_000_000, bytes_accessed=4_000_000, transcendentals=0),
-    )(first, second, shifted, inverse)
+    )(first, second, shifted, inverse, *held_back)
 
 
 def arrange_kernel(*refs):
@@ -403,13 +409,21 @@
     )
     shifted, inverse = station_tables(waveforms, tail)
     routed = route(held, inverse)
-    arrived = []
-    for step, units in zip(PLANE_STEPS, routed):
-        if step != (0, 0):
-            pairs = [(PLANE * z + p, PLANE * z + member_after(p, step)) for z, p in members]
-            units = lax.ppermute(units, "wide", pairs)
-        arrived.append(units)
-    scores = [slot_scores(arrived[a], arrived[b], shifted, inverse) for a, b in CALLS]
+    routed = list(routed)
+    scores = []
+    for call, kept in zip(CALLS, HELD_BACK):
+        units = []
+        for number in call:
+            value = routed[number]
+            if number > 0:
+                step = PLANE_STEPS[number]
+                pairs = [(PLANE * z + p, PLANE * z + member_after(p, step)) for z, p in members]
+                value = lax.ppermute(value, "wide", pairs)
+            units.append(value)
+        found, *passed = slot_scores(*units, shifted, inverse, [routed[number] for number in kept])
+        for number, value in zip(kept, passed):
+            routed[number] = value
+        scores.append(found)
     returned = lax.all_to_all(arrange(scores), "wide", split_axis=0, concat_axis=0, tiled=True)
     limit = det_count - lax.axis_index("narrow") * rows_part
     return unpack(place, limit, returned, (own_count, rows_part, BLK))

time: 93.3 us -> 96.5 us (1.034); the launches traced: 93 us -> 95 us
  waiting for transfers between devices: 18.8 us -> 22.7 us
  starting transfers between devices: 37.4 us -> 35.6 us
    ppermute x7, waiting for transfers between devices: 1.01 us -> 4.95 us  [local(): value = lax.ppermute(value, 'wide', pairs)]
    all_to_all x1, starting transfers between devices: 9.15 us -> 5.41 us  [local(): lax.all_to_all(arrange(scores), 'wide', split_axis=0, concat_axis=0, tile...]
    ppermute x7, starting transfers between devices: 17.8 us -> 19.8 us  [local(): value = lax.ppermute(value, 'wide', pairs)]
where the time goes in v5:
time: 96.5 us; the launch traced here: 95 us
  starting transfers between devices  35.6 us (37%)
  Pallas kernels  30.2 us (31%)
  waiting for transfers between devices  22.7 us (24%)
  local copies, waits for them, and re-layouts  6.42 us (7%)
    ppermute x7, starting transfers between devices, local(): value = lax.ppermute(value, 'wide', pairs)  19.8 us
    pallas_call x4, Pallas kernels, slot_scores(): pl.pallas_call(score_kernel, out_shape=[jax.ShapeDtypeStruct((slots // CA...  18.5 us
    all_to_all x1, waiting for transfers between devices, local(): lax.all_to_all(arrange(scores), 'wide', split_axis=0, concat_axis=0, tile...  12.4 us
    all_to_all x1, starting transfers between devices, local(): lax.all_to_all(sent.reshape(planes, (own_count + 1) * UNIT, 128), 'wide',...  8.48 us
    unnamed x9, local copies, waits for them, and re-layouts  6.41 us
    all_to_all x1, starting transfers between devices, local(): lax.all_to_all(arrange(scores), 'wide', split_axis=0, concat_axis=0, tile...  5.41 us
    pallas_call x1, Pallas kernels, station_tables(): pl.pallas_call(station_kernel, grid=(stations,), out_shape=(jax.ShapeDtyp...  5.2 us
    ppermute x7, waiting for transfers between devices, local(): value = lax.ppermute(value, 'wide', pairs)  4.95 us
  transfers between devices with their start and end apart: 10, of which 5 were waited for; matrix products, arithmetic and copies ran while one was open for 2% of the time, Pallas kernels for 20%

profile of v5, /device:TPU:8, one launch (start us, length us, event | category | flops | bytes accessed | tf_op | source)
XLA Modules:
  0.0 95.0 jit_solution(10631217542150105687)
XLA Ops:
  0.0 2.9 %shard_map.55 = (bf16[8,9,32,128]{3,2,1,0:T(8,128)(2,1)}, s32[128]{0:T(128)}) custom-call(s32[8,16]{1,0:T(8,128)} %station_ref.1, s32[8,16]{1,0:T(8,128)} %block_ref.1, bf16[12,8,300]{2,1,0:T(8,128)(2,1)} %bitcast.5), custom_call_target="tpu_custom_call" | custom-call | tf_op jit(solution)/shard_map/pallas_call | solution.py:111
  2.9 8.5 %all-to-all-start = ((bf16[8,288,128]{2,1,0:T(8,128)(2,1)}), bf16[8,288,128]{2,1,0:T(8,128)(2,1)S(1)}, u32[]{:S(2)}, u32[]{:S(2)}) async-start(bf16[8,288,128]{2,1,0:T(8,128)(2,1)} %bitcast.4), calls=%async_computation | async-start | bytes 1179648 | tf_op jit(solution)/shard_map/all_to_all | solution.py:398
  11.4 1.6 %copy.9.wave_ref = bf16[8,12,4096]{2,1,0:T(8,128)(2,1)S(1)} copy(bf16[8,12,4096]{2,0,1:T(8,128)(2,1)} %param.5) | data formatting | bytes 1572864 | tf_op args[0]
  13.0 1.9 %collective-permute-start = (bf16[8,12,384]{2,1,0:T(8,128)(2,1)S(1)}, bf16[8,12,384]{2,1,0:T(8,128)(2,1)S(1)}, u32[]{:S(2)}, u32[]{:S(2)}) collective-permute-start(bf16[8,12,384]{2,1,0:T(8,128)(2,1)S(1)} %slice.4), channel_id=1, source_target_pairs={{1,0},{2,1},{3,2},{5,4},{6,5},{7,6},{9,8},{10,9},{11,10},{13,12},{... | collective-permute-start | bytes 221192 | tf_op jit(solution)/shard_map/ppermute | solution.py:407
  14.9 2.2 %collective-permute-done.tail_ref = bf16[8,12,384]{2,1,0:T(8,128)(2,1)S(1)} collective-permute-done((bf16[8,12,384]{2,1,0:T(8,128)(2,1)S(1)}, bf16[8,12,384]{2,1,0:T(8,128)(2,1)S(1)}, u32[]{:S(2)}, u32[]{:S(2)}) %collective-permute-start) | collective-permute-done | bytes 73760 | tf_op jit(solution)/shard_map/ppermute | solution.py:407
  17.1 5.2 %shard_map.56 = (bf16[8,34,12,16,128]{4,3,2,1,0:T(8,128)(2,1)S(1)}, f32[8,32,16,128]{3,2,1,0:T(8,128)S(1)}) custom-call(bf16[8,12,4096]{2,1,0:T(8,128)(2,1)S(1)} %copy.9.wave_ref, bf16[8,12,384]{2,1,0:T(8,128)(2,1)S(1)} %collective-permute-done.tail_ref), custom_call_target="tpu_custom_call" | custom-call | flops 3000000000 | bytes 20000000 | tf_op jit(solution)/shard_map/pallas_call | solution.py:214
  22.3 4.8 %copy-done = bf16[8,34,12,16,128]{4,3,2,1,0:T(8,128)(2,1)} copy-done((bf16[8,34,12,16,128]{4,3,2,1,0:T(8,128)(2,1)}, bf16[8,34,12,16,128]{4,3,2,1,0:T(8,128)(2,1)S(1)}, u32[]{:S(2)}) %copy-start) | copy-done | bytes 13369368
  27.1 3.1 %all-to-all-done = bf16[8,288,128]{2,1,0:T(8,128)(2,1)S(1)} async-done(((bf16[8,288,128]{2,1,0:T(8,128)(2,1)}), bf16[8,288,128]{2,1,0:T(8,128)(2,1)S(1)}, u32[]{:S(2)}, u32[]{:S(2)}) %all-to-all-start) | async-done | bytes 589856 | tf_op jit(solution)/shard_map/all_to_all | solution.py:398
  30.3 1.4 %shard_map.57 = (bf16[32,32,128]{2,1,0:T(8,128)(2,1)S(1)}, bf16[32,32,128]{2,1,0:T(8,128)(2,1)S(1)}, bf16[32,32,128]{2,1,0:T(8,128)(2,1)S(1)}, bf16[32,32,128]{2...) custom-call(bf16[8,9,32,128]{3,2,1,0:T(8,128)(2,1)S(1)} %bitcast.3, ...), custom_call_target="tpu_custom_call" | custom-call | flops 10000000000 | bytes 40000000 | tf_op jit(solution)/shard_map/pallas_call | solution.py:158
  31.7 1.6 %collective-permute-start.1 = (bf16[32,32,128]{2,1,0:T(8,128)(2,1)S(1)}, bf16[32,32,128]{2,1,0:T(8,128)(2,1)S(1)}, u32[]{:S(2)}, u32[]{:S(2)}) collective-permute-start(bf16[32,32,128]{2,1,0:T(8,128)(2,1)S(1)} %get-tuple-element.24), channel_id=1, source_target_pairs={{0,8},{4,12},{8,16},{12,20},{16,24},{20,28},{24,0},{28,4},{32,40},... | collective-permute-start | bytes 786440 | tf_op jit(solution)/shard_map/ppermute | solution.py:421
  33.3 2.7 %collective-permute-start.4 = (bf16[32,32,128]{2,1,0:T(8,128)(2,1)S(1)}, bf16[32,32,128]{2,1,0:T(8,128)(2,1)S(1)}, u32[]{:S(2)}, u32[]{:S(2)}) collective-permute-start(bf16[32,32,128]{2,1,0:T(8,128)(2,1)S(1)} %get-tuple-element.31), channel_id=1, source_target_pairs={{0,16},{4,20},{8,24},{12,28},{16,0},{20,4},{24,8},{28,12},{32,48},... | collective-permute-start | bytes 786440 | tf_op jit(solution)/shard_map/ppermute | solution.py:421
  36.0 1.6 %collective-permute-start.5 = (bf16[32,32,128]{2,1,0:T(8,128)(2,1)S(1)}, bf16[32,32,128]{2,1,0:T(8,128)(2,1)S(1)}, u32[]{:S(2)}, u32[]{:S(2)}) collective-permute-start(bf16[32,32,128]{2,1,0:T(8,128)(2,1)S(1)} %get-tuple-element.32), channel_id=1, source_target_pairs={{0,12},{4,8},{8,20},{12,16},{16,28},{20,24},{24,4},{28,0},{32,44},... | collective-permute-start | bytes 786440 | tf_op jit(solution)/shard_map/ppermute | solution.py:421
  37.6 3.4 %collective-permute-start.2 = (bf16[32,32,128]{2,1,0:T(8,128)(2,1)S(1)}, bf16[32,32,128]{2,1,0:T(8,128)(2,1)S(1)}, u32[]{:S(2)}, u32[]{:S(2)}) collective-permute-start(bf16[32,32,128]{2,1,0:T(8,128)(2,1)S(1)} %get-tuple-element.29), channel_id=1, source_target_pairs={{0,24},{4,28},{8,0},{12,4},{16,8},{20,12},{24,16},{28,20},{32,56},... | collective-permute-start | bytes 786440 | tf_op jit(solution)/shard_map/ppermute | solution.py:421
  41.0 1.2 %collective-permute-start.3 = (bf16[32,32,128]{2,1,0:T(8,128)(2,1)S(1)}, bf16[32,32,128]{2,1,0:T(8,128)(2,1)S(1)}, u32[]{:S(2)}, u32[]{:S(2)}) collective-permute-start(bf16[32,32,128]{2,1,0:T(8,128)(2,1)S(1)} %get-tuple-element.30), channel_id=1, source_target_pairs={{0,4},{4,0},{8,12},{12,8},{16,20},{20,16},{24,28},{28,24},{32,36},... | collective-permute-start | bytes 786440 | tf_op jit(solution)/shard_map/ppermute | solution.py:421
  42.2 0.0 collective-permute-done.1.second_ref
  42.2 4.6 %shard_map.58 = (f32[16,4,128]{2,1,0:T(4,128)S(1)}, bf16[32,32,128]{2,1,0:T(8,128)(2,1)S(1)}, bf16[32,32,128]{2,1,0:T(8,128)(2,1)S(1)}) custom-call(bf16[32,32,128]{2,1,0:T(8,128)(2,1)S(1)} %get-tuple-element.23.first_ref, bf16[32,32,128]{2,1,0:T(8,128)(2,1)S(1)} %collective-permute-done.1.second_ref, ...), custom_call_target="tpu_custom_call", output_to_operand_aliasing={{1}: (4, {}), {2}: (5, {})} | custom-call | flops 4000000000 | bytes 4000000 | tf_op jit(solution)/shard_map/pallas_call | solution.py:326
  46.8 3.3 %collective-permute-start.6 = (bf16[32,32,128]{2,1,0:T(8,128)(2,1)S(1)}, bf16[32,32,128]{2,1,0:T(8,128)(2,1)S(1)}, u32[]{:S(2)}, u32[]{:S(2)}) collective-permute-start(bf16[32,32,128]{2,1,0:T(8,128)(2,1)S(1)} %get-tuple-element.33), channel_id=1, source_target_pairs={{0,28},{4,24},{8,4},{12,0},{16,12},{20,8},{24,20},{28,16},{32,60},... | collective-permute-start | bytes 786440 | tf_op jit(solution)/shard_map/ppermute | solution.py:421
  50.1 0.0 collective-permute-done.4.first_ref
  50.1 6.0 %collective-permute-start.7 = (bf16[32,32,128]{2,1,0:T(8,128)(2,1)S(1)}, bf16[32,32,128]{2,1,0:T(8,128)(2,1)S(1)}, u32[]{:S(2)}, u32[]{:S(2)}) collective-permute-start(bf16[32,32,128]{2,1,0:T(8,128)(2,1)S(1)} %get-tuple-element.34), channel_id=1, source_target_pairs={{0,20},{4,16},{8,28},{12,24},{16,4},{20,0},{24,12},{28,8},{32,52},... | collective-permute-start | bytes 786440 | tf_op jit(solution)/shard_map/ppermute | solution.py:421
  56.1 0.8 collective-permute-done.5.second_ref
  56.9 4.6 %shard_map.60.refs_2_ = f32[16,4,128]{2,1,0:T(4,128)S(1)} custom-call(bf16[32,32,128]{2,1,0:T(8,128)(2,1)S(1)} %collective-permute-done.4.first_ref, bf16[32,32,128]{2,1,0:T(8,128)(2,1)S(1)} %collective-permute-done.5.second_ref, bf16[8,34,12,16,128]{4,3,2,1,0:T(8,128)(2,1)S(1)} %copy-done.1, f32[8,32,16,128]{3,2,1,0:T(8,128)S(1)} %get-tuple-element.22.ready_ref.inverse_ref), custom_call_target="tpu_custom_call" | custom-call | flops 4000000000 | bytes 4000000 | tf_op jit(solution)/shard_map/pallas_call | solution.py:326
  61.5 0.0 copy-start.3
  61.5 0.0 copy-start.2
  61.5 4.2 %collective-permute-done.3.second_ref = bf16[32,32,128]{2,1,0:T(8,128)(2,1)S(1)} collective-permute-done((bf16[32,32,128]{2,1,0:T(8,128)(2,1)S(1)}, bf16[32,32,128]{2,1,0:T(8,128)(2,1)S(1)}, u32[]{:S(2)}, u32[]{:S(2)}) %collective-permute-start.3) | collective-permute-done | bytes 262176 | tf_op jit(solution)/shard_map/ppermute | solution.py:421
  65.7 4.6 %shard_map.59.refs_1_ = f32[16,4,128]{2,1,0:T(4,128)S(1)} custom-call(bf16[32,32,128]{2,1,0:T(8,128)(2,1)S(1)} %collective-permute-done.2.first_ref, bf16[32,32,128]{2,1,0:T(8,128)(2,1)S(1)} %collective-permute-done.3.second_ref, bf16[8,34,12,16,128]{4,3,2,1,0:T(8,128)(2,1)S(1)} %copy-done.1, f32[8,32,16,128]{3,2,1,0:T(8,128)S(1)} %get-tuple-element.22.ready_ref.inverse_ref), custom_call_target="tpu_custom_call" | custom-call | flops 4000000000 | bytes 4000000 | tf_op jit(solution)/shard_map/pallas_call | solution.py:326
  70.3 0.0 collective-permute-done.6.first_ref
  70.3 0.0 collective-permute-done.7.second_ref
  70.3 4.6 %shard_map.61.refs_3_ = f32[16,4,128]{2,1,0:T(4,128)S(1)} custom-call(bf16[32,32,128]{2,1,0:T(8,128)(2,1)S(1)} %collective-permute-done.6.first_ref, bf16[32,32,128]{2,1,0:T(8,128)(2,1)S(1)} %collective-permute-done.7.second_ref, bf16[8,34,12,16,128]{4,3,2,1,0:T(8,128)(2,1)S(1)} %copy-done.1, f32[8,32,16,128]{3,2,1,0:T(8,128)S(1)} %get-tuple-element.22.ready_ref.inverse_ref), custom_call_target="tpu_custom_call" | custom-call | flops 4000000000 | bytes 4000000 | tf_op jit(solution)/shard_map/pallas_call | solution.py:326
  75.0 0.7 shard_map.62
  75.7 5.4 %all-to-all-start.1 = ((f32[64,4,128]{2,1,0:T(4,128)}), f32[64,4,128]{2,1,0:T(4,128)S(1)}, u32[]{:S(2)}, u32[]{:S(2)}) async-start(f32[64,4,128]{2,1,0:T(4,128)} %shard_map.62), calls=%async_computation.1 | async-start | bytes 262144 | tf_op jit(solution)/shard_map/all_to_all | solution.py:427
  81.1 12.4 %all-to-all-done.1.scores_ref = f32[64,4,128]{2,1,0:T(4,128)S(1)} async-done(((f32[64,4,128]{2,1,0:T(4,128)}), f32[64,4,128]{2,1,0:T(4,128)S(1)}, u32[]{:S(2)}, u32[]{:S(2)}) %all-to-all-start.1) | async-done | bytes 131104 | tf_op jit(solution)/shard_map/all_to_all | solution.py:427
  93.6 1.5 %shard_map.63 = f32[8,16,128]{2,1,0:T(8,128)} custom-call(s32[128]{0:T(128)S(1)} %copy-done.2, s32[8]{0:T(128)S(1)} %broadcast_subtract_fusion.limit_ref, f32[64,4,128]{2,1,0:T(4,128)S(1)} %all-to-all-done.1.scores_ref), custom_call_target="tpu_custom_call" | custom-call | tf_op jit(solution)/shard_map/pallas_call | solution.py:382
  (8 shorter events, 0.0 us)
Async XLA Ops:
  2.9 27.4 %all-to-all-start = ((bf16[8,288,128]{2,1,0:T(8,128)(2,1)}), bf16[8,288,128]{2,1,0:T(8,128)(2,1)S(1)}, u32[]{:S(2)}, u32[]{:S(2)}) async-start(bf16[8,288,128]{2,1,0:T(8,128)(2,1)} %bitcast.4), calls=%async_computation | async-start | bytes 1179648 | tf_op jit(solution)/shard_map/all_to_all | solution.py:398
  13.0 4.1 %collective-permute-start = (bf16[8,12,384]{2,1,0:T(8,128)(2,1)S(1)}, bf16[8,12,384]{2,1,0:T(8,128)(2,1)S(1)}, u32[]{:S(2)}, u32[]{:S(2)}) collective-permute-start(bf16[8,12,384]{2,1,0:T(8,128)(2,1)S(1)} %slice.4), channel_id=1, source_target_pairs={{1,0},{2,1},{3,2},{5,4},{6,5},{7,6},{9,8},{10,9},{11,10},{13,12},{... | collective-permute-start | bytes 221192 | tf_op jit(solution)/shard_map/ppermute | solution.py:407
  22.3 4.8 %copy-start = (bf16[8,34,12,16,128]{4,3,2,1,0:T(8,128)(2,1)}, bf16[8,34,12,16,128]{4,3,2,1,0:T(8,128)(2,1)S(1)}, u32[]{:S(2)}) copy-start(bf16[8,34,12,16,128]{4,3,2,1,0:T(8,128)(2,1)S(1)} %get-tuple-element.25.shifted_ref) | copy-start | bytes 40108036
  30.3 11.9 %copy-start.1 = (bf16[8,34,12,16,128]{4,3,2,1,0:T(8,128)(2,1)S(1)}, bf16[8,34,12,16,128]{4,3,2,1,0:T(8,128)(2,1)}, u32[]{:S(2)}) copy-start(bf16[8,34,12,16,128]{4,3,2,1,0:T(8,128)(2,1)} %copy-done) | copy-start | bytes 40108036
  31.7 10.5 %collective-permute-start.1 = (bf16[32,32,128]{2,1,0:T(8,128)(2,1)S(1)}, bf16[32,32,128]{2,1,0:T(8,128)(2,1)S(1)}, u32[]{:S(2)}, u32[]{:S(2)}) collective-permute-start(bf16[32,32,128]{2,1,0:T(8,128)(2,1)S(1)} %get-tuple-element.24), channel_id=1, source_target_pairs={{0,8},{4,12},{8,16},{12,20},{16,24},{20,28},{24,0},{28,4},{32,40},... | collective-permute-start | bytes 786440 | tf_op jit(solution)/shard_map/ppermute | solution.py:421
  33.3 16.9 %collective-permute-start.4 = (bf16[32,32,128]{2,1,0:T(8,128)(2,1)S(1)}, bf16[32,32,128]{2,1,0:T(8,128)(2,1)S(1)}, u32[]{:S(2)}, u32[]{:S(2)}) collective-permute-start(bf16[32,32,128]{2,1,0:T(8,128)(2,1)S(1)} %get-tuple-element.31), channel_id=1, source_target_pairs={{0,16},{4,20},{8,24},{12,28},{16,0},{20,4},{24,8},{28,12},{32,48},... | collective-permute-start | bytes 786440 | tf_op jit(solution)/shard_map/ppermute | solution.py:421
  36.0 20.9 %collective-permute-start.5 = (bf16[32,32,128]{2,1,0:T(8,128)(2,1)S(1)}, bf16[32,32,128]{2,1,0:T(8,128)(2,1)S(1)}, u32[]{:S(2)}, u32[]{:S(2)}) collective-permute-start(bf16[32,32,128]{2,1,0:T(8,128)(2,1)S(1)} %get-tuple-element.32), channel_id=1, source_target_pairs={{0,12},{4,8},{8,20},{12,16},{16,28},{20,24},{24,4},{28,0},{32,44},... | collective-permute-start | bytes 786440 | tf_op jit(solution)/shard_map/ppermute | solution.py:421
  37.6 23.9 %collective-permute-start.2 = (bf16[32,32,128]{2,1,0:T(8,128)(2,1)S(1)}, bf16[32,32,128]{2,1,0:T(8,128)(2,1)S(1)}, u32[]{:S(2)}, u32[]{:S(2)}) collective-permute-start(bf16[32,32,128]{2,1,0:T(8,128)(2,1)S(1)} %get-tuple-element.29), channel_id=1, source_target_pairs={{0,24},{4,28},{8,0},{12,4},{16,8},{20,12},{24,16},{28,20},{32,56},... | collective-permute-start | bytes 786440 | tf_op jit(solution)/shard_map/ppermute | solution.py:421
  41.0 24.7 %collective-permute-start.3 = (bf16[32,32,128]{2,1,0:T(8,128)(2,1)S(1)}, bf16[32,32,128]{2,1,0:T(8,128)(2,1)S(1)}, u32[]{:S(2)}, u32[]{:S(2)}) collective-permute-start(bf16[32,32,128]{2,1,0:T(8,128)(2,1)S(1)} %get-tuple-element.30), channel_id=1, source_target_pairs={{0,4},{4,0},{8,12},{12,8},{16,20},{20,16},{24,28},{28,24},{32,36},... | collective-permute-start | bytes 786440 | tf_op jit(solution)/shard_map/ppermute | solution.py:421
  46.8 23.5 %collective-permute-start.6 = (bf16[32,32,128]{2,1,0:T(8,128)(2,1)S(1)}, bf16[32,32,128]{2,1,0:T(8,128)(2,1)S(1)}, u32[]{:S(2)}, u32[]{:S(2)}) collective-permute-start(bf16[32,32,128]{2,1,0:T(8,128)(2,1)S(1)} %get-tuple-element.33), channel_id=1, source_target_pairs={{0,28},{4,24},{8,4},{12,0},{16,12},{20,8},{24,20},{28,16},{32,60},... | collective-permute-start | bytes 786440 | tf_op jit(solution)/shard_map/ppermute | solution.py:421
  50.1 20.2 %collective-permute-start.7 = (bf16[32,32,128]{2,1,0:T(8,128)(2,1)S(1)}, bf16[32,32,128]{2,1,0:T(8,128)(2,1)S(1)}, u32[]{:S(2)}, u32[]{:S(2)}) collective-permute-start(bf16[32,32,128]{2,1,0:T(8,128)(2,1)S(1)} %get-tuple-element.34), channel_id=1, source_target_pairs={{0,20},{4,16},{8,28},{12,24},{16,4},{20,0},{24,12},{28,8},{32,52},... | collective-permute-start | bytes 786440 | tf_op jit(solution)/shard_map/ppermute | solution.py:421
  61.5 19.6 %copy-start.3 = (s32[8]{0:T(128)S(1)}, s32[8]{0:T(128)}, u32[]{:S(2)}) copy-start(s32[8]{0:T(128)} %param.9) | copy-start | bytes 100
  61.5 32.0 %copy-start.2 = (s32[128]{0:T(128)S(1)}, s32[128]{0:T(128)}, u32[]{:S(2)}) copy-start(s32[128]{0:T(128)} %get-tuple-element.20.place_ref) | copy-start | bytes 1540
  75.7 17.9 %all-to-all-start.1 = ((f32[64,4,128]{2,1,0:T(4,128)}), f32[64,4,128]{2,1,0:T(4,128)S(1)}, u32[]{:S(2)}, u32[]{:S(2)}) async-start(f32[64,4,128]{2,1,0:T(4,128)} %shard_map.62), calls=%async_computation.1 | async-start | bytes 262144 | tf_op jit(solution)/shard_map/all_to_all | solution.py:427

commit v6 on v4

--- a/solution.py
+++ b/solution.py
@@ -14,7 +14,7 @@
 PLANE = 8
 X, Y = 4, 2
 PLANE_STEPS = ((0, 0), (1, 0), (3, 0), (0, 1), (2, 0), (1, 1), (3, 1), (2, 1))
-CALLS = ((6, 7), (4, 5), (2, 3), (0, 1))
+CALLS = ((3, 6), (5, 2), (7, 4), (0, 1))
 SHIFTS = 16
 GROUP = 16
 VMEM_LIMIT = 24 * 1024 * 1024

time: 93.3 us -> 96.7 us (1.036)
  waiting for transfers between devices: 18.8 us -> 26.3 us
  starting transfers between devices: 37.4 us -> 32.7 us
    ppermute x7, waiting for transfers between devices: 1.01 us -> 8.47 us  [local(): units = lax.ppermute(units, 'wide', pairs)]
    ppermute x7, starting transfers between devices: 17.8 us -> 13.8 us  [local(): units = lax.ppermute(units, 'wide', pairs)]
  transfers between devices with their start and end apart: 10 -> 10, of which waited for: 5 -> 6; matrix products, arithmetic and copies ran while one was open for 2% -> 2% of each run, Pallas kernels for 20% -> 20%
where the time goes in v6:
time: 96.7 us; the launch traced here: 95.7 us
  starting transfers between devices  32.7 us (34%)
  Pallas kernels  30.2 us (31%)
  waiting for transfers between devices  26.3 us (27%)
  local copies, waits for them, and re-layouts  6.4 us (7%)
    pallas_call x4, Pallas kernels, slot_scores(): pl.pallas_call(score_kernel, out_shape=jax.ShapeDtypeStruct((slots // CAP...  18.5 us
    ppermute x7, starting transfers between devices, local(): units = lax.ppermute(units, 'wide', pairs)  13.8 us
    all_to_all x1, waiting for transfers between devices, local(): lax.all_to_all(arrange(scores), 'wide', split_axis=0, concat_axis=0, tile...  12.4 us
    all_to_all x1, starting transfers between devices, local(): lax.all_to_all(arrange(scores), 'wide', split_axis=0, concat_axis=0, tile...  8.52 us
    all_to_all x1, starting transfers between devices, local(): lax.all_to_all(sent.reshape(planes, (own_count + 1) * UNIT, 128), 'wide',...  8.48 us
    ppermute x7, waiting for transfers between devices, local(): units = lax.ppermute(units, 'wide', pairs)  8.47 us
    unnamed x9, local copies, waits for them, and re-layouts  6.39 us
    pallas_call x1, Pallas kernels, station_tables(): pl.pallas_call(station_kernel, grid=(stations,), out_shape=(jax.ShapeDtyp...  5.19 us
  transfers between devices with their start and end apart: 10, of which 6 were waited for; matrix products, arithmetic and copies ran while one was open for 2% of the time, Pallas kernels for 20%

profile of v6, /device:TPU:8, one launch (start us, length us, event | category | flops | bytes accessed | tf_op | source)
XLA Modules:
  0.0 95.7 jit_solution(8877485930257560212)
XLA Ops:
  0.0 2.9 %shard_map.55 = (bf16[8,9,32,128]{3,2,1,0:T(8,128)(2,1)}, s32[128]{0:T(128)}) custom-call(s32[8,16]{1,0:T(8,128)} %station_ref.1, s32[8,16]{1,0:T(8,128)} %block_ref.1, bf16[12,8,300]{2,1,0:T(8,128)(2,1)} %bitcast.5), custom_call_target="tpu_custom_call" | custom-call | tf_op jit(solution)/shard_map/pallas_call | solution.py:110
  2.9 8.5 %all-to-all-start = ((bf16[8,288,128]{2,1,0:T(8,128)(2,1)}), bf16[8,288,128]{2,1,0:T(8,128)(2,1)S(1)}, u32[]{:S(2)}, u32[]{:S(2)}) async-start(bf16[8,288,128]{2,1,0:T(8,128)(2,1)} %bitcast.4), calls=%async_computation | async-start | bytes 1179648 | tf_op jit(solution)/shard_map/all_to_all | solution.py:392
  11.4 1.6 %copy.7.wave_ref = bf16[8,12,4096]{2,1,0:T(8,128)(2,1)S(1)} copy(bf16[8,12,4096]{2,0,1:T(8,128)(2,1)} %param.5) | data formatting | bytes 1572864 | tf_op args[0]
  13.0 1.9 %collective-permute-start = (bf16[8,12,384]{2,1,0:T(8,128)(2,1)S(1)}, bf16[8,12,384]{2,1,0:T(8,128)(2,1)S(1)}, u32[]{:S(2)}, u32[]{:S(2)}) collective-permute-start(bf16[8,12,384]{2,1,0:T(8,128)(2,1)S(1)} %slice.4), channel_id=1, source_target_pairs={{1,0},{2,1},{3,2},{5,4},{6,5},{7,6},{9,8},{10,9},{11,10},{13,12},{... | collective-permute-start | bytes 221192 | tf_op jit(solution)/shard_map/ppermute | solution.py:401
  14.9 2.2 %collective-permute-done.tail_ref = bf16[8,12,384]{2,1,0:T(8,128)(2,1)S(1)} collective-permute-done((bf16[8,12,384]{2,1,0:T(8,128)(2,1)S(1)}, bf16[8,12,384]{2,1,0:T(8,128)(2,1)S(1)}, u32[]{:S(2)}, u32[]{:S(2)}) %collective-permute-start) | collective-permute-done | bytes 73760 | tf_op jit(solution)/shard_map/ppermute | solution.py:401
  17.1 5.2 %shard_map.56 = (bf16[8,34,12,16,128]{4,3,2,1,0:T(8,128)(2,1)S(1)}, f32[8,32,16,128]{3,2,1,0:T(8,128)S(1)}) custom-call(bf16[8,12,4096]{2,1,0:T(8,128)(2,1)S(1)} %copy.7.wave_ref, bf16[8,12,384]{2,1,0:T(8,128)(2,1)S(1)} %collective-permute-done.tail_ref), custom_call_target="tpu_custom_call" | custom-call | flops 3000000000 | bytes 20000000 | tf_op jit(solution)/shard_map/pallas_call | solution.py:213
  22.3 4.8 %copy-done = bf16[8,34,12,16,128]{4,3,2,1,0:T(8,128)(2,1)} copy-done((bf16[8,34,12,16,128]{4,3,2,1,0:T(8,128)(2,1)}, bf16[8,34,12,16,128]{4,3,2,1,0:T(8,128)(2,1)S(1)}, u32[]{:S(2)}) %copy-start) | copy-done | bytes 13369368
  27.1 3.2 %all-to-all-done = bf16[8,288,128]{2,1,0:T(8,128)(2,1)S(1)} async-done(((bf16[8,288,128]{2,1,0:T(8,128)(2,1)}), bf16[8,288,128]{2,1,0:T(8,128)(2,1)S(1)}, u32[]{:S(2)}, u32[]{:S(2)}) %all-to-all-start) | async-done | bytes 589856 | tf_op jit(solution)/shard_map/all_to_all | solution.py:392
  30.3 1.4 %shard_map.57 = (bf16[32,32,128]{2,1,0:T(8,128)(2,1)S(1)}, bf16[32,32,128]{2,1,0:T(8,128)(2,1)S(1)}, bf16[32,32,128]{2,1,0:T(8,128)(2,1)S(1)}, bf16[32,32,128]{2...) custom-call(bf16[8,9,32,128]{3,2,1,0:T(8,128)(2,1)S(1)} %bitcast.3, ...), custom_call_target="tpu_custom_call" | custom-call | flops 10000000000 | bytes 40000000 | tf_op jit(solution)/shard_map/pallas_call | solution.py:157
  31.7 1.6 %collective-permute-start.7 = (bf16[32,32,128]{2,1,0:T(8,128)(2,1)S(1)}, bf16[32,32,128]{2,1,0:T(8,128)(2,1)S(1)}, u32[]{:S(2)}, u32[]{:S(2)}) collective-permute-start(bf16[32,32,128]{2,1,0:T(8,128)(2,1)S(1)} %get-tuple-element.28), channel_id=1, source_target_pairs={{0,8},{4,12},{8,16},{12,20},{16,24},{20,28},{24,0},{28,4},{32,40},... | collective-permute-start | bytes 786440 | tf_op jit(solution)/shard_map/ppermute | solution.py:410
  33.3 4.5 %collective-permute-start.5 = (bf16[32,32,128]{2,1,0:T(8,128)(2,1)S(1)}, bf16[32,32,128]{2,1,0:T(8,128)(2,1)S(1)}, u32[]{:S(2)}, u32[]{:S(2)}) collective-permute-start(bf16[32,32,128]{2,1,0:T(8,128)(2,1)S(1)} %get-tuple-element.25), channel_id=1, source_target_pairs={{0,20},{4,16},{8,28},{12,24},{16,4},{20,0},{24,12},{28,8},{32,52},... | collective-permute-start | bytes 786440 | tf_op jit(solution)/shard_map/ppermute | solution.py:410
  37.7 0.8 collective-permute-start.6
  38.5 2.2 %collective-permute-start.3 = (bf16[32,32,128]{2,1,0:T(8,128)(2,1)S(1)}, bf16[32,32,128]{2,1,0:T(8,128)(2,1)S(1)}, u32[]{:S(2)}, u32[]{:S(2)}) collective-permute-start(bf16[32,32,128]{2,1,0:T(8,128)(2,1)S(1)} %get-tuple-element.23), channel_id=1, source_target_pairs={{0,12},{4,8},{8,20},{12,16},{16,28},{20,24},{24,4},{28,0},{32,44},... | collective-permute-start | bytes 786440 | tf_op jit(solution)/shard_map/ppermute | solution.py:410
  40.7 1.7 %collective-permute-start.4 = (bf16[32,32,128]{2,1,0:T(8,128)(2,1)S(1)}, bf16[32,32,128]{2,1,0:T(8,128)(2,1)S(1)}, u32[]{:S(2)}, u32[]{:S(2)}) collective-permute-start(bf16[32,32,128]{2,1,0:T(8,128)(2,1)S(1)} %get-tuple-element.24), channel_id=1, source_target_pairs={{0,24},{4,28},{8,0},{12,4},{16,8},{20,12},{24,16},{28,20},{32,56},... | collective-permute-start | bytes 786440 | tf_op jit(solution)/shard_map/ppermute | solution.py:410
  42.5 2.3 %collective-permute-start.1 = (bf16[32,32,128]{2,1,0:T(8,128)(2,1)S(1)}, bf16[32,32,128]{2,1,0:T(8,128)(2,1)S(1)}, u32[]{:S(2)}, u32[]{:S(2)}) collective-permute-start(bf16[32,32,128]{2,1,0:T(8,128)(2,1)S(1)} %get-tuple-element.20), channel_id=1, source_target_pairs={{0,4},{4,0},{8,12},{12,8},{16,20},{20,16},{24,28},{28,24},{32,36},... | collective-permute-start | bytes 786440 | tf_op jit(solution)/shard_map/ppermute | solution.py:410
  44.8 4.6 %shard_map.61.refs_3_ = f32[16,4,128]{2,1,0:T(4,128)S(1)} custom-call(bf16[32,32,128]{2,1,0:T(8,128)(2,1)S(1)} %get-tuple-element.27.first_ref, bf16[32,32,128]{2,1,0:T(8,128)(2,1)S(1)} %collective-permute-done.7.second_ref, bf16[8,34,12,16,128]{4,3,2,1,0:T(8,128)(2,1)S(1)} %copy-done.1, f32[8,32,16,128]{3,2,1,0:T(8,128)S(1)} %get-tuple-element.19.ready_ref.inverse_ref), custom_call_target="tpu_custom_call" | custom-call | flops 4000000000 | bytes 4000000 | tf_op jit(solution)/shard_map/pallas_call | solution.py:324
  49.4 1.3 %collective-permute-done.5.first_ref = bf16[32,32,128]{2,1,0:T(8,128)(2,1)S(1)} collective-permute-done((bf16[32,32,128]{2,1,0:T(8,128)(2,1)S(1)}, bf16[32,32,128]{2,1,0:T(8,128)(2,1)S(1)}, u32[]{:S(2)}, u32[]{:S(2)}) %collective-permute-start.5) | collective-permute-done | bytes 262176 | tf_op jit(solution)/shard_map/ppermute | solution.py:410
  50.6 0.7 collective-permute-start.2
  51.4 3.0 %collective-permute-done.6.second_ref = bf16[32,32,128]{2,1,0:T(8,128)(2,1)S(1)} collective-permute-done((bf16[32,32,128]{2,1,0:T(8,128)(2,1)S(1)}, bf16[32,32,128]{2,1,0:T(8,128)(2,1)S(1)}, u32[]{:S(2)}, u32[]{:S(2)}) %collective-permute-start.6) | collective-permute-done | bytes 262176 | tf_op jit(solution)/shard_map/ppermute | solution.py:410
  54.4 4.6 %shard_map.60.refs_2_ = f32[16,4,128]{2,1,0:T(4,128)S(1)} custom-call(bf16[32,32,128]{2,1,0:T(8,128)(2,1)S(1)} %collective-permute-done.5.first_ref, bf16[32,32,128]{2,1,0:T(8,128)(2,1)S(1)} %collective-permute-done.6.second_ref, bf16[8,34,12,16,128]{4,3,2,1,0:T(8,128)(2,1)S(1)} %copy-done.1, f32[8,32,16,128]{3,2,1,0:T(8,128)S(1)} %get-tuple-element.19.ready_ref.inverse_ref), custom_call_target="tpu_custom_call" | custom-call | flops 4000000000 | bytes 4000000 | tf_op jit(solution)/shard_map/pallas_call | solution.py:324
  59.0 0.0 copy-start.3
  59.1 0.0 copy-start.2
  59.1 4.2 %collective-permute-done.3.first_ref = bf16[32,32,128]{2,1,0:T(8,128)(2,1)S(1)} collective-permute-done((bf16[32,32,128]{2,1,0:T(8,128)(2,1)S(1)}, bf16[32,32,128]{2,1,0:T(8,128)(2,1)S(1)}, u32[]{:S(2)}, u32[]{:S(2)}) %collective-permute-start.3) | collective-permute-done | bytes 262176 | tf_op jit(solution)/shard_map/ppermute | solution.py:410
  63.2 0.0 collective-permute-done.4.second_ref
  63.2 4.6 %shard_map.59.refs_1_ = f32[16,4,128]{2,1,0:T(4,128)S(1)} custom-call(bf16[32,32,128]{2,1,0:T(8,128)(2,1)S(1)} %collective-permute-done.3.first_ref, bf16[32,32,128]{2,1,0:T(8,128)(2,1)S(1)} %collective-permute-done.4.second_ref, bf16[8,34,12,16,128]{4,3,2,1,0:T(8,128)(2,1)S(1)} %copy-done.1, f32[8,32,16,128]{3,2,1,0:T(8,128)S(1)} %get-tuple-element.19.ready_ref.inverse_ref), custom_call_target="tpu_custom_call" | custom-call | flops 4000000000 | bytes 4000000 | tf_op jit(solution)/shard_map/pallas_call | solution.py:324
  67.9 0.0 collective-permute-done.1.first_ref
  67.9 0.0 collective-permute-done.2.second_ref
  67.9 4.6 %shard_map.58.refs_0_ = f32[16,4,128]{2,1,0:T(4,128)S(1)} custom-call(bf16[32,32,128]{2,1,0:T(8,128)(2,1)S(1)} %collective-permute-done.1.first_ref, bf16[32,32,128]{2,1,0:T(8,128)(2,1)S(1)} %collective-permute-done.2.second_ref, bf16[8,34,12,16,128]{4,3,2,1,0:T(8,128)(2,1)S(1)} %copy-done.1, f32[8,32,16,128]{3,2,1,0:T(8,128)S(1)} %get-tuple-element.19.ready_ref.inverse_ref), custom_call_target="tpu_custom_call" | custom-call | flops 4000000000 | bytes 4000000 | tf_op jit(solution)/shard_map/pallas_call | solution.py:324
  72.5 0.7 shard_map.62
  73.2 8.5 %all-to-all-start.1 = ((f32[64,4,128]{2,1,0:T(4,128)}), f32[64,4,128]{2,1,0:T(4,128)S(1)}, u32[]{:S(2)}, u32[]{:S(2)}) async-start(f32[64,4,128]{2,1,0:T(4,128)} %shard_map.62), calls=%async_computation.1 | async-start | bytes 262144 | tf_op jit(solution)/shard_map/all_to_all | solution.py:413
  81.8 12.4 %all-to-all-done.1.scores_ref = f32[64,4,128]{2,1,0:T(4,128)S(1)} async-done(((f32[64,4,128]{2,1,0:T(4,128)}), f32[64,4,128]{2,1,0:T(4,128)S(1)}, u32[]{:S(2)}, u32[]{:S(2)}) %all-to-all-start.1) | async-done | bytes 131104 | tf_op jit(solution)/shard_map/all_to_all | solution.py:413
  94.2 1.5 %shard_map.63 = f32[8,16,128]{2,1,0:T(8,128)} custom-call(s32[128]{0:T(128)S(1)} %copy-done.2, s32[8]{0:T(128)S(1)} %broadcast_subtract_fusion.limit_ref, f32[64,4,128]{2,1,0:T(4,128)S(1)} %all-to-all-done.1.scores_ref), custom_call_target="tpu_custom_call" | custom-call | tf_op jit(solution)/shard_map/pallas_call | solution.py:376
  (8 shorter events, 0.0 us)
Async XLA Ops:
  2.9 27.4 %all-to-all-start = ((bf16[8,288,128]{2,1,0:T(8,128)(2,1)}), bf16[8,288,128]{2,1,0:T(8,128)(2,1)S(1)}, u32[]{:S(2)}, u32[]{:S(2)}) async-start(bf16[8,288,128]{2,1,0:T(8,128)(2,1)} %bitcast.4), calls=%async_computation | async-start | bytes 1179648 | tf_op jit(solution)/shard_map/all_to_all | solution.py:392
  13.0 4.1 %collective-permute-start = (bf16[8,12,384]{2,1,0:T(8,128)(2,1)S(1)}, bf16[8,12,384]{2,1,0:T(8,128)(2,1)S(1)}, u32[]{:S(2)}, u32[]{:S(2)}) collective-permute-start(bf16[8,12,384]{2,1,0:T(8,128)(2,1)S(1)} %slice.4), channel_id=1, source_target_pairs={{1,0},{2,1},{3,2},{5,4},{6,5},{7,6},{9,8},{10,9},{11,10},{13,12},{... | collective-permute-start | bytes 221192 | tf_op jit(solution)/shard_map/ppermute | solution.py:401
  22.3 4.8 %copy-start = (bf16[8,34,12,16,128]{4,3,2,1,0:T(8,128)(2,1)}, bf16[8,34,12,16,128]{4,3,2,1,0:T(8,128)(2,1)S(1)}, u32[]{:S(2)}) copy-start(bf16[8,34,12,16,128]{4,3,2,1,0:T(8,128)(2,1)S(1)} %get-tuple-element.22.shifted_ref) | copy-start | bytes 40108036
  30.3 14.5 %copy-start.1 = (bf16[8,34,12,16,128]{4,3,2,1,0:T(8,128)(2,1)S(1)}, bf16[8,34,12,16,128]{4,3,2,1,0:T(8,128)(2,1)}, u32[]{:S(2)}) copy-start(bf16[8,34,12,16,128]{4,3,2,1,0:T(8,128)(2,1)} %copy-done) | copy-start | bytes 40108036
  31.7 10.7 %collective-permute-start.7 = (bf16[32,32,128]{2,1,0:T(8,128)(2,1)S(1)}, bf16[32,32,128]{2,1,0:T(8,128)(2,1)S(1)}, u32[]{:S(2)}, u32[]{:S(2)}) collective-permute-start(bf16[32,32,128]{2,1,0:T(8,128)(2,1)S(1)} %get-tuple-element.28), channel_id=1, source_target_pairs={{0,8},{4,12},{8,16},{12,20},{16,24},{20,28},{24,0},{28,4},{32,40},... | collective-permute-start | bytes 786440 | tf_op jit(solution)/shard_map/ppermute | solution.py:410
  33.3 17.4 %collective-permute-start.5 = (bf16[32,32,128]{2,1,0:T(8,128)(2,1)S(1)}, bf16[32,32,128]{2,1,0:T(8,128)(2,1)S(1)}, u32[]{:S(2)}, u32[]{:S(2)}) collective-permute-start(bf16[32,32,128]{2,1,0:T(8,128)(2,1)S(1)} %get-tuple-element.25), channel_id=1, source_target_pairs={{0,20},{4,16},{8,28},{12,24},{16,4},{20,0},{24,12},{28,8},{32,52},... | collective-permute-start | bytes 786440 | tf_op jit(solution)/shard_map/ppermute | solution.py:410
  37.7 16.7 %collective-permute-start.6 = (bf16[32,32,128]{2,1,0:T(8,128)(2,1)S(1)}, bf16[32,32,128]{2,1,0:T(8,128)(2,1)S(1)}, u32[]{:S(2)}, u32[]{:S(2)}) collective-permute-start(bf16[32,32,128]{2,1,0:T(8,128)(2,1)S(1)} %get-tuple-element.26), channel_id=1, source_target_pairs={{0,16},{4,20},{8,24},{12,28},{16,0},{20,4},{24,8},{28,12},{32,48},... | collective-permute-start | bytes 786440 | tf_op jit(solution)/shard_map/ppermute | solution.py:410
  38.5 24.7 %collective-permute-start.3 = (bf16[32,32,128]{2,1,0:T(8,128)(2,1)S(1)}, bf16[32,32,128]{2,1,0:T(8,128)(2,1)S(1)}, u32[]{:S(2)}, u32[]{:S(2)}) collective-permute-start(bf16[32,32,128]{2,1,0:T(8,128)(2,1)S(1)} %get-tuple-element.23), channel_id=1, source_target_pairs={{0,12},{4,8},{8,20},{12,16},{16,28},{20,24},{24,4},{28,0},{32,44},... | collective-permute-start | bytes 786440 | tf_op jit(solution)/shard_map/ppermute | solution.py:410
  40.7 22.5 %collective-permute-start.4 = (bf16[32,32,128]{2,1,0:T(8,128)(2,1)S(1)}, bf16[32,32,128]{2,1,0:T(8,128)(2,1)S(1)}, u32[]{:S(2)}, u32[]{:S(2)}) collective-permute-start(bf16[32,32,128]{2,1,0:T(8,128)(2,1)S(1)} %get-tuple-element.24), channel_id=1, source_target_pairs={{0,24},{4,28},{8,0},{12,4},{16,8},{20,12},{24,16},{28,20},{32,56},... | collective-permute-start | bytes 786440 | tf_op jit(solution)/shard_map/ppermute | solution.py:410
  42.5 25.4 %collective-permute-start.1 = (bf16[32,32,128]{2,1,0:T(8,128)(2,1)S(1)}, bf16[32,32,128]{2,1,0:T(8,128)(2,1)S(1)}, u32[]{:S(2)}, u32[]{:S(2)}) collective-permute-start(bf16[32,32,128]{2,1,0:T(8,128)(2,1)S(1)} %get-tuple-element.20), channel_id=1, source_target_pairs={{0,4},{4,0},{8,12},{12,8},{16,20},{20,16},{24,28},{28,24},{32,36},... | collective-permute-start | bytes 786440 | tf_op jit(solution)/shard_map/ppermute | solution.py:410
  50.6 17.2 %collective-permute-start.2 = (bf16[32,32,128]{2,1,0:T(8,128)(2,1)S(1)}, bf16[32,32,128]{2,1,0:T(8,128)(2,1)S(1)}, u32[]{:S(2)}, u32[]{:S(2)}) collective-permute-start(bf16[32,32,128]{2,1,0:T(8,128)(2,1)S(1)} %get-tuple-element.21), channel_id=1, source_target_pairs={{0,28},{4,24},{8,4},{12,0},{16,12},{20,8},{24,20},{28,16},{32,60},... | collective-permute-start | bytes 786440 | tf_op jit(solution)/shard_map/ppermute | solution.py:410
  59.0 22.7 %copy-start.3 = (s32[8]{0:T(128)S(1)}, s32[8]{0:T(128)}, u32[]{:S(2)}) copy-start(s32[8]{0:T(128)} %param.9) | copy-start | bytes 100
  59.1 35.2 %copy-start.2 = (s32[128]{0:T(128)S(1)}, s32[128]{0:T(128)}, u32[]{:S(2)}) copy-start(s32[128]{0:T(128)} %get-tuple-element.17.place_ref) | copy-start | bytes 1540
  73.2 21.0 %all-to-all-start.1 = ((f32[64,4,128]{2,1,0:T(4,128)}), f32[64,4,128]{2,1,0:T(4,128)S(1)}, u32[]{:S(2)}, u32[]{:S(2)}) async-start(f32[64,4,128]{2,1,0:T(4,128)} %shard_map.62), calls=%async_computation.1 | async-start | bytes 262144 | tf_op jit(solution)/shard_map/all_to_all | solution.py:413
